TPU v7x, 32 devices: a whole 2x2x4 slice. The times are simulated.
32 devices in a mesh: row: 2 (over x), seq: 16 (over z, y, core).
Axes of the slice: x: 2, y: 2, z: 4, core: 2. Of those that a mesh axis runs over, the one named last changes fastest.
Arguments:
- tokens: bfloat16 [2, 2048, 1024], P('row', 'seq'), may hold values from -6 to 6
- attention_gain: bfloat16 [1024], P(('row', 'seq')), may hold values from 0.099609375 to 1.8984375
- expert_gain: bfloat16 [1024], P(('row', 'seq')), may hold values from 0.099609375 to 1.8984375
- query_weight: bfloat16 [1024, 1024], P(('row', 'seq')), may hold values from -0.1875 to 0.1875
- key_matrix: bfloat16 [1024, 512], P(('row', 'seq')), may hold values from -0.1875 to 0.1875
- value_matrix: bfloat16 [1024, 512], P(('row', 'seq')), may hold values from -0.1875 to 0.1875
- output_weight: bfloat16 [1024, 1024], P(('row', 'seq')), may hold values from -6 to 6
- router_weight: bfloat16 [1024, 16], P(('row', 'seq')), may hold values from -0.09375 to 0.09375
- gate_weight: bfloat16 [1024, 16, 512], P(('row', 'seq')), may hold values from -0.1875 to 0.1875
- up_weight: bfloat16 [1024, 16, 512], P(('row', 'seq')), may hold values from -0.1875 to 0.1875
- down_weight: bfloat16 [1024, 16, 512], P(('row', 'seq')), may hold values from -2 to 2
- routes: int32 [2, 2048, 8], P('row', 'seq'), may hold values from 0 to 15, all different within a row; in each aligned block of 128 rows (0 to 127, 128 to 255, ..., all dimensions but the last counted through in order) at most 96 rows name the same one
- segments: int32 [2, 2048], P('row', 'seq'), may hold values from 0 to 2, as said below
- rope_index: int32 [2], P('row'), may hold values from 0 to 3
- cotangent: bfloat16 [2, 2048, 1024], P('row', 'seq'), may hold values from -6 to 6
Outputs:
- mixed: bfloat16 [2, 2048, 1024], P('row', 'seq')
- grad_tokens: float32 [2, 2048, 1024], P('row', 'seq')
- grad_attention_gain: float32 [1024], P(('row', 'seq'))
- grad_expert_gain: float32 [1024], P(('row', 'seq'))
- grad_query_weight: float32 [1024, 1024], P(('row', 'seq'))
- grad_key_weight: float32 [1024, 512], P(('row', 'seq'))
- grad_value_weight: float32 [1024, 512], P(('row', 'seq'))
- grad_output_weight: float32 [1024, 1024], P(('row', 'seq'))
- grad_router_weight: float32 [1024, 16], P(('row', 'seq'))
- grad_gate_weight: float32 [1024, 16, 512], P(('row', 'seq'))
- grad_up_weight: float32 [1024, 16, 512], P(('row', 'seq'))
- grad_down_weight: float32 [1024, 16, 512], P(('row', 'seq'))
Inputs may be any that keep to these rules, and one draw needn't show every extreme that they name: `routes`: each token names 8 different experts; in each aligned block of 128 positions of a row no expert is named by more than 96 of its tokens. `segments`: along each row the numbers never fall; number 0 ends within the row's first 128 positions and number 2 begins within its last 128, so that document 1 runs from the row's first device to its last.
All inputs are finite; a program needn't handle non-finite values.
Results may differ from a plain program's by a relative error of at most 0.028.
Values may be sent and summed in bfloat16 or wider, within the bound.
A program may use at most 384 MiB of HBM per device.

v0:
```python
from functools import partial
import math

import jax
import jax.numpy as jnp
from jax import lax
from jax.sharding import PartitionSpec as P

MODEL_WIDTH = 1024
QUERY_HEADS = 16
KEY_VALUE_HEADS = 8
HEAD_SIZE = 64
F = 512
E = 16
K = 8
CAP = 96


EPSILON = 1e-05
ROPE_BASE = 10000.0
MASKED = -1e30


def rms_scale(values):
    return lax.rsqrt(jnp.mean(values * values, axis=-1, keepdims=True) + EPSILON)


def frequencies(head_dim):
    halves = head_dim // 2
    return jnp.power(ROPE_BASE, -jnp.arange(halves, dtype=jnp.float32) * (2.0 / head_dim))


def apply_rotary(values, cosine_lookup, sine_lookup):
    halves = values.shape[-1] // 2
    first_half = values[..., :halves]
    second_half = values[..., halves:]
    return jnp.concatenate(
        [
            first_half * cosine_lookup - second_half * sine_lookup,
            second_half * cosine_lookup + first_half * sine_lookup,
        ],
        axis=-1,
    )


def unrotate(values, cosine_lookup, sine_lookup):
    halves = values.shape[-1] // 2
    first_half = values[..., :halves]
    second_half = values[..., halves:]
    return jnp.concatenate(
        [
            first_half * cosine_lookup + second_half * sine_lookup,
            second_half * cosine_lookup - first_half * sine_lookup,
        ],
        axis=-1,
    )


def block_mask(key_start, block_size, query_pos, query_seg, seg_block):
    key_pos = key_start + jnp.arange(block_size, dtype=jnp.int32)
    causal = key_pos[None, :] <= query_pos[:, None]
    same_doc = seg_block[:, None, :] == query_seg[:, :, None]
    return (causal[None] & same_doc)[:, None, None]


def attend_piece(running, pieces, first_key, queries, query_pos, query_seg, scaling):
    key_rows, value_rows, key_segments = pieces
    sequence_count, key_span = (key_rows.shape[0], key_rows.shape[1])
    block_size = math.gcd(key_span, 512)
    kv_heads, head_dim = (queries.shape[2], queries.shape[4])

    def advance(block_index, carried):
        top_score, denominator, numerator = carried
        offset = block_index * block_size
        key_block = lax.dynamic_slice_in_dim(key_rows, offset, block_size, 1).reshape(
            sequence_count, block_size, kv_heads, head_dim
        )
        value_block = lax.dynamic_slice_in_dim(value_rows, offset, block_size, 1).reshape(
            sequence_count, block_size, kv_heads, head_dim
        )
        seg_block = lax.dynamic_slice_in_dim(key_segments, offset, block_size, 1).astype(jnp.int32)
        allowed = block_mask(offset, block_size, query_pos, query_seg, seg_block)
        scores = (
            jnp.einsum("sqkgd,sjkd->skgqj", queries, key_block, preferred_element_type=jnp.float32)
            * scaling
        )
        fresh_top = jnp.maximum(top_score, jnp.max(jnp.where(allowed, scores, MASKED), axis=-1))
        weights = jnp.where(allowed, jnp.exp(scores - fresh_top[..., None]), 0.0)
        decay_factor = jnp.exp(top_score - fresh_top)
        denominator = denominator * decay_factor + jnp.sum(weights, axis=-1)
        numerator = numerator * decay_factor[..., None] + jnp.einsum(
            "skgqj,sjkd->skgqd",
            weights.astype(jnp.bfloat16),
            value_block,
            preferred_element_type=jnp.float32,
        )
        return (fresh_top, denominator, numerator)

    return lax.fori_loop(0, key_span // block_size, advance, running)


def attend_back(pieces, queries, query_pos, query_seg, grad_attn, log_total, row_delta, scaling):
    key_rows, value_rows, key_segments = pieces
    sequence_count, key_span, key_value_width = key_rows.shape
    block_size = math.gcd(key_span, 512)
    kv_heads, head_dim = (queries.shape[2], queries.shape[4])

    def advance(block_index, carried):
        grad_queries, gradient_couples = carried
        offset = block_index * block_size
        key_block = lax.dynamic_slice_in_dim(key_rows, offset, block_size, 1).reshape(
            sequence_count, block_size, kv_heads, head_dim
        )
        value_block = lax.dynamic_slice_in_dim(value_rows, offset, block_size, 1).reshape(
            sequence_count, block_size, kv_heads, head_dim
        )
        seg_block = lax.dynamic_slice_in_dim(key_segments, offset, block_size, 1).astype(jnp.int32)
        allowed = block_mask(offset, block_size, query_pos, query_seg, seg_block)
        scores = (
            jnp.einsum("sqkgd,sjkd->skgqj", queries, key_block, preferred_element_type=jnp.float32)
            * scaling
        )
        weights = jnp.where(allowed, jnp.exp(scores - log_total[..., None]), 0.0)
        grad_weights = jnp.einsum(
            "sqkgd,sjkd->skgqj", grad_attn, value_block, preferred_element_type=jnp.float32
        )
        grad_scores = (weights * (grad_weights - row_delta[..., None])).astype(jnp.bfloat16)
        grad_queries = grad_queries + jnp.einsum(
            "skgqj,sjkd->sqkgd", grad_scores, key_block, preferred_element_type=jnp.float32
        )
        grad_keys = (
            jnp.einsum(
                "skgqj,sqkgd->sjkd", grad_scores, queries, preferred_element_type=jnp.float32
            )
            * scaling
        )
        grad_values = jnp.einsum(
            "skgqj,sqkgd->sjkd",
            weights.astype(jnp.bfloat16),
            grad_attn,
            preferred_element_type=jnp.float32,
        )
        produced = jnp.concatenate(
            [
                grad_keys.reshape(sequence_count, block_size, key_value_width),
                grad_values.reshape(sequence_count, block_size, key_value_width),
            ],
            axis=-1,
        )
        return (
            grad_queries,
            lax.dynamic_update_slice_in_dim(gradient_couples, produced, offset, 1),
        )

    starting = (
        jnp.zeros(queries.shape, jnp.float32),
        jnp.zeros((sequence_count, key_span, 2 * key_value_width), jnp.float32),
    )
    grad_queries, gradient_couples = lax.fori_loop(0, key_span // block_size, advance, starting)
    return (grad_queries * scaling, gradient_couples)


def project_in(pieces, routed):
    gate_rows, up_rows = pieces
    return (
        jnp.einsum("erd,def->erf", routed, gate_rows, preferred_element_type=jnp.float32),
        jnp.einsum("erd,def->erf", routed, up_rows, preferred_element_type=jnp.float32),
    )


def project_out(down_rows, hidden):
    produced = jnp.einsum("erf,def->erd", hidden, down_rows, preferred_element_type=jnp.float32)
    return produced


def back_through_down(down_rows, grad_output):
    return jnp.einsum("erd,def->erf", grad_output, down_rows, preferred_element_type=jnp.float32)


def back_through_in(pieces, grad_gate, grad_up):
    gate_rows, up_rows = pieces
    produced = jnp.einsum(
        "erf,def->erd", grad_gate, gate_rows, preferred_element_type=jnp.float32
    ) + jnp.einsum("erf,def->erd", grad_up, up_rows, preferred_element_type=jnp.float32)
    return produced


def take_slots(slot_data, destination):
    experts, width = (slot_data.shape[0], slot_data.shape[-1])
    sequence_count, sequence_rows, picks = destination.shape
    flat = jnp.transpose(
        slot_data.reshape(experts, sequence_count, -1, width), (1, 0, 2, 3)
    ).reshape(sequence_count, -1, width)
    taken = jax.vmap(lambda table, spots: table[spots])(
        flat, destination.reshape(sequence_count, sequence_rows * picks)
    )
    return taken.reshape(sequence_count, sequence_rows, picks, width)


def place_slots(values, destination, experts, capacity):
    sequence_count, width = (values.shape[0], values.shape[-1])
    empty = jnp.zeros((sequence_count, experts * capacity, width), values.dtype)
    filled = jax.vmap(lambda table, spots, rows: table.at[spots].set(rows))(
        empty, destination.reshape(sequence_count, -1), values.reshape(sequence_count, -1, width)
    )
    return jnp.transpose(
        filled.reshape(sequence_count, experts, capacity, width), (1, 0, 2, 3)
    ).reshape(experts, sequence_count * capacity, width)


def per_device(
    tokens,
    attention_gain,
    expert_gain,
    query_weight,
    key_matrix,
    value_matrix,
    output_weight,
    router_weight,
    gate_weight,
    up_weight,
    down_weight,
    routes,
    segments,
    rope_index,
    cotangent,
):
    sequence_count, sequence_rows = (tokens.shape[0], tokens.shape[1])
    queries_per_group = QUERY_HEADS // KEY_VALUE_HEADS
    key_value_width = KEY_VALUE_HEADS * HEAD_SIZE
    scaling = 1.0 / math.sqrt(HEAD_SIZE)
    experts_slots = E * CAP
    gathered = (
        lax.all_gather(attention_gain, ("row", "seq"), axis=0, tiled=True),
        lax.all_gather(expert_gain, ("row", "seq"), axis=0, tiled=True),
        lax.all_gather(query_weight, ("row", "seq"), axis=0, tiled=True),
        lax.all_gather(key_matrix, ("row", "seq"), axis=0, tiled=True),
        lax.all_gather(value_matrix, ("row", "seq"), axis=0, tiled=True),
        lax.all_gather(output_weight, ("row", "seq"), axis=0, tiled=True),
        lax.all_gather(router_weight, ("row", "seq"), axis=0, tiled=True),
    )
    gain_first = gathered[0].astype(jnp.float32)
    gain_second = gathered[1].astype(jnp.float32)
    full_query, full_key, full_value, full_output, full_router = gathered[2:]
    inputs = tokens.astype(jnp.float32)
    scale_first = rms_scale(inputs)
    normed_first = inputs * scale_first
    hidden_first = (normed_first * gain_first).astype(jnp.bfloat16)
    query_unrotated = jnp.einsum(
        "sqd,dc->sqc", hidden_first, full_query, preferred_element_type=jnp.float32
    )
    key_unrotated = jnp.einsum(
        "sqd,dc->sqc", hidden_first, full_key, preferred_element_type=jnp.float32
    )
    value_raw = jnp.einsum(
        "sqd,dc->sqc", hidden_first, full_value, preferred_element_type=jnp.float32
    )
    positions = lax.axis_index("seq") * sequence_rows + jnp.arange(sequence_rows, dtype=jnp.int32)
    factor = jnp.power(2.0, rope_index.astype(jnp.float32))
    angles = (positions.astype(jnp.float32)[None, :] / factor[:, None])[..., None] * frequencies(
        HEAD_SIZE
    )
    cosine_lookup = jnp.cos(angles)[:, :, None, :]
    sine_lookup = jnp.sin(angles)[:, :, None, :]
    query_turned = (
        apply_rotary(
            query_unrotated.reshape(sequence_count, sequence_rows, QUERY_HEADS, HEAD_SIZE),
            cosine_lookup,
            sine_lookup,
        )
        .astype(jnp.bfloat16)
        .reshape(sequence_count, sequence_rows, KEY_VALUE_HEADS, queries_per_group, HEAD_SIZE)
    )
    key_turned = (
        apply_rotary(
            key_unrotated.reshape(sequence_count, sequence_rows, KEY_VALUE_HEADS, HEAD_SIZE),
            cosine_lookup,
            sine_lookup,
        )
        .astype(jnp.bfloat16)
        .reshape(sequence_count, sequence_rows, key_value_width)
    )
    value_reduced = value_raw.astype(jnp.bfloat16)
    segment_low = segments.astype(jnp.float32).astype(jnp.bfloat16)
    statistic_shape = (sequence_count, KEY_VALUE_HEADS, queries_per_group, sequence_rows)
    starting = (
        jnp.full(statistic_shape, MASKED, jnp.float32),
        jnp.zeros(statistic_shape, jnp.float32),
        jnp.zeros(statistic_shape + (HEAD_SIZE,), jnp.float32),
    )
    attend = partial(
        attend_piece, queries=query_turned, query_pos=positions, query_seg=segments, scaling=scaling
    )
    top_score, denominator, numerator = attend(
        starting,
        (
            lax.all_gather(key_turned, "seq", axis=1, tiled=True),
            lax.all_gather(value_reduced, "seq", axis=1, tiled=True),
            lax.all_gather(segment_low, "seq", axis=1, tiled=True),
        ),
        jnp.int32(0),
    )
    attn_heads = numerator / denominator[..., None]
    log_total = top_score + jnp.log(denominator)
    attn_rows = jnp.transpose(attn_heads, (0, 3, 1, 2, 4))
    attn_low = attn_rows.astype(jnp.bfloat16).reshape(
        sequence_count, sequence_rows, QUERY_HEADS * HEAD_SIZE
    )
    branch = jnp.einsum("sqc,dc->sqd", attn_low, full_output, preferred_element_type=jnp.float32)
    residual = inputs + branch
    scale_second = rms_scale(residual)
    normed_second = residual * scale_second
    hidden_second = (normed_second * gain_second).astype(jnp.bfloat16)
    logits = jnp.einsum(
        "sqd,de->sqe", hidden_second, full_router, preferred_element_type=jnp.float32
    )
    router_probs = jax.nn.softmax(logits, axis=-1)
    picked = routes[..., None] == jnp.arange(E, dtype=jnp.int32)
    picked_int = picked.astype(jnp.int32).reshape(sequence_count, sequence_rows * K, E)
    earlier = jnp.cumsum(picked_int, axis=1, dtype=jnp.int32) - picked_int
    slot_ids = jnp.sum(earlier * picked_int, axis=-1, dtype=jnp.int32).reshape(
        sequence_count, sequence_rows, K
    )
    destination = routes * CAP + slot_ids
    chosen = destination[..., None] == jnp.arange(experts_slots, dtype=jnp.int32)
    gate_probs = jnp.sum(jnp.where(picked, router_probs[:, :, None, :], 0.0), axis=-1)
    dispatch = jnp.sum(chosen, axis=2, dtype=jnp.float32).reshape(
        sequence_count, sequence_rows, E, CAP
    )
    slot_rows = sequence_count * CAP
    routed = (
        jnp.einsum(
            "sqec,sqd->escd",
            dispatch.astype(jnp.bfloat16),
            hidden_second,
            preferred_element_type=jnp.float32,
        )
        .astype(jnp.bfloat16)
        .reshape(E, slot_rows, MODEL_WIDTH)
    )
    grad_mixed = cotangent.astype(jnp.float32)
    grad_slot_values = (gate_probs[..., None] * grad_mixed[:, :, None, :]).astype(jnp.bfloat16)
    grad_expert = place_slots(grad_slot_values, destination, E, CAP)
    gate_pre, up_pre = project_in(
        (
            lax.all_gather(gate_weight, ("row", "seq"), axis=0, tiled=True),
            lax.all_gather(up_weight, ("row", "seq"), axis=0, tiled=True),
        ),
        routed=routed,
    )
    hidden_low = (jax.nn.silu(gate_pre) * up_pre).astype(jnp.bfloat16)
    expert_out = project_out(
        lax.all_gather(down_weight, ("row", "seq"), axis=0, tiled=True), hidden=hidden_low
    )
    grad_hidden = back_through_down(
        lax.all_gather(down_weight, ("row", "seq"), axis=0, tiled=True), grad_output=grad_expert
    )
    sigmoid_gate = jax.nn.sigmoid(gate_pre)
    grad_gate = (
        grad_hidden * up_pre * sigmoid_gate * (1.0 + gate_pre * (1.0 - sigmoid_gate))
    ).astype(jnp.bfloat16)
    grad_up = (grad_hidden * (gate_pre * sigmoid_gate)).astype(jnp.bfloat16)
    grad_routed = back_through_in(
        (
            lax.all_gather(gate_weight, ("row", "seq"), axis=0, tiled=True),
            lax.all_gather(up_weight, ("row", "seq"), axis=0, tiled=True),
        ),
        grad_gate=grad_gate,
        grad_up=grad_up,
    )
    expert_grads = lax.psum_scatter(
        jnp.concatenate(
            [
                jnp.einsum("erd,erf->def", routed, grad_gate, preferred_element_type=jnp.float32),
                jnp.einsum("erd,erf->def", routed, grad_up, preferred_element_type=jnp.float32),
                jnp.einsum(
                    "erd,erf->def", grad_expert, hidden_low, preferred_element_type=jnp.float32
                ),
            ],
            axis=2,
        ),
        ("row", "seq"),
        scatter_dimension=0,
        tiled=True,
    )
    grad_gate_weight = expert_grads[:, :, :F]
    grad_up_weight = expert_grads[:, :, F : 2 * F]
    grad_down_weight = expert_grads[:, :, 2 * F :]
    taken_out = take_slots(expert_out, destination)
    expert_mix = jnp.sum(gate_probs[..., None] * taken_out, axis=2)
    mixed = (residual + expert_mix).astype(jnp.bfloat16)
    grad_gates = jnp.sum(taken_out * grad_mixed[:, :, None, :], axis=-1)
    grad_probs = jnp.sum(jnp.where(picked, grad_gates[..., None], 0.0), axis=2)
    grad_logits = (
        router_probs * (grad_probs - jnp.sum(router_probs * grad_probs, axis=-1, keepdims=True))
    ).astype(jnp.bfloat16)
    grad_second = jnp.sum(take_slots(grad_routed, destination), axis=2) + jnp.einsum(
        "sqe,de->sqd", grad_logits, full_router, preferred_element_type=jnp.float32
    )
    grad_gain_second = jnp.sum(grad_second * normed_second, axis=(0, 1))
    scaled_second = grad_second * gain_second
    grad_residual = grad_mixed + scale_second * (
        scaled_second
        - normed_second * jnp.mean(scaled_second * normed_second, axis=-1, keepdims=True)
    )
    grad_branch = grad_residual.astype(jnp.bfloat16)
    grad_attn = (
        jnp.einsum("sqd,dc->sqc", grad_branch, full_output, preferred_element_type=jnp.float32)
        .astype(jnp.bfloat16)
        .reshape(sequence_count, sequence_rows, KEY_VALUE_HEADS, queries_per_group, HEAD_SIZE)
    )
    row_delta = jnp.transpose(
        jnp.sum(grad_attn.astype(jnp.float32) * attn_rows, axis=-1), (0, 2, 3, 1)
    )
    keys_back = (
        lax.all_gather(key_turned, "seq", axis=1, tiled=True),
        lax.all_gather(value_reduced, "seq", axis=1, tiled=True),
        lax.all_gather(segment_low, "seq", axis=1, tiled=True),
    )
    grad_query_rot, grad_pair_rows = attend_back(
        keys_back, query_turned, positions, segments, grad_attn, log_total, row_delta, scaling
    )
    gradient_couples = lax.psum_scatter(grad_pair_rows, "seq", scatter_dimension=1, tiled=True)
    grad_query = (
        unrotate(
            grad_query_rot.reshape(sequence_count, sequence_rows, QUERY_HEADS, HEAD_SIZE),
            cosine_lookup,
            sine_lookup,
        )
        .astype(jnp.bfloat16)
        .reshape(sequence_count, sequence_rows, QUERY_HEADS * HEAD_SIZE)
    )
    grad_key = (
        unrotate(
            gradient_couples[..., :key_value_width].reshape(
                sequence_count, sequence_rows, KEY_VALUE_HEADS, HEAD_SIZE
            ),
            cosine_lookup,
            sine_lookup,
        )
        .astype(jnp.bfloat16)
        .reshape(sequence_count, sequence_rows, key_value_width)
    )
    grad_value = gradient_couples[..., key_value_width:].astype(jnp.bfloat16)
    grad_first = (
        jnp.einsum("sqc,dc->sqd", grad_query, full_query, preferred_element_type=jnp.float32)
        + jnp.einsum("sqc,dc->sqd", grad_key, full_key, preferred_element_type=jnp.float32)
        + jnp.einsum("sqc,dc->sqd", grad_value, full_value, preferred_element_type=jnp.float32)
    )
    grad_gain_first = jnp.sum(grad_first * normed_first, axis=(0, 1))
    scaled_first = grad_first * gain_first
    grad_tokens = grad_residual + scale_first * (
        scaled_first - normed_first * jnp.mean(scaled_first * normed_first, axis=-1, keepdims=True)
    )
    attention_grads = lax.psum_scatter(
        jnp.concatenate(
            [
                jnp.einsum(
                    "sqd,sqc->dc", hidden_first, grad_query, preferred_element_type=jnp.float32
                ),
                jnp.einsum(
                    "sqd,sqc->dc", hidden_first, grad_key, preferred_element_type=jnp.float32
                ),
                jnp.einsum(
                    "sqd,sqc->dc", hidden_first, grad_value, preferred_element_type=jnp.float32
                ),
                jnp.einsum(
                    "sqd,sqc->dc", grad_branch, attn_low, preferred_element_type=jnp.float32
                ),
                jnp.einsum(
                    "sqd,sqe->de", hidden_second, grad_logits, preferred_element_type=jnp.float32
                ),
                grad_gain_first[:, None],
                grad_gain_second[:, None],
            ],
            axis=1,
        ),
        ("row", "seq"),
        scatter_dimension=0,
        tiled=True,
    )
    query_cols = QUERY_HEADS * HEAD_SIZE
    edge_two = query_cols + key_value_width
    edge_three = edge_two + key_value_width
    edge_four = edge_three + query_cols
    edge_five = edge_four + E
    return (
        mixed,
        grad_tokens,
        attention_grads[:, edge_five],
        attention_grads[:, edge_five + 1],
        attention_grads[:, :query_cols],
        attention_grads[:, query_cols:edge_two],
        attention_grads[:, edge_two:edge_three],
        attention_grads[:, edge_three:edge_four],
        attention_grads[:, edge_four:edge_five],
        grad_gate_weight,
        grad_up_weight,
        grad_down_weight,
    )


def solution(mesh):
    in_specs = (
        P("row", "seq", None),
        P(("row", "seq")),
        P(("row", "seq")),
        P(("row", "seq"), None),
        P(("row", "seq"), None),
        P(("row", "seq"), None),
        P(("row", "seq"), None),
        P(("row", "seq"), None),
        P(("row", "seq"), None, None),
        P(("row", "seq"), None, None),
        P(("row", "seq"), None, None),
        P("row", "seq", None),
        P("row", "seq"),
        P("row"),
        P("row", "seq", None),
    )
    out_specs = (
        P("row", "seq", None),
        P("row", "seq", None),
        P(("row", "seq")),
        P(("row", "seq")),
        P(("row", "seq"), None),
        P(("row", "seq"), None),
        P(("row", "seq"), None),
        P(("row", "seq"), None),
        P(("row", "seq"), None),
        P(("row", "seq"), None, None),
        P(("row", "seq"), None, None),
        P(("row", "seq"), None, None),
    )
    return jax.shard_map(
        per_device, mesh=mesh, in_specs=in_specs, out_specs=out_specs, check_vma=False
    )
```

profile of v0, /device:TPU:0, one launch (start us, length us, event | category | flops | bytes accessed | tf_op | source)
XLA Modules:
  0.0 2027.3 jit_solution(2158472535076558235)
XLA Ops:
  11.2 42.0 %all-reduce.2 = (bf16[1024]{0:T(1024)(128)(2,1)S(1)}, bf16[1024]{0:T(1024)(128)(2,1)S(1)}) all-reduce(bf16[1024]{0:T(1024)(128)(2,1)S(1)} %dynamic-update-slice, bf16[1024]{0:T(1024)(128)(2,1)S(1)} %dynamic-update-slice.1), channel_id=1, replica_groups=mesh['row'=2,'seq'=16] {'row','seq'}, use_global_device_ids=true, to_apply=%add | all-reduce | flops 2048 | bytes 8192
  54.3 13.3 all-gather.18.cloned.1.call-done
  67.6 2.3 convolution_convert_fusion.1
  71.0 52.3 %all-gather.12.cloned.1.call-done = bf16[1024,512]{1,0:T(8,128)(2,1)} async-done(((bf16[32,512]{1,0:T(8,128)(2,1)}), bf16[1024,512]{1,0:T(8,128)(2,1)}) %all-gather.12.cloned.1.call-update) | async-done | bytes 1048592 | tf_op jit(solution)/shard_map/all_gather | solution.py:237
  130.5 4.5 reduce-window.6
  136.0 39.9 %all-gather.1 = bf16[32,32,16]{1,2,0:T(8,128)(2,1)S(1)} all-gather(bf16[1,32,16]{1,2,0:T(8,128)(2,1)S(1)} %bitcast.480), channel_id=1, replica_groups=mesh['row'=2,'seq'=16] {'row','seq'}, dimensions={0}, use_global_device_ids=true | all-gather | bytes 33792 | tf_op jit(solution)/shard_map/all_gather | solution.py:240
  176.1 17.5 all_gather.45
  193.8 3.9 convert_reduce_fusion
  198.6 2.9 copy.188
  202.4 22.0 %all-gather.28.cloned.1.call-done = bf16[2048,512]{1,0:T(8,128)(2,1)} async-done(((bf16[128,512]{1,0:T(8,128)(2,1)}), bf16[2048,512]{1,0:T(8,128)(2,1)}) %all-gather.28.cloned.1.call-update) | async-done | bytes 2097168 | tf_op jit(solution)/shard_map/all_gather | solution.py:298
  224.4 2.9 copy.189
  227.3 39.6 %all-gather.14.cloned.1.call-done = bf16[1,2048,512]{1,2,0:T(8,128)(2,1)} async-done(((bf16[1,128,512]{1,2,0:T(8,128)(2,1)}), bf16[1,2048,512]{1,2,0:T(8,128)(2,1)}) %all-gather.14.cloned.1.call-update) | async-done | bytes 2097168 | tf_op jit(solution)/shard_map/all_gather | solution.py:297
  267.0 17.0 while.34
  285.5 39.6 %all-gather.20.cloned.1.call-done = bf16[1024,1024]{1,0:T(8,128)(2,1)} async-done(((bf16[32,1024]{1,0:T(8,128)(2,1)}), bf16[1024,1024]{1,0:T(8,128)(2,1)}) %all-gather.20.cloned.1.call-update) | async-done | bytes 2097168 | tf_op jit(solution)/shard_map/all_gather | solution.py:239
  325.1 2.5 multiply_reduce_fusion
  327.7 2.1 fusion.135
  330.7 111.7 %all-gather.22.cloned.1.call-done = bf16[1024,16,512]{2,0,1:T(8,128)(2,1)} async-done(((bf16[32,16,512]{2,0,1:T(8,128)(2,1)}), bf16[1024,16,512]{2,0,1:T(8,128)(2,1)}) %all-gather.22.cloned.1.call-update) | async-done | bytes 16777232 | tf_op jit(solution)/shard_map/all_gather | solution.py:346
  442.4 10.2 fusion.66
  452.6 106.6 %all-gather.24.cloned.1.call-done = bf16[1024,16,512]{2,0,1:T(8,128)(2,1)} async-done(((bf16[32,16,512]{2,0,1:T(8,128)(2,1)}), bf16[1024,16,512]{2,0,1:T(8,128)(2,1)}) %all-gather.24.cloned.1.call-update) | async-done | bytes 16777232 | tf_op jit(solution)/shard_map/all_gather | solution.py:347
  559.2 12.0 multiply_convert_fusion.2
  571.2 104.2 %all-gather.26.cloned.1.call-done = bf16[1024,16,512]{2,0,1:T(8,128)(2,1)} async-done(((bf16[32,16,512]{2,0,1:T(8,128)(2,1)}), bf16[1024,16,512]{2,0,1:T(8,128)(2,1)}) %all-gather.26.cloned.1.call-update) | async-done | bytes 16777232 | tf_op jit(solution)/shard_map/all_gather | solution.py:353
  675.4 14.0 fusion.131
  689.4 20.0 gather_fusion
  709.4 2.9 fusion.59
  712.5 4.2 fusion.61
  716.9 7.0 scatter_custom_fusion
  723.9 13.8 multiply_convert_fusion
  737.7 14.1 fusion.132
  751.9 12.0 convolution_add_fusion
  763.9 19.7 gather_fusion.1
  783.6 3.4 bitcast_reduce_fusion
  789.1 4.3 broadcast_in_dim.187
  793.5 30.1 %while.35 = (s32[]{:T(128)}, f32[1,128,8,2,64]{1,4,3,2,0:T(8,128)S(1)}, f32[1,2048,1024]{1,2,0:T(8,128)}, bf16[1,2048,512]{1,2,0:T(8,128)(2,1)}, bf16[1,2048]{1,...) while((s32[]{:T(128)}, ...), condition=%wide.region_22.23_spmd.clone, body=%wide.region_21.22_spmd.clone.sunk | while | flops 682820736 | bytes 31165160 | solution.py:159
  824.7 3.2 fusion.133
  827.9 2.7 fusion.103
  830.7 2.7 fusion.95
  833.3 93.6 %reduce-scatter.6.cloned.1.call-done = f32[1,128,1024]{1,2,0:T(8,128)} async-done(((f32[1,2048,1024]{1,2,0:T(8,128)}), f32[1,128,1024]{1,2,0:T(8,128)}) %reduce-scatter.6.cloned.1.call-update) | async-done | bytes 524304 | tf_op jit(solution)/shard_map/reduce_scatter | solution.py:423
  928.6 2.8 fusion.100
  931.9 1.8 fusion.85
  933.7 30.2 %concatenate.64 = f32[1024,3090]{0,1:T(8,128)} concatenate(f32[1024,1024]{0,1:T(8,128)} %fusion.103, f32[1024,512]{0,1:T(8,128)S(1)} %fusion.105, f32[1024,512]{0,1:T(8,128)} %fusion.100, f32[1024,1024]{0,1:T(8,128)} %fusion.95, f32[1024,16]{0,1:T(8,128)S(1)} %fusion.134, f32[1024,1]{0,1:T(1,128)S(1)} %bitcast.473, f32[1024,1]{0,1:T(1,128)S(1)} %bitcast.472), dimensions={1} | concatenate | bytes 25313280 | tf_op jit(solution)/shard_map/concatenate | solution.py:456
  964.0 13.4 copy.221
  977.7 18.4 convolution_bitcast_fusion
  996.1 13.3 convolution_bitcast_fusion.1
  1009.5 13.5 convolution_bitcast_fusion.2
  1023.0 67.6 %pad_maximum_fusion = f32[1024,16,1536]{0,2,1:T(8,128)} fusion(f32[1024,16,512]{0,2,1:T(8,128)} %convolution_bitcast_fusion, f32[1024,16,512]{0,2,1:T(8,128)} %convolution_bitcast_fusion.1, f32[1024,16,512]{0,2,1:T(8,128)} %convolution_bitcast_fusion.2), kind=kLoop, calls=%fused_computation.69 | loop fusion | flops 50331648 | bytes 201326592 | tf_op jit(solution)/shard_map/concatenate | solution.py:372
  1090.5 99.9 %copy.206 = f32[1024,16,1536]{2,1,0:T(8,128)} copy(f32[1024,16,1536]{0,2,1:T(8,128)} %pad_maximum_fusion) | data formatting | bytes 201326592 | tf_op jit(solution)/shard_map/concatenate | solution.py:372
  1199.5 817.1 %reduce-scatter.8.cloned.1.call-done = f32[32,16,1536]{2,1,0:T(8,128)} async-done(((f32[1024,16,1536]{2,1,0:T(8,128)}), f32[32,16,1536]{2,1,0:T(8,128)}) %reduce-scatter.8.cloned.1.call-update) | async-done | bytes 3145744 | tf_op jit(solution)/shard_map/reduce_scatter | solution.py:371
  2016.6 3.6 fusion.126
  (319 shorter events, 78.9 us)
Async XLA Ops:
  7.2 117.6 %copy-start.2 = (bf16[1,128,1024]{2,1,0:T(8,128)(2,1)S(1)}, bf16[1,128,1024]{2,1,0:T(8,128)(2,1)}, u32[]{:S(2)}) copy-start(bf16[1,128,1024]{2,1,0:T(8,128)(2,1)} %param.19) | copy-start | bytes 786436
  7.2 119.5 %copy-start.32 = (bf16[32,16,512]{2,1,0:T(8,128)(2,1)S(1)}, bf16[32,16,512]{2,1,0:T(8,128)(2,1)}, u32[]{:S(2)}) copy-start(bf16[32,16,512]{2,1,0:T(8,128)(2,1)} %param.27) | copy-start | bytes 1572868
  7.2 120.7 %copy-start.33 = (bf16[32,16,512]{2,1,0:T(8,128)(2,1)S(1)}, bf16[32,16,512]{2,1,0:T(8,128)(2,1)}, u32[]{:S(2)}) copy-start(bf16[32,16,512]{2,1,0:T(8,128)(2,1)} %param.28) | copy-start | bytes 1572868
  7.2 60.4 %all-gather.18.cloned.1.call-start = ((), (), s32[]{:S(2)}) async-start(), calls=%async_computation.6 | async-start | bytes 1081344 | tf_op jit(solution)/shard_map/all_gather | solution.py:238
  7.9 115.3 %all-gather.12.cloned.1.call-start = ((), (), s32[]{:S(2)}) async-start(), calls=%async_computation.3 | async-start | bytes 1081344 | tf_op jit(solution)/shard_map/all_gather | solution.py:237
  8.7 189.9 %all-gather.16.cloned.1.call-start = ((), (), s32[]{:S(2)}) async-start(), calls=%async_computation.5 | async-start | bytes 2162688 | tf_op jit(solution)/shard_map/all_gather | solution.py:236
  9.4 215.0 %all-gather.28.cloned.1.call-start = ((), (), s32[]{:S(2)}) async-start(), calls=%async_computation.13 | async-start | bytes 2228224 | tf_op jit(solution)/shard_map/all_gather | solution.py:298
  53.2 148.2 %copy-start.39 = (f32[1024]{0:T(1024)}, f32[1024]{0:T(1024)S(1)}, u32[]{:S(2)}) copy-start(f32[1024]{0:T(1024)S(1)} %convert_element_type.264) | copy-start | bytes 12292
  54.3 147.1 %copy-start.44 = (f32[128]{0:T(128)}, f32[128]{0:T(128)S(1)}, u32[]{:S(2)}) copy-start(f32[128]{0:T(128)S(1)} %add_rsqrt_fusion.1) | copy-start | bytes 1540
  70.0 59.1 %copy-start.34 = (bf16[32,16,512]{2,1,0:T(8,128)(2,1)S(1)}, bf16[32,16,512]{2,1,0:T(8,128)(2,1)}, u32[]{:S(2)}) copy-start(bf16[32,16,512]{2,1,0:T(8,128)(2,1)} %param.29) | copy-start | bytes 1572868
  70.0 197.0 %all-gather.14.cloned.1.call-start = ((), (), s32[]{:S(2)}) async-start(), calls=%async_computation.4 | async-start | bytes 2228224 | tf_op jit(solution)/shard_map/all_gather | solution.py:297
  71.0 131.3 %copy-start.35 = (f32[128,32]{0,1:T(8,128)}, f32[128,32]{0,1:T(8,128)S(1)}, u32[]{:S(2)}) copy-start(f32[128,32]{0,1:T(8,128)S(1)} %get-tuple-element.787) | copy-start | bytes 49156
  71.0 131.3 %copy-start.37 = (f32[128,32]{0,1:T(8,128)}, f32[128,32]{0,1:T(8,128)S(1)}, u32[]{:S(2)}) copy-start(f32[128,32]{0,1:T(8,128)S(1)} %get-tuple-element.788) | copy-start | bytes 49156
  123.2 7.0 copy-start.43
  124.8 11.2 copy-start.47
  125.3 50.8 %copy-start.42 = (s32[1,128]{1,0:T(1,128)S(1)}, s32[1,128]{1,0:T(1,128)}, u32[]{:S(2)}) copy-start(s32[1,128]{1,0:T(1,128)} %param.31) | copy-start | bytes 1540
  125.3 68.3 %copy-start.50 = (s32[2]{0:T(128)S(1)}, s32[2]{0:T(128)}, u32[]{:S(2)}) copy-start(s32[2]{0:T(128)} %constant.151) | copy-start | bytes 28
  125.3 68.4 %copy-start.49 = (s32[2]{0:T(128)S(1)}, s32[2]{0:T(128)}, u32[]{:S(2)}) copy-start(s32[2]{0:T(128)} %constant.148) | copy-start | bytes 28
  125.3 72.4 %copy-start.30 = (bf16[1,128,1024]{2,1,0:T(8,128)(2,1)S(1)}, bf16[1,128,1024]{2,1,0:T(8,128)(2,1)}, u32[]{:S(2)}) copy-start(bf16[1,128,1024]{2,1,0:T(8,128)(2,1)} %param.33) | copy-start | bytes 786436
  126.1 199.0 %all-gather.20.cloned.1.call-start = ((), (), s32[]{:S(2)}) async-start(), calls=%async_computation.7 | async-start | bytes 2162688 | tf_op jit(solution)/shard_map/all_gather | solution.py:239
  126.7 315.7 %all-gather.22.cloned.1.call-start = ((), (), s32[]{:S(2)}) async-start(), calls=%async_computation.8 | async-start | bytes 17301504 | tf_op jit(solution)/shard_map/all_gather | solution.py:346
  127.8 431.4 %all-gather.24.cloned.1.call-start = ((), (), s32[]{:S(2)}) async-start(), calls=%async_computation.9 | async-start | bytes 17301504 | tf_op jit(solution)/shard_map/all_gather | solution.py:347
  129.0 546.4 %all-gather.26.cloned.1.call-start = ((), (), s32[]{:S(2)}) async-start(), calls=%async_computation.10 | async-start | bytes 17301504 | tf_op jit(solution)/shard_map/all_gather | solution.py:353
  130.2 796.7 %reduce-scatter.6.cloned.1.call-start = ((), (), s32[]{:S(2)}) async-start(), calls=%async_computation.11 | async-start | bytes 8912896 | tf_op jit(solution)/shard_map/reduce_scatter | solution.py:423
  284.0 45.9 %copy-start.5 = (bf16[1,2048,512]{1,2,0:T(8,128)(2,1)}, bf16[1,2048,512]{1,2,0:T(8,128)(2,1)S(1)}, u32[]{:S(2)}) copy-start(bf16[1,2048,512]{1,2,0:T(8,128)(2,1)S(1)} %get-tuple-element.1056) | copy-start | bytes 6291460
  285.5 44.4 %copy-start.21 = (bf16[1,128,8,2,64]{1,4,3,2,0:T(8,128)(2,1)}, bf16[1,128,8,2,64]{1,4,3,2,0:T(8,128)(2,1)S(1)}, u32[]{:S(2)}) copy-start(bf16[1,128,8,2,64]{1,4,3,2,0:T(8,128)(2,1)S(1)} %bitcast_convert_fusion) | copy-start | bytes 786436
  330.4 228.8 %copy-start = (bf16[1024,16,96]{0,2,1:T(8,128)(2,1)}, bf16[1024,16,96]{0,2,1:T(8,128)(2,1)S(1)}, u32[]{:S(2)}) copy-start(bf16[1024,16,96]{0,2,1:T(8,128)(2,1)S(1)} %convert_element_type.279) | copy-start | bytes 9437188
  689.4 20.0 copy-start.16
  723.9 13.8 copy-start.6
  737.7 14.1 copy-start.7
  783.6 3.8 copy-start.24
  783.6 3.8 copy-start.31
  783.6 4.8 copy-start.13
  788.4 42.3 %copy-start.11 = (f32[1,128,1024]{2,1,0:T(8,128)}, f32[1,128,1024]{2,1,0:T(8,128)S(1)}, u32[]{:S(2)}) copy-start(f32[1,128,1024]{2,1,0:T(8,128)S(1)} %get-tuple-element.773) | copy-start | bytes 1572868
  789.1 4.3 copy-start.9
  823.6 4.3 copy-start.3
  823.6 4.3 copy-start.40
  823.6 4.3 copy-start.45
  823.6 369.1 %reduce-scatter.10.cloned.1.call-start = ((), (), s32[]{:S(2)}) async-start(), calls=%async_computation.14 | async-start | bytes 13516800
  824.4 6.3 copy-start.22
  833.3 98.6 %copy-start.17 = (bf16[1024,512]{1,0:T(8,128)(2,1)S(1)}, bf16[1024,512]{1,0:T(8,128)(2,1)}, u32[]{:S(2)}) copy-start(bf16[1024,512]{1,0:T(8,128)(2,1)} %all-gather.18.cloned.1.call-done) | copy-start | bytes 3145732
  926.9 4.5 copy-start.18
  926.9 4.5 copy-start.28
  926.9 5.0 copy-start.29
  977.4 18.7 copy-start.1
  977.4 1039.1 %reduce-scatter.8.cloned.1.call-start = ((), (), s32[]{:S(2)}) async-start(), calls=%async_computation.12 | async-start | bytes 103809024 | tf_op jit(solution)/shard_map/reduce_scatter | solution.py:371
  977.7 18.4 copy-start.8
  996.1 13.4 copy-start.10
  (21 other events, 32.2 us)
Sparse Core Ops, SparseCore 0:
  10.9 56.6 all-gather.17
  70.5 52.6 all-gather.11
  126.1 55.3 all-gather.15
  184.1 40.2 all-gather.27
  227.0 39.9 all-gather.13
  269.7 55.3 all-gather.19
  328.6 113.7 all-gather.21
  445.9 113.2 all-gather.23
  562.1 113.2 all-gather.25
  823.7 103.1 reduce-scatter.5
  977.6 157.2 reduce-scatter.9
  1190.6 825.8 reduce-scatter.7
where the time goes:
time: 2030 us
  waiting for transfers between devices  1400 us (69%)
  local copies, waits for them, and re-layouts  225 us (11%)
  matrix products  170 us (8%)
  other arithmetic  113 us (6%)
  blocking collectives  99.4 us (5%)
    reduce_scatter x1, waiting for transfers between devices, per_device(): lax.psum_scatter(jnp.concatenate([jnp.einsum('erd,erf->def', routed, grad...  817 us
    all_gather x1, waiting for transfers between devices, per_device(): lax.all_gather(gate_weight, ('row', 'seq'), axis=0, tiled=True)  112 us
    all_gather x1, waiting for transfers between devices, per_device(): lax.all_gather(up_weight, ('row', 'seq'), axis=0, tiled=True)  107 us
    all_gather x1, waiting for transfers between devices, per_device(): lax.all_gather(down_weight, ('row', 'seq'), axis=0, tiled=True)  104 us
    concatenate x1, local copies, waits for them, and re-layouts, per_device(): jnp.concatenate([jnp.einsum('erd,erf->def', routed, grad_gate, preferred_...  99.9 us
    reduce_scatter x1, waiting for transfers between devices, per_device(): lax.psum_scatter(grad_pair_rows, 'seq', scatter_dimension=1, tiled=True)  93.6 us
    concatenate x1, other arithmetic, per_device(): jnp.concatenate([jnp.einsum('erd,erf->def', routed, grad_gate, preferred_...  67.6 us
    all_gather x1, waiting for transfers between devices, per_device(): lax.all_gather(key_matrix, ('row', 'seq'), axis=0, tiled=True)  52.3 us
  transfers between devices with their start and end apart: 12, of which 10 were waited for; matrix products, arithmetic and copies ran while one was open for 15% of the time, Pallas kernels for 0%

commit v1 on v0

--- a/solution.py
+++ b/solution.py
@@ -4,6 +4,8 @@
 import jax
 import jax.numpy as jnp
 from jax import lax
+from jax.experimental import pallas as pl
+from jax.experimental.pallas import tpu as pltpu
 from jax.sharding import PartitionSpec as P
 
 MODEL_WIDTH = 1024
@@ -15,19 +17,954 @@
 K = 8
 CAP = 96
 
-
 EPSILON = 1e-05
 ROPE_BASE = 10000.0
 MASKED = -1e30
+MESH = pl.DeviceIdType.MESH
+VM = pltpu.VMEM
+BF = jnp.bfloat16
+F32 = jnp.float32
+DMA = pltpu.SemaphoreType.DMA
+UP, DOWN, SIDE, CORE = range(4)
+VMEM_LIMIT = 60 * 1024 * 1024
+
+NN = (((1,), (0,)), ((), ()))
+NT = (((1,), (1,)), ((), ()))
+TN = (((0,), (0,)), ((), ()))
+
+
+def dot(a, b, dims=NN):
+    return lax.dot_general(a, b, dims, preferred_element_type=F32)
+
+
+def when(cond, f):
+    if cond is None:
+        f()
+    else:
+        pl.when(cond)(f)
+
+
+def both(a, b):
+    if a is None:
+        return b
+    return a if b is None else a & b
+
+
+def place():
+    x = lax.axis_index("row")
+    s = lax.axis_index("seq")
+    return x, s, s // 4, (s // 2) % 2, s % 2
+
+
+def seat(z, y, c):
+    return z * 4 + y * 2 + c
+
+
+def remote(src, dst, send, recv, dev):
+    return pltpu.make_async_remote_copy(src, dst, send, recv, device_id=dev, device_id_type=MESH)
+
+
+def barrier_all():
+    x, s = lax.axis_index("row"), lax.axis_index("seq")
+    sem = pltpu.get_barrier_semaphore()
+    for k in range(1, 16):
+        pl.semaphore_signal(sem, inc=1, device_id=(x, (s + k) % 16), device_id_type=MESH)
+    for k in range(16):
+        pl.semaphore_signal(sem, inc=1, device_id=(1 - x, (s + k) % 16), device_id_type=MESH)
+    pl.semaphore_wait(sem, 31)
+
+
+def barrier_row(partner=False):
+    x, s = lax.axis_index("row"), lax.axis_index("seq")
+    sem = pltpu.get_barrier_semaphore()
+    for k in range(1, 16):
+        pl.semaphore_signal(sem, inc=1, device_id=(x, (s + k) % 16), device_id_type=MESH)
+    if partner:
+        pl.semaphore_signal(sem, inc=1, device_id=(1 - x, s), device_id_type=MESH)
+    pl.semaphore_wait(sem, 16 if partner else 15)
+
+
+def barrier_near():
+    x, s, z, y, c = place()
+    sem = pltpu.get_barrier_semaphore()
+    for cond, dev in (
+        (z < 3, (x, seat(z + 1, y, c))),
+        (z > 0, (x, seat(z - 1, y, c))),
+        (None, (x, seat(z, 1 - y, c))),
+        (None, (x, seat(z, y, 1 - c))),
+    ):
+        when(cond, lambda dev=dev: pl.semaphore_signal(sem, inc=1, device_id=dev, device_id_type=MESH))
+    pl.semaphore_wait(sem, 2 + (z < 3).astype(jnp.int32) + (z > 0).astype(jnp.int32))
+
+
+class Gather:
+    def __init__(self, own, at, send, recv):
+        self.own, self.at, self.send, self.recv = own, at, send, recv
+        self.sent = []
+        self.x, self.s, self.z, self.y, self.c = place()
+
+    def device(self, k):
+        x, z, y, c = self.x, self.z, self.y, self.c
+        return {
+            UP: (x, seat(z + 1, y, c)),
+            DOWN: (x, seat(z - 1, y, c)),
+            SIDE: (x, seat(z, 1 - y, c)),
+            CORE: (x, seat(z, y, 1 - c)),
+        }[k]
+
+    def copy(self, src, h, k, own):
+        ref = self.own(h) if own else self.at(src, h)
+        return remote(ref, self.at(src, h), self.send.at[src, h, k], self.recv.at[src, h], self.device(k))
+
+    def go(self, src, h, k, cond=None, own=False):
+        if k == UP:
+            cond = both(cond, self.z < 3)
+        if k == DOWN:
+            cond = both(cond, self.z > 0)
+        when(cond, lambda: self.copy(src, h, k, own).start())
+        self.sent.append((cond, src, h, k, own))
+
+    def wait(self, src, h, cond=None):
+        when(cond, lambda: self.copy(src, h, SIDE, False).wait_recv())
+
+    def begin(self):
+        own = self.own is not None
+        for h, k in ((0, UP), (0, DOWN), (1, SIDE), (0, SIDE), (1, UP), (1, DOWN), (0, CORE), (1, CORE)):
+            self.go(self.s, h, k, own=own)
+
+    def near(self):
+        src = seat(self.z, 1 - self.y, self.c)
+        self.wait(src, 1)
+        for k in (UP, DOWN, CORE):
+            self.go(src, 1, k)
+        self.wait(src, 0)
+        self.go(src, 0, CORE)
+
+    def step(self, t):
+        z, y, c = self.z, self.y, self.c
+        for cond, zz, k in ((z - t >= 0, z - t, UP), (z + t <= 3, z + t, DOWN)):
+            mine, other = seat(zz, y, c), seat(zz, 1 - y, c)
+            self.wait(mine, 0, cond)
+            for way in (k, SIDE, CORE):
+                self.go(mine, 0, way, cond)
+            self.wait(mine, 1, cond)
+            for way in (k, CORE):
+                self.go(mine, 1, way, cond)
+            self.wait(other, 1, cond)
+            for way in (k, CORE):
+                self.go(other, 1, way, cond)
+
+    def step_side(self, t):
+        z, y, c = self.z, self.y, self.c
+        for cond, zz in ((z - t >= 0, z - t), (z + t <= 3, z + t)):
+            other = seat(zz, 1 - y, c)
+            self.wait(other, 0, cond)
+            self.go(other, 0, CORE, cond)
+
+    def end_core(self):
+        for zz in range(4):
+            for yy in range(2):
+                for h in range(2):
+                    self.wait(seat(zz, yy, 1 - self.c), h)
+
+    def end_sends(self):
+        for cond, src, h, k, own in self.sent:
+            when(cond, lambda: self.copy(src, h, k, own).wait_send())
+
+
+GATHER_SEMS = [DMA((16, 2, 4)), DMA((16, 2))]
+
+
+def run_gathers(gathers):
+    for g in gathers:
+        g.begin()
+    for g in gathers:
+        g.near()
+    for t in (1, 2, 3):
+        for g in gathers:
+            g.step(t)
+    for t in (1, 2, 3):
+        for g in gathers:
+            g.step_side(t)
+    for g in gathers:
+        g.end_core()
+    for g in gathers:
+        g.end_sends()
+
+
+class Exchange:
+    def __init__(self, src, dst, send, recv, wide=False):
+        x, s = lax.axis_index("row"), lax.axis_index("seq")
+        self.me = x * 16 + s if wide else s
+        self.n = 32 if wide else 16
+        self.device = (lambda r: (r // 16, r % 16)) if wide else (lambda r: (x, r))
+        self.src, self.dst, self.send, self.recv = src, dst, send, recv
+
+    def copy(self, k):
+        to = (self.me + k) % self.n
+        return remote(self.src(to), self.dst(self.me), self.send.at[k], self.recv.at[k], self.device(to))
+
+    def begin(self):
+        self.local = pltpu.make_async_copy(self.src(self.me), self.dst(self.me), self.recv.at[0])
+        self.local.start()
+        for k in range(1, self.n):
+            self.copy(k).start()
+
+    def arrive(self, k):
+        frm = (self.me + self.n - k) % self.n
+        remote(self.src(self.me), self.dst(frm), self.send.at[k], self.recv.at[k], self.device(frm)).wait_recv()
+        return frm
+
+    def end(self, arrivals=True):
+        self.local.wait()
+        for k in range(1, self.n):
+            if arrivals:
+                self.arrive(k)
+            self.copy(k).wait_send()
+
+
+def comm_call(body, outs, ins, sems, cid, scratch=()):
+    return pl.pallas_call(
+        body,
+        out_shape=outs,
+        in_specs=[pl.BlockSpec(memory_space=VM)] * len(ins),
+        out_specs=[pl.BlockSpec(memory_space=VM)] * len(outs),
+        scratch_shapes=list(scratch) + list(sems),
+        compiler_params=pltpu.CompilerParams(
+            collective_id=cid, has_side_effects=True, vmem_limit_bytes=VMEM_LIMIT
+        ),
+    )(*ins)
+
+
+def compute_call(body, outs, ins, scratch=()):
+    return pl.pallas_call(
+        body,
+        out_shape=outs,
+        in_specs=[pl.BlockSpec(memory_space=VM)] * len(ins),
+        out_specs=[pl.BlockSpec(memory_space=VM)] * len(outs),
+        scratch_shapes=list(scratch),
+        compiler_params=pltpu.CompilerParams(vmem_limit_bytes=VMEM_LIMIT),
+    )(*ins)
+
+
+def sds(shape, dtype):
+    return jax.ShapeDtypeStruct(shape, dtype)
+
+
+def gather_first(tok, wperm, small, wo, tok_all, w_mine, small_all, wo_all, *sems):
+    x, s, z, y, c = place()
+    t_send, t_recv, o_send, o_recv, w_send, w_recv, s_send, s_recv, x_sem = sems
+    barrier_all()
+    over = remote(wo, wo_all.at[x, s], x_sem.at[0], x_sem.at[1], (1 - x, s))
+    over.start()
+    tokens = Gather(lambda h: tok.at[h], lambda src, h: tok_all.at[src, h], t_send, t_recv)
+    tokens.begin()
+    keep_tok = pltpu.make_async_copy(tok, tok_all.at[s], x_sem.at[2])
+    keep_tok.start()
+    keep = pltpu.make_async_copy(wo, wo_all.at[x, s], x_sem.at[3])
+    keep.start()
+    minor = Exchange(lambda r: small, lambda r: small_all.at[r], s_send, s_recv, wide=True)
+    minor.begin()
+    slices = Exchange(
+        lambda r: wperm.at[:, pl.ds(pl.multiple_of(((r % 16) // 2) * 256, 256), 256)],
+        lambda r: w_mine.at[r],
+        w_send,
+        w_recv,
+        wide=True,
+    )
+    slices.begin()
+    keep.wait()
+    remote(wo, wo_all.at[1 - x, s], x_sem.at[0], x_sem.at[1], (1 - x, s)).wait_recv()
+    outw = Gather(None, lambda src, h: wo_all.at[h, src], o_send, o_recv)
+    outw.begin()
+    tokens.near()
+    outw.near()
+    for t in (1, 2, 3):
+        tokens.step(t)
+        outw.step(t)
+    for t in (1, 2, 3):
+        tokens.step_side(t)
+        outw.step_side(t)
+    tokens.end_core()
+    outw.end_core()
+    minor.end()
+    slices.end()
+    tokens.end_sends()
+    outw.end_sends()
+    keep_tok.wait()
+    over.wait_send()
+
+
+QB = 256
+
+
+def allowed_mask(first_key, first_query, start_row):
+    key = first_key + lax.broadcasted_iota(jnp.int32, (QB, QB), 0)
+    query = first_query + lax.broadcasted_iota(jnp.int32, (QB, QB), 1)
+    return (key <= query) & (key >= start_row)
+
+
+def lane_block(i, size=QB):
+    return pl.ds(pl.multiple_of(i * size, size), size)
+
+
+SCORE = math.log2(math.e) / math.sqrt(HEAD_SIZE)
+
+
+def attention_forward(
+    tok, w_mine, small, cos, sin, start, hid, q_t, k_t, v_t, o_t, lse, o_low, k_n, gain, w_t
+):
+    core = lax.axis_index("seq") % 2
+    gain[...] = jnp.transpose(small[...].astype(F32))
+    w_t[...] = jnp.transpose(w_mine[...].astype(F32)).astype(BF)
+
+    def project(i, _):
+        rows = lane_block(i, 512)
+        values = tok[rows, :].astype(F32)
+        scale = lax.rsqrt(jnp.mean(values * values, axis=-1, keepdims=True) + EPSILON)
+        hidden = (values * scale * gain[E : E + 1, :]).astype(BF)
+        hid[rows, :] = hidden
+        made = dot(w_t[...], hidden, NT)
+        co, si = cos[:, rows], sin[:, rows]
+        own = jnp.where(core == 0, made[0:64], made[128:192])
+        for ref, part in ((q_t, own), (k_t, made[64:128])):
+            a, b = part[:32], part[32:]
+            ref[0:32, rows] = (a * co - b * si).astype(BF)
+            ref[32:64, rows] = (b * co + a * si).astype(BF)
+        v_t[:, rows] = made[192:256].astype(BF)
+        k_n[rows, :] = jnp.transpose(k_t[:, rows].astype(F32)).astype(BF)
+        return 0
+
+    lax.fori_loop(0, 4, project, 0)
+
+    def query_block(i, _):
+        cols = lane_block(i)
+        queries = q_t[:, cols]
+        begin = start[:, cols]
+
+        def key_block(j, carried):
+            top, total, acc = carried
+            rows = lane_block(j)
+            scores = dot(k_n[rows, :], queries) * SCORE
+            scores = jnp.where(allowed_mask(j * QB, i * QB, begin), scores, MASKED)
+            fresh = jnp.maximum(top, jnp.max(scores, axis=0, keepdims=True))
+            weights = jnp.exp2(scores - fresh)
+            decay = jnp.exp2(top - fresh)
+            total = total * decay + jnp.sum(weights, axis=0, keepdims=True)
+            acc = acc * decay + dot(v_t[:, rows], weights.astype(BF))
+            return fresh, total, acc
+
+        top, total, acc = lax.fori_loop(
+            0,
+            i + 1,
+            key_block,
+            (jnp.full((1, QB), MASKED, F32), jnp.zeros((1, QB), F32), jnp.zeros((HEAD_SIZE, QB), F32)),
+        )
+        out = acc / total
+        o_t[:, cols] = out
+        o_low[:, cols] = out.astype(BF)
+        lse[:, cols] = top + jnp.log2(total)
+        return 0
+
+    lax.fori_loop(0, tok.shape[0] // QB, query_block, 0)
+
+
+def heads_to_tokens(o_low, w3, att_t, wexp, *sems):
+    a_send, a_recv, w_send, w_recv, x_send, x_recv = sems
+    x, s, z, y, c = place()
+    barrier_row(partner=True)
+    heads = Exchange(lambda t: o_low.at[:, lane_block(t, 128)], lambda h: att_t.at[h], a_send, a_recv)
+    heads.begin()
+    weights = Exchange(lambda e: w3.at[e], lambda r: wexp.at[:, x * 16 + r], w_send, w_recv)
+    weights.begin()
+    over = []
+
+    def cross(k, src, row):
+        copy = remote(src, wexp.at[:, x * 16 + row], x_send.at[k], x_recv.at[k], (1 - x, s))
+        copy.start()
+        over.append(copy)
+
+    cross(0, w3.at[s], s)
+    for k in range(1, 16):
+        frm = weights.arrive(k)
+        cross(k, wexp.at[:, x * 16 + frm], frm)
+    heads.end()
+    weights.end(arrivals=False)
+    for k, copy in enumerate(over):
+        copy.wait_send()
+        frm = (s + 16 - k) % 16
+        remote(
+            wexp.at[:, 0], wexp.at[:, (1 - x) * 16 + frm], x_send.at[k], x_recv.at[k], (1 - x, s)
+        ).wait_recv()
+
+
+def between(tok, att_t, wo, small, routes, residual, normed, scale_out, h2, att, probs, picked, p_t):
+    gain = jnp.transpose(small[...].astype(F32))[E + 1 : E + 2, :]
+    att[...] = jnp.transpose(att_t[...].astype(F32)).astype(BF)
+    res = tok[...].astype(F32) + dot(att[...], wo[...], NT)
+    residual[...] = res
+    scale = lax.rsqrt(jnp.mean(res * res, axis=-1, keepdims=True) + EPSILON)
+    norm = res * scale
+    normed[...] = norm
+    scale_out[...] = jnp.broadcast_to(scale, scale_out.shape)
+    hidden = (norm * gain).astype(BF)
+    h2[...] = hidden
+    lanes = lax.broadcasted_iota(jnp.int32, (128, 128), 1)
+    logits = jnp.where(lanes < E, dot(hidden, small[...]), MASKED)
+    top = jnp.max(logits, axis=-1, keepdims=True)
+    weights = jnp.exp(logits - top)
+    prob = weights / jnp.sum(weights, axis=-1, keepdims=True)
+    probs[...] = prob
+    mask = jnp.zeros((128, 128), F32)
+    for k in range(K):
+        mask = mask + jnp.where(lanes == routes[:, k : k + 1], 1.0, 0.0)
+    picked[...] = mask
+    p_t[...] = jnp.transpose(prob * mask)[0:E, :]
+
+
+def gather_second(h2, p_t, h_all, p_all, *sems):
+    h_send, h_recv, p_send, p_recv, keep_sem = sems
+    x, s, z, y, c = place()
+    barrier_row()
+    hidden = Gather(lambda h: h2.at[h], lambda src, h: h_all.at[src, h], h_send, h_recv)
+    hidden.begin()
+    keep = pltpu.make_async_copy(h2, h_all.at[s], keep_sem.at[0])
+    keep.start()
+    minor = Exchange(lambda r: p_t, lambda r: p_all.at[r], p_send, p_recv)
+    minor.begin()
+    hidden.near()
+    for t in (1, 2, 3):
+        hidden.step(t)
+    for t in (1, 2, 3):
+        hidden.step_side(t)
+    hidden.end_core()
+    hidden.end_sends()
+    minor.end()
+    keep.wait()
+
+
+TB = 512
+
+
+def expert_body(h_all, cot, p_all, wexp, mixp, backp, gg, dw, acc):
+    e = lax.axis_index("seq")
+    acc[...] = jnp.zeros(acc.shape, F32)
+
+    def chunk(i, _):
+        rows = lane_block(i, TB)
+        hidden, grad = h_all[rows, :], cot[rows, :]
+        cols = [jnp.broadcast_to(p_all[i * 4 + b, pl.ds(e, 1), :], (128, 128)) for b in range(4)]
+        prob = jnp.concatenate([jnp.transpose(v)[:, 0:1] for v in cols], axis=0)
+        gate = dot(hidden, wexp[0])
+        up = dot(hidden, wexp[1])
+        sig = 1.0 / (1.0 + jnp.exp(-gate))
+        silu = gate * sig
+        act = silu * up
+        low = act.astype(BF)
+        out = dot(low, wexp[2], NT)
+        mixp[rows, :] = (prob * out).astype(BF)
+        back = dot(grad, wexp[2])
+        seen = jnp.sum(low.astype(F32) * back, axis=-1, keepdims=True)
+        for b in range(4):
+            line = jnp.transpose(jnp.broadcast_to(seen[b * 128 : b * 128 + 128], (128, 128)))[0:8]
+            gg[i * 4 + b] = line
+        grad_hidden = back * prob
+        grad_gate = (grad_hidden * up * (sig * (1.0 + gate * (1.0 - sig)))).astype(BF)
+        grad_up = (grad_hidden * silu).astype(BF)
+        backp[rows, :] = (dot(grad_gate, wexp[0], NT) + dot(grad_up, wexp[1], NT)).astype(BF)
+        acc[0] += dot(hidden, grad_gate, TN)
+        acc[1] += dot(hidden, grad_up, TN)
+        acc[2] += dot(grad, (prob * low.astype(F32)).astype(BF), TN)
+        return 0
+
+    lax.fori_loop(0, h_all.shape[0] // TB, chunk, 0)
+    dw[...] = acc[...].astype(BF)
+
+
+class Reduce:
+    def __init__(self, part, out, bufs, sems):
+        self.part, self.out = part, out
+        self.r1, self.ra, self.ua, self.da, self.ub, self.db, self.rb = bufs
+        (self.s1, self.q1, self.sa, self.qa, self.su, self.qu, self.sd, self.qd, self.sb) = sems
+        self.x, self.s, self.z, self.y, self.c = place()
+        self.pending = []
+
+    @staticmethod
+    def bufs(rows, width):
+        b = (rows, width)
+        return [
+            VM((4, 2, 2) + b, BF),
+            VM((4,) + b, BF),
+            VM((4,) + b, BF),
+            VM((4,) + b, BF),
+            VM((2, 4) + b, BF),
+            VM((2, 4) + b, BF),
+            VM(b, BF),
+        ]
+
+    SEMS = [DMA((4, 2)), DMA((4, 2)), DMA((4,)), DMA((4,)), DMA((3, 4)), DMA((3, 4)), DMA((3, 4)), DMA((3, 4)), DMA((2,))]
+
+    def add(self, dst, src):
+        dst[...] = (dst[...].astype(F32) + src[...].astype(F32)).astype(BF)
+
+    def first(self, zz, yy):
+        return remote(
+            self.part.at[seat(zz, yy, 1 - self.c)],
+            self.r1.at[zz, yy],
+            self.s1.at[zz, yy],
+            self.q1.at[zz, yy],
+            (self.x, seat(self.z, self.y, 1 - self.c)),
+        )
+
+    def side(self, zz):
+        return remote(
+            self.r1.at[zz, 1 - self.y, 0],
+            self.ra.at[zz],
+            self.sa.at[zz],
+            self.qa.at[zz],
+            (self.x, seat(self.z, 1 - self.y, self.c)),
+        )
+
+    def line(self, lane, zz, up):
+        z, y, c = self.z, self.y, self.c
+        src = self.ra.at[zz] if lane == 0 else self.r1.at[zz, lane - 1, 1]
+        if up:
+            dst = self.ua.at[zz] if lane == 0 else self.ub.at[lane - 1, zz]
+            return remote(src, dst, self.su.at[lane, zz], self.qu.at[lane, zz], (self.x, seat(z + 1, y, c)))
+        dst = self.da.at[zz] if lane == 0 else self.db.at[lane - 1, zz]
+        return remote(src, dst, self.sd.at[lane, zz], self.qd.at[lane, zz], (self.x, seat(z - 1, y, c)))
+
+    def landed(self, lane, zz, up):
+        if lane == 0:
+            return (self.ua if up else self.da).at[zz]
+        return (self.ub if up else self.db).at[lane - 1, zz]
+
+    def held(self, lane, zz):
+        return self.ra.at[zz] if lane == 0 else self.r1.at[zz, lane - 1, 1]
+
+    def order(self):
+        z = self.z
+        for t in (3, 2, 1):
+            yield z + t <= 3, z + t, True
+            yield z - t >= 0, z - t, False
+        yield None, z, None
+
+    def begin(self):
+        for cond, zz, _ in self.order():
+            for yy in range(2):
+                when(cond, lambda: self.first(zz, yy).start())
+
+    def pass_on(self, lane, zz, up, cond):
+        def go():
+            def add():
+                self.line(lane, zz, up).wait_recv()
+                self.add(self.held(lane, zz), self.landed(lane, zz, up))
+
+            pl.when(self.z > 0 if up else self.z < 3)(add)
+            self.line(lane, zz, up).start()
+
+        when(cond, go)
+
+    def core_step(self, cond, zz):
+        def go():
+            for yy in range(2):
+                self.first(zz, yy).wait_recv()
+                mine = self.part.at[seat(zz, yy, self.c)]
+                self.add(self.r1.at[zz, yy], mine)
+            self.side(zz).start()
+
+        when(cond, go)
+
+    def run(self):
+        order = list(self.order())
+        for cond, zz, up in order:
+            self.core_step(cond, zz)
+            if up is not None:
+                for lane in (1, 2):
+                    at_end = (self.z == 0) if up else (self.z == 3)
+                    when(both(cond, at_end), lambda: self.line(lane, zz, up).start())
+        for cond, zz, up in order:
+
+            def ready():
+                self.side(zz).wait_recv()
+                self.add(self.ra.at[zz], self.r1.at[zz, self.y, 0])
+
+            when(cond, ready)
+            if up is None:
+                continue
+            inner = (self.z > 0) if up else (self.z < 3)
+            for lane in (1, 2):
+                self.pass_on(lane, zz, up, both(cond, inner))
+            self.pass_on(0, zz, up, cond)
+        z = self.z
+        for lane in (1, 2, 0):
+            for up, cond in ((True, z > 0), (False, z < 3)):
+
+                def take():
+                    self.line(lane, z, up).wait_recv()
+                    self.add(self.held(lane, z), self.landed(lane, z, up))
+
+                when(cond, take)
+            if lane == 2:
+                self.last().start()
+        self.out[0] = self.ra[z]
+        self.last().wait_recv()
+        self.out[1] = (self.r1[z, self.y, 1].astype(F32) + self.rb[...].astype(F32)).astype(BF)
+
+    def last(self):
+        return remote(
+            self.r1.at[self.z, 1 - self.y, 1],
+            self.rb,
+            self.sb.at[0],
+            self.sb.at[1],
+            (self.x, seat(self.z, 1 - self.y, self.c)),
+        )
+
+    def end(self):
+        for cond, zz, up in self.order():
+            for yy in range(2):
+                when(cond, lambda: self.first(zz, yy).wait_send())
+            when(cond, lambda: self.side(zz).wait_send())
+            if up is not None:
+                for lane in range(3):
+                    when(cond, lambda: self.line(lane, zz, up).wait_send())
+        self.last().wait_send()
+
+
+NBUF = 7
+NSEM = 9
+
+
+def reduce_rows(backp, mixp, gg, back, mix, g_all, *rest):
+    bufs_a, bufs_b = rest[:NBUF], rest[NBUF : 2 * NBUF]
+    sems = rest[2 * NBUF :]
+    barrier_row()
+    one = Reduce(backp, back, bufs_a, sems[:NSEM])
+    two = Reduce(mixp, mix, bufs_b, sems[NSEM : 2 * NSEM])
+    g_send, g_recv = sems[2 * NSEM :]
+    one.begin()
+    minor = Exchange(lambda r: gg.at[r], lambda r: g_all.at[r], g_send, g_recv)
+    minor.begin()
+    one.run()
+    two.begin()
+    two.run()
+    one.end()
+    two.end()
+    minor.end()
+
+
+def back_between(
+    back, g_all, cot, probs, picked, normed, scale, small, wo, att, h2, g_res, ga_t, dwo
+):
+    gain = jnp.transpose(small[...].astype(F32))[E + 1 : E + 2, :]
+    seen = jnp.concatenate([g_all[e, 0:1, :] for e in range(E)] + [jnp.zeros((128 - E, 128), F32)], axis=0)
+    grad_probs = jnp.transpose(seen) * picked[...]
+    prob = probs[...]
+    grad_logits = (prob * (grad_probs - jnp.sum(prob * grad_probs, axis=-1, keepdims=True))).astype(BF)
+    grad_second = back[...].astype(F32) + dot(grad_logits, small[...], NT)
+    u = grad_second * gain
+    norm = normed[...]
+    grad = cot[...].astype(F32) + scale[:, 0:1] * (u - norm * jnp.mean(u * norm, axis=-1, keepdims=True))
+    g_res[...] = grad
+    branch = grad.astype(BF)
+    ga_t[...] = jnp.transpose(dot(branch, wo[...])).astype(BF)
+    dwo[:, 0:1024] = dot(jnp.transpose(grad).astype(BF), att[...]).astype(BF)
+    dwo[:, 1024:1152] = dot(h2[...], grad_logits, TN).astype(BF)
+
+
+def grads_out(ga_t, dw, dwo, go_t, dw_all, dwo_sum, *rest):
+    bufs = rest[:NBUF]
+    dwx, dwo_x = rest[NBUF : NBUF + 2]
+    sems = rest[NBUF + 2 :]
+    a_send, a_recv, w_send, w_recv, x_sem = sems[NSEM:]
+    x, s, z, y, c = place()
+    barrier_row(partner=True)
+    heads = Exchange(lambda h: ga_t.at[h], lambda t: go_t.at[:, lane_block(t, 128)], a_send, a_recv)
+    heads.begin()
+    over = remote(dw.at[:, 1 - x], dwx, x_sem.at[0], x_sem.at[1], (1 - x, s))
+    over.start()
+    over_o = remote(dwo.at[1 - x], dwo_x, x_sem.at[2], x_sem.at[3], (1 - x, s))
+    over_o.start()
+    over_o.wait_recv()
+    dwo_x[...] = (dwo_x[...].astype(F32) + dwo[x].astype(F32)).astype(BF)
+    out = Reduce(dwo_x, dwo_sum, bufs, sems[:NSEM])
+    out.begin()
+    out.run()
+    over.wait_recv()
+    dwx[...] = (dwx[...].astype(F32) + dw[:, x].astype(F32)).astype(BF)
+    weights = Exchange(lambda r: dwx.at[:, r], lambda e: dw_all.at[e], w_send, w_recv)
+    weights.begin()
+    weights.end()
+    heads.end()
+    out.end()
+    over.wait_send()
+    over_o.wait_send()
+
+
+def attention_backward(q_t, k_t, v_t, lse, o_t, go_t, start, gq_t, gkv_t, k_n, v_n, delta):
+    k_n[...] = jnp.transpose(k_t[...].astype(F32)).astype(BF)
+    v_n[...] = jnp.transpose(v_t[...].astype(F32)).astype(BF)
+    gkv_t[...] = jnp.zeros(gkv_t.shape, F32)
+    delta[...] = jnp.sum(go_t[...].astype(F32) * o_t[...], axis=0, keepdims=True)
+
+    def query_block(i, _):
+        cols = lane_block(i)
+        queries, grads = q_t[:, cols], go_t[:, cols]
+        begin, log_total, shift = start[:, cols], lse[:, cols], delta[:, cols]
+
+        def key_block(j, acc):
+            rows = lane_block(j)
+            scores = dot(k_n[rows, :], queries) * SCORE
+            weights = jnp.where(
+                allowed_mask(j * QB, i * QB, begin), jnp.exp2(scores - log_total), 0.0
+            )
+            moved = dot(v_n[rows, :], grads)
+            grad_scores = (weights * (moved - shift)).astype(BF)
+            gkv_t[0:64, rows] += dot(queries, grad_scores, NT)
+            gkv_t[64:128, rows] += dot(grads, weights.astype(BF), NT)
+            return acc + dot(k_t[:, rows], grad_scores)
+
+        gq_t[:, cols] = lax.fori_loop(0, i + 1, key_block, jnp.zeros((HEAD_SIZE, QB), F32))
+        return 0
+
+    lax.fori_loop(0, q_t.shape[1] // QB, query_block, 0)
+
+
+def share_pair(gkv, got, send, recv):
+    x, s, z, y, c = place()
+    sem = pltpu.get_barrier_semaphore()
+    mate = (x, seat(z, y, 1 - c))
+    pl.semaphore_signal(sem, inc=1, device_id=mate, device_id_type=MESH)
+    pl.semaphore_wait(sem, 1)
+    copy = remote(gkv.at[1 - c], got, send, recv, mate)
+    copy.start()
+    copy.wait()
+
+
+def back_projection(gq_t, gkv, got, hid, cos, sin, g_t, wg):
+    core = lax.axis_index("seq") % 2
+    scaling = 1.0 / math.sqrt(HEAD_SIZE)
+    co, si = cos[...], sin[...]
+
+    def unturn(part):
+        a, b = part[:32], part[32:]
+        return jnp.concatenate([a * co + b * si, b * co - a * si], axis=0)
+
+    g_t[0:64, :] = unturn(gq_t[...] * scaling).astype(BF)
+    mine = gkv[core] + got[...]
+    g_t[64:128, :] = jnp.where(core == 0, unturn(mine * scaling), mine).astype(BF)
+    wg[...] = jnp.transpose(dot(g_t[...], hid[...])).astype(BF)
+
+
+def last_exchange(g_t, wg, g_mine, wg_all, *sems):
+    a_send, a_recv, w_send, w_recv = sems
+    barrier_all()
+    heads = Exchange(lambda t: g_t.at[:, lane_block(t, 128)], lambda h: g_mine.at[h], a_send, a_recv)
+    heads.begin()
+    weights = Exchange(lambda r: wg.at[r], lambda r: wg_all.at[r], w_send, w_recv, wide=True)
+    weights.begin()
+    heads.end()
+    weights.end()
+
+
+def last_rows(g_mine, wp, tok, small, g_res, grad_tokens):
+    gain = jnp.transpose(small[...].astype(F32))[E : E + 1, :]
+    first = jnp.transpose(dot(wp[...], g_mine[...]))
+    values = tok[...].astype(F32)
+    scale = lax.rsqrt(jnp.mean(values * values, axis=-1, keepdims=True) + EPSILON)
+    norm = values * scale
+    w = first * gain
+    grad_tokens[...] = g_res[...] + scale * (w - norm * jnp.mean(w * norm, axis=-1, keepdims=True))
+
+
+def frequencies(head_dim):
+    halves = head_dim // 2
+    return jnp.power(ROPE_BASE, -jnp.arange(halves, dtype=F32) * (2.0 / head_dim))
+
+
+def sixteen_seats(
+    tokens,
+    attention_gain,
+    expert_gain,
+    query_weight,
+    key_matrix,
+    value_matrix,
+    output_weight,
+    router_weight,
+    gate_weight,
+    up_weight,
+    down_weight,
+    routes,
+    segments,
+    rope_index,
+    cotangent,
+):
+    D = MODEL_WIDTH
+    rows = tokens.shape[1]
+    length = 16 * rows
+    pair = jnp.stack([key_matrix.reshape(32, 8, 64), value_matrix.reshape(32, 8, 64)], axis=2).reshape(32, 16, 64)
+    wperm = jnp.concatenate([query_weight.reshape(32, 16, 64), pair], axis=2).reshape(32, 2048)
+    small = jnp.concatenate(
+        [router_weight, attention_gain[:, None], expert_gain[:, None], jnp.zeros((32, 128 - E - 2), BF)], axis=1
+    )
+    w3 = jnp.stack([gate_weight, up_weight, down_weight]).transpose(2, 0, 1, 3)
+    angle = (
+        jnp.arange(length, dtype=F32)[None, :] / jnp.power(2.0, rope_index.astype(F32))[:, None]
+    ) * frequencies(HEAD_SIZE)[:, None]
+    cos, sin = jnp.cos(angle), jnp.sin(angle)
+    segment_all = lax.all_gather(segments.astype(jnp.int32), "seq", axis=1, tiled=True)
+    start = jnp.sum((segment_all[:, None, :] < segment_all[:, :, None]).astype(jnp.int32), axis=-1, dtype=jnp.int32)
+    wp_all = lax.all_gather(wperm, ("row", "seq"), axis=0, tiled=True)
+    cot_all = lax.all_gather(cotangent[0], "seq", axis=0, tiled=True)
+
+    tok_all, w_mine, small_all, wo_all = comm_call(
+        gather_first,
+        [sds((16, 2, rows // 2, D), BF), sds((32, 32, 256), BF), sds((32, 32, 128), BF), sds((2, 16, 32, D), BF)],
+        [tokens.reshape(2, rows // 2, D), wperm, small, output_weight],
+        GATHER_SEMS * 2 + [DMA((32,))] * 4 + [DMA((4,))],
+        0,
+    )
+    small_all = small_all.reshape(D, 128)
+    wo_all = wo_all.reshape(D, D)
+    hid, q_t, k_t, v_t, o_t, lse, o_low = compute_call(
+        attention_forward,
+        [
+            sds((length, D), BF),
+            sds((64, length), BF),
+            sds((64, length), BF),
+            sds((64, length), BF),
+            sds((64, length), F32),
+            sds((1, length), F32),
+            sds((64, length), BF),
+        ],
+        [tok_all.reshape(length, D), w_mine.reshape(D, 256), small_all, cos, sin, start],
+        [VM((length, 64), BF), VM((128, D), F32), VM((256, D), BF)],
+    )
+    att_t, wexp = comm_call(
+        heads_to_tokens,
+        [sds((16, 64, rows), BF), sds((3, 32, 32, F), BF)],
+        [o_low, w3],
+        [DMA((16,))] * 6,
+        1,
+    )
+    tok_mine = tokens.reshape(rows, D)
+    residual, normed, scale, h2, att, probs, picked, p_t = compute_call(
+        between,
+        [
+            sds((rows, D), F32),
+            sds((rows, D), F32),
+            sds((rows, 128), F32),
+            sds((rows, D), BF),
+            sds((rows, D), BF),
+            sds((rows, 128), F32),
+            sds((rows, 128), F32),
+            sds((E, rows), F32),
+        ],
+        [tok_mine, att_t.reshape(D, rows), wo_all, small_all, routes.reshape(rows, K)],
+    )
+    h_all, p_all = comm_call(
+        gather_second,
+        [sds((16, 2, rows // 2, D), BF), sds((16, E, rows), F32)],
+        [h2.reshape(2, rows // 2, D), p_t],
+        GATHER_SEMS + [DMA((16,))] * 2 + [DMA((1,))],
+        2,
+    )
+    mixp, backp, gg, dw = compute_call(
+        expert_body,
+        [sds((length, D), BF), sds((length, D), BF), sds((16, 8, 128), F32), sds((3, D, F), BF)],
+        [h_all.reshape(length, D), cot_all, p_all, wexp.reshape(3, D, F)],
+        [VM((3, D, F), F32)],
+    )
+    back, mix, g_all = comm_call(
+        reduce_rows,
+        [sds((2, rows // 2, D), BF), sds((2, rows // 2, D), BF), sds((16, 8, 128), F32)],
+        [backp.reshape(16, 2, rows // 2, D), mixp.reshape(16, 2, rows // 2, D), gg],
+        Reduce.SEMS * 2 + [DMA((16,))] * 2,
+        3,
+        Reduce.bufs(rows // 2, D) * 2,
+    )
+    mixed = (residual + mix.reshape(rows, D).astype(F32)).astype(BF)
+    g_res, ga_t, dwo = compute_call(
+        back_between,
+        [sds((rows, D), F32), sds((D, rows), BF), sds((D, D + 128), BF)],
+        [
+            back.reshape(rows, D),
+            g_all,
+            cotangent.reshape(rows, D),
+            probs,
+            picked,
+            normed,
+            scale,
+            small_all,
+            wo_all,
+            att,
+            h2,
+        ],
+    )
+    go_t, dw_all, dwo_sum = comm_call(
+        grads_out,
+        [sds((64, length), BF), sds((16, 3, 32, F), BF), sds((2, 16, D + 128), BF)],
+        [ga_t.reshape(16, 64, rows), dw.reshape(3, 2, 16, 32, F), dwo.reshape(2, 16, 2, 16, D + 128)],
+        Reduce.SEMS + [DMA((16,))] * 4 + [DMA((4,))],
+        4,
+        Reduce.bufs(16, D + 128) + [VM((3, 16, 32, F), BF), VM((16, 2, 16, D + 128), BF)],
+    )
+    gq_t, gkv_t = compute_call(
+        attention_backward,
+        [sds((64, length), F32), sds((128, length), F32)],
+        [q_t, k_t, v_t, lse, o_t, go_t, start],
+        [VM((length, 64), BF), VM((length, 64), BF), VM((1, length), F32)],
+    )
+    gkv = gkv_t.reshape(2, 64, length)
+    (got,) = comm_call(share_pair, [sds((64, length), F32)], [gkv], [DMA, DMA], 5)
+    g_t, wg = compute_call(
+        back_projection, [sds((128, length), BF), sds((D, 128), BF)], [gq_t, gkv, got, hid, cos, sin]
+    )
+    g_mine, wg_all = comm_call(
+        last_exchange,
+        [sds((16, 128, rows), BF), sds((32, 32, 128), BF)],
+        [g_t, wg.reshape(32, 32, 128)],
+        [DMA((16,))] * 2 + [DMA((32,))] * 2,
+        6,
+    )
+    (grad_tokens,) = compute_call(
+        last_rows, [sds((rows, D), F32)], [g_mine.reshape(2 * D, rows), wp_all, tok_mine, small_all, g_res]
+    )
+    wg_sum = wg_all.reshape(2, 16, 32, 128).astype(F32).sum(axis=0).transpose(1, 0, 2)
+    grad_query_weight = wg_sum[:, :, :64].reshape(32, D)
+    grad_key_weight = wg_sum[:, 0::2, 64:].reshape(32, 512)
+    grad_value_weight = wg_sum[:, 1::2, 64:].reshape(32, 512)
+    own_o = dwo_sum.reshape(32, D + 128).astype(F32)
+    grad_output_weight, grad_router_weight = own_o[:, :D], own_o[:, D : D + E]
+    expert_grads = dw_all.transpose(1, 2, 0, 3).astype(F32)
+    grad_gate_weight, grad_up_weight, grad_down_weight = expert_grads[0], expert_grads[1], expert_grads[2]
+    grad_attention_gain = (
+        jnp.sum(grad_query_weight * query_weight.astype(F32), axis=1)
+        + jnp.sum(grad_key_weight * key_matrix.astype(F32), axis=1)
+        + jnp.sum(grad_value_weight * value_matrix.astype(F32), axis=1)
+    ) / attention_gain.astype(F32)
+    grad_expert_gain = (
+        jnp.sum(grad_gate_weight * gate_weight.astype(F32) + grad_up_weight * up_weight.astype(F32), axis=(1, 2))
+        + jnp.sum(grad_router_weight * router_weight.astype(F32), axis=1)
+    ) / expert_gain.astype(F32)
+    return (
+        mixed.reshape(tokens.shape),
+        grad_tokens.reshape(tokens.shape),
+        grad_attention_gain,
+        grad_expert_gain,
+        grad_query_weight,
+        grad_key_weight,
+        grad_value_weight,
+        grad_output_weight,
+        grad_router_weight,
+        grad_gate_weight,
+        grad_up_weight,
+        grad_down_weight,
+    )
 
 
 def rms_scale(values):
     return lax.rsqrt(jnp.mean(values * values, axis=-1, keepdims=True) + EPSILON)
-
-
-def frequencies(head_dim):
-    halves = head_dim // 2
-    return jnp.power(ROPE_BASE, -jnp.arange(halves, dtype=jnp.float32) * (2.0 / head_dim))
 
 
 def apply_rotary(values, cosine_lookup, sine_lookup):
@@ -208,7 +1145,7 @@
     ).reshape(experts, sequence_count * capacity, width)
 
 
-def per_device(
+def any_seats(
     tokens,
     attention_gain,
     expert_gain,
@@ -341,51 +1278,56 @@
     grad_mixed = cotangent.astype(jnp.float32)
     grad_slot_values = (gate_probs[..., None] * grad_mixed[:, :, None, :]).astype(jnp.bfloat16)
     grad_expert = place_slots(grad_slot_values, destination, E, CAP)
-    gate_pre, up_pre = project_in(
+    groups = 4
+    width = E // groups
+
+    def some_experts(_, given):
+        rows, grads, gate_part, up_part, down_part = given
+        pieces = (
+            lax.all_gather(gate_part, ("row", "seq"), axis=0, tiled=True),
+            lax.all_gather(up_part, ("row", "seq"), axis=0, tiled=True),
+        )
+        down_rows = lax.all_gather(down_part, ("row", "seq"), axis=0, tiled=True)
+        gate_pre, up_pre = project_in(pieces, routed=rows)
+        hidden_low = (jax.nn.silu(gate_pre) * up_pre).astype(jnp.bfloat16)
+        expert_out = project_out(down_rows, hidden=hidden_low)
+        grad_hidden = back_through_down(down_rows, grad_output=grads)
+        sigmoid_gate = jax.nn.sigmoid(gate_pre)
+        grad_gate = (
+            grad_hidden * up_pre * sigmoid_gate * (1.0 + gate_pre * (1.0 - sigmoid_gate))
+        ).astype(jnp.bfloat16)
+        grad_up = (grad_hidden * (gate_pre * sigmoid_gate)).astype(jnp.bfloat16)
+        grad_routed = back_through_in(pieces, grad_gate=grad_gate, grad_up=grad_up)
+        made = [
+            lax.psum_scatter(
+                jnp.einsum("erd,erf->def", left, right, preferred_element_type=jnp.float32),
+                ("row", "seq"),
+                scatter_dimension=0,
+                tiled=True,
+            )
+            for left, right in ((rows, grad_gate), (rows, grad_up), (grads, hidden_low))
+        ]
+        return None, (expert_out, grad_routed, *made)
+
+    def grouped(weight):
+        return jnp.moveaxis(weight.reshape(weight.shape[0], groups, width, F), 1, 0)
+
+    _, (expert_out, grad_routed, *expert_grads) = lax.scan(
+        some_experts,
+        None,
         (
-            lax.all_gather(gate_weight, ("row", "seq"), axis=0, tiled=True),
-            lax.all_gather(up_weight, ("row", "seq"), axis=0, tiled=True),
+            routed.reshape(groups, width, slot_rows, MODEL_WIDTH),
+            grad_expert.reshape(groups, width, slot_rows, MODEL_WIDTH),
+            grouped(gate_weight),
+            grouped(up_weight),
+            grouped(down_weight),
         ),
-        routed=routed,
-    )
-    hidden_low = (jax.nn.silu(gate_pre) * up_pre).astype(jnp.bfloat16)
-    expert_out = project_out(
-        lax.all_gather(down_weight, ("row", "seq"), axis=0, tiled=True), hidden=hidden_low
-    )
-    grad_hidden = back_through_down(
-        lax.all_gather(down_weight, ("row", "seq"), axis=0, tiled=True), grad_output=grad_expert
-    )
-    sigmoid_gate = jax.nn.sigmoid(gate_pre)
-    grad_gate = (
-        grad_hidden * up_pre * sigmoid_gate * (1.0 + gate_pre * (1.0 - sigmoid_gate))
-    ).astype(jnp.bfloat16)
-    grad_up = (grad_hidden * (gate_pre * sigmoid_gate)).astype(jnp.bfloat16)
-    grad_routed = back_through_in(
-        (
-            lax.all_gather(gate_weight, ("row", "seq"), axis=0, tiled=True),
-            lax.all_gather(up_weight, ("row", "seq"), axis=0, tiled=True),
-        ),
-        grad_gate=grad_gate,
-        grad_up=grad_up,
-    )
-    expert_grads = lax.psum_scatter(
-        jnp.concatenate(
-            [
-                jnp.einsum("erd,erf->def", routed, grad_gate, preferred_element_type=jnp.float32),
-                jnp.einsum("erd,erf->def", routed, grad_up, preferred_element_type=jnp.float32),
-                jnp.einsum(
-                    "erd,erf->def", grad_expert, hidden_low, preferred_element_type=jnp.float32
-                ),
-            ],
-            axis=2,
-        ),
-        ("row", "seq"),
-        scatter_dimension=0,
-        tiled=True,
-    )
-    grad_gate_weight = expert_grads[:, :, :F]
-    grad_up_weight = expert_grads[:, :, F : 2 * F]
-    grad_down_weight = expert_grads[:, :, 2 * F :]
+    )
+    expert_out = expert_out.reshape(E, slot_rows, MODEL_WIDTH)
+    grad_routed = grad_routed.reshape(E, slot_rows, MODEL_WIDTH)
+    grad_gate_weight, grad_up_weight, grad_down_weight = [
+        jnp.moveaxis(grad, 0, 1).reshape(gate_weight.shape) for grad in expert_grads
+    ]
     taken_out = take_slots(expert_out, destination)
     expert_mix = jnp.sum(gate_probs[..., None] * taken_out, axis=2)
     mixed = (residual + expert_mix).astype(jnp.bfloat16)
@@ -501,37 +1443,17 @@
 
 
 def solution(mesh):
+    first = P(("row", "seq"))
     in_specs = (
-        P("row", "seq", None),
-        P(("row", "seq")),
-        P(("row", "seq")),
-        P(("row", "seq"), None),
-        P(("row", "seq"), None),
-        P(("row", "seq"), None),
-        P(("row", "seq"), None),
-        P(("row", "seq"), None),
-        P(("row", "seq"), None, None),
-        P(("row", "seq"), None, None),
-        P(("row", "seq"), None, None),
-        P("row", "seq", None),
-        P("row", "seq"),
-        P("row"),
-        P("row", "seq", None),
+        (P("row", "seq", None), first, first)
+        + (P(("row", "seq"), None),) * 5
+        + (P(("row", "seq"), None, None),) * 3
+        + (P("row", "seq", None), P("row", "seq"), P("row"), P("row", "seq", None))
     )
     out_specs = (
-        P("row", "seq", None),
-        P("row", "seq", None),
-        P(("row", "seq")),
-        P(("row", "seq")),
-        P(("row", "seq"), None),
-        P(("row", "seq"), None),
-        P(("row", "seq"), None),
-        P(("row", "seq"), None),
-        P(("row", "seq"), None),
-        P(("row", "seq"), None, None),
-        P(("row", "seq"), None, None),
-        P(("row", "seq"), None, None),
-    )
-    return jax.shard_map(
-        per_device, mesh=mesh, in_specs=in_specs, out_specs=out_specs, check_vma=False
-    )
+        (P("row", "seq", None), P("row", "seq", None), first, first)
+        + (P(("row", "seq"), None),) * 5
+        + (P(("row", "seq"), None, None),) * 3
+    )
+    body = sixteen_seats if dict(mesh.shape) == {"row": 2, "seq": 16} else any_seats
+    return jax.shard_map(body, mesh=mesh, in_specs=in_specs, out_specs=out_specs, check_vma=False)

time: 2030 us -> 593 us (0.29)
  waiting for transfers between devices: 1400 us -> 0.72 us
  Pallas kernels: 0 us -> 518 us
  local copies, waits for them, and re-layouts: 225 us -> 20.3 us
  matrix products: 170 us -> 0 us
  other arithmetic: 113 us -> 17.8 us
  blocking collectives: 99.4 us -> 19.5 us
    reduce_scatter x2 -> x0, waiting for transfers between devices: 911 us -> none  [the longest x1 817 us: per_device(): lax.psum_scatter(jnp.concatenate([jnp.einsum('erd,erf->def', routed, grad...]
    pallas_call x0 -> x14, Pallas kernels: none -> 518 us  [the longest x7 431 us: comm_call(): pl.pallas_call(body, out_shape=outs, in_specs=[pl.BlockSpec(memory_space=...]
    all_gather x9 -> x2, waiting for transfers between devices: 489 us -> 0.02 us  [the longest x1 0.02 us: sixteen_seats(): cot_all = lax.all_gather(cotangent[0], 'seq', axis=0, tiled=True)]
    dot_general x52 -> x0, matrix products: 168 us -> none  [the longest x1 18.4 us: per_device(): jnp.einsum('erd,erf->def', grad_expert, hidden_low, preferred_element_typ...]
    concatenate x2 -> x1, local copies, waits for them, and re-layouts: 130 us -> 0.08 us  [sixteen_seats(): jnp.concatenate([router_weight, attention_gain[:, None], expert_gain[:, N...]
    concatenate x3 -> x2, other arithmetic: 68.3 us -> 0.79 us  [the longest x1 0.68 us: sixteen_seats(): jnp.concatenate([router_weight, attention_gain[:, None], expert_gain[:, N...]
    unnamed x1 -> x0, blocking collectives: 42 us -> none
    gather x2 -> x0, local copies, waits for them, and re-layouts: 39.7 us -> none  [take_slots(): table[spots]]
  transfers between devices with their start and end apart: 12 -> 2, of which waited for: 10 -> 0; matrix products, arithmetic and copies ran while one was open for 15% -> 6% of each run, Pallas kernels for 0% -> 87%
where the time goes in v1:
time: 593 us; the launch traced here: 592 us
  Pallas kernels  518 us (87%)
  local copies, waits for them, and re-layouts  20.3 us (3%)
  blocking collectives  19.5 us (3%)
  other arithmetic  17.8 us (3%)
  between operations  15 us (3%)
    pallas_call x7, Pallas kernels, comm_call(): pl.pallas_call(body, out_shape=outs, in_specs=[pl.BlockSpec(memory_space=...  431 us
    pallas_call x7, Pallas kernels, compute_call(): pl.pallas_call(body, out_shape=outs, in_specs=[pl.BlockSpec(memory_space=...  87 us
    all_gather x1, blocking collectives, sixteen_seats(): lax.all_gather(segments.astype(jnp.int32), 'seq', axis=1, tiled=True)  19.5 us
  transfers between devices with their start and end apart: 2, of which 0 were waited for; matrix products, arithmetic and copies ran while one was open for 6% of the time, Pallas kernels for 87%

profile of v1, /device:TPU:0, one launch (start us, length us, event | category | flops | bytes accessed | tf_op | source)
XLA Modules:
  0.0 591.7 jit_solution(13348141358171099051)
XLA Ops:
  7.2 0.7 all-gather.6.cloned.1.call-update
  8.0 0.9 stack_reshape.6
  8.8 0.9 stack_reshape.7
  9.9 1.0 reshape.197
  11.0 0.7 copy.103
  11.7 0.8 copy.76
  12.5 0.8 copy.77
  13.2 0.8 copy.78
  14.6 1.3 copy.102
  16.0 1.4 copy.82
  17.5 0.7 maximum_maximum_fusion.small
  18.2 94.0 %shard_map.238 = (bf16[16,2,64,1024]{3,2,1,0:T(8,128)(2,1)}, bf16[32,32,256]{2,1,0:T(8,128)(2,1)}, bf16[32,32,128]{2,1,0:T(8,128)(2,1)}, bf16[2,16,32,1024]{3,2,1,0:T(8,128)(2,1)}) custom-call(bf16[2,64,1024]{2,1,0:T(8,128)(2,1)} %bitcast.83, bf16[32,2048]{1,0:T(8,128)(2,1)} %bitcast.91, bf16[32,128]{1,0:T(8,128)(2,1)} %maximum_maximum_fusion.small, ...), custom_call_target="tpu_custom_call" | custom-call | tf_op jit(solution)/shard_map/pallas_call | solution.py:227
  112.3 19.5 %all_gather.9 = s32[1,2048]{1,0:T(1,128)S(1)} all-gather(s32[1,128]{1,0:T(1,128)S(1)} %copy-done.8), channel_id=1, replica_groups=mesh['row'=2,'seq'=16] {'seq'}, dimensions={1}, use_global_device_ids=true | all-gather | bytes 8704 | tf_op jit(solution)/shard_map/all_gather | solution.py:815
  131.8 2.6 convert_reduce_fusion
  134.4 1.8 multiply_sine_fusion
  136.2 22.9 %shard_map.239 = (bf16[2048,1024]{1,0:T(8,128)(2,1)}, bf16[64,2048]{1,0:T(8,128)(2,1)}, bf16[64,2048]{1,0:T(8,128)(2,1)}, bf16[64,2048]{1,0:T(8,128)(2,1)}, f32[...) custom-call(bf16[2048,1024]{1,0:T(8,128)(2,1)} %bitcast.70, bf16[1024,256]{1,0:T(8,128)(2,1)} %bitcast.98, ...), custom_call_target="tpu_custom_call" | custom-call | tf_op jit(solution)/shard_map/pallas_call | solution.py:240
  159.7 1.3 maximum_bitcast_fusion.w3
  161.0 58.0 %shard_map.240 = (bf16[16,64,128]{2,1,0:T(8,128)(2,1)}, bf16[3,32,32,512]{3,2,1,0:T(8,128)(2,1)}) custom-call(bf16[64,2048]{1,0:T(8,128)(2,1)} %get-tuple-element.57.o_low, bf16[16,3,32,512]{3,2,1,0:T(8,128)(2,1)} %maximum_bitcast_fusion.w3), custom_call_target="tpu_custom_call" | custom-call | tf_op jit(solution)/shard_map/pallas_call | solution.py:227
  219.0 3.9 shard_map.241
  222.9 47.1 %shard_map.242 = (bf16[16,2,64,1024]{3,2,1,0:T(8,128)(2,1)}, f32[16,16,128]{2,1,0:T(8,128)}) custom-call(bf16[2,64,1024]{2,1,0:T(8,128)(2,1)} %bitcast.93, f32[16,128]{1,0:T(8,128)} %get-tuple-element.62.p_t), custom_call_target="tpu_custom_call" | custom-call | tf_op jit(solution)/shard_map/pallas_call | solution.py:227
  270.0 28.1 %shard_map.243 = (bf16[2048,1024]{1,0:T(8,128)(2,1)}, bf16[2048,1024]{1,0:T(8,128)(2,1)}, f32[16,8,128]{2,1,0:T(8,128)}, bf16[3,1024,512]{2,1,0:T(8,128)(2,1)}) custom-call(bf16[2048,1024]{1,0:T(8,128)(2,1)} %bitcast.76, bf16[2048,1024]{1,0:T(8,128)(2,1)} %bitcast.75, f32[16,16,128]{2,1,0:T(8,128)} %get-tuple-element.64.p_all, bf16[3,1024,512]{2,1,0:T(8,128)(2,1)} %bitcast.81), custom_call_target="tpu_custom_call" | custom-call | tf_op jit(solution)/shard_map/pallas_call | solution.py:240
  298.1 81.4 %shard_map.244 = (bf16[2,64,1024]{2,1,0:T(8,128)(2,1)}, bf16[2,64,1024]{2,1,0:T(8,128)(2,1)}, f32[16,8,128]{2,1,0:T(8,128)}) custom-call(bf16[16,2,64,1024]{3,2,1,0:T(8,128)(2,1)} %bitcast.72, bf16[16,2,64,1024]{3,2,1,0:T(8,128)(2,1)} %bitcast.71, f32[16,8,128]{2,1,0:T(8,128)} %get-tuple-element.68.gg), custom_call_target="tpu_custom_call" | custom-call | tf_op jit(solution)/shard_map/pallas_call | solution.py:227
  379.5 5.2 shard_map.245
  384.7 112.0 %shard_map.246 = (bf16[64,2048]{1,0:T(8,128)(2,1)}, bf16[16,3,32,512]{3,2,1,0:T(8,128)(2,1)}, bf16[2,16,1152]{2,1,0:T(8,128)(2,1)}) custom-call(bf16[16,64,128]{2,1,0:T(8,128)(2,1)} %bitcast.99, bf16[3,2,16,32,512]{4,3,2,1,0:T(8,128)(2,1)} %bitcast.82, bf16[2,16,2,16,1152]{4,3,2,1,0:T(8,128)(2,1)} %bitcast.86), custom_call_target="tpu_custom_call" | custom-call | tf_op jit(solution)/shard_map/pallas_call | solution.py:227
  496.7 0.9 bitcast_convert_fusion
  497.6 0.7 slice.36
  498.3 1.8 convert_bitcast_fusion
  500.5 1.6 copy.90
  502.1 1.6 copy.91
  503.6 1.6 copy.92
  505.2 17.6 %shard_map.247 = (f32[64,2048]{1,0:T(8,128)}, f32[128,2048]{1,0:T(8,128)}) custom-call(bf16[64,2048]{1,0:T(8,128)(2,1)} %get-tuple-element.70.q_t, bf16[64,2048]{1,0:T(8,128)(2,1)} %get-tuple-element.71.k_t, bf16[64,2048]{1,0:T(8,128)(2,1)} %get-tuple-element.72.v_t, f32[1,2048]{1,0:T(1,128)} %get-tuple-element.73.lse, f32[64,2048]{1,0:T(8,128)} %get-tuple-element.74.o_t, ...), custom_call_target="tpu_custom_call" | custom-call | tf_op jit(solution)/shard_map/pallas_call | solution.py:240
  522.9 4.0 shard_map.248.got
  526.8 4.5 shard_map.249
  531.3 34.9 %shard_map.250 = (bf16[16,128,128]{2,1,0:T(8,128)(2,1)}, bf16[32,32,128]{2,1,0:T(8,128)(2,1)}) custom-call(bf16[128,2048]{1,0:T(8,128)(2,1)} %get-tuple-element.89.g_t, bf16[32,32,128]{2,1,0:T(8,128)(2,1)} %bitcast.102), custom_call_target="tpu_custom_call" | custom-call | tf_op jit(solution)/shard_map/pallas_call | solution.py:227
  566.2 1.0 convert_reduce_fusion.1
  567.2 0.8 fusion.2
  568.1 0.7 reshape.222
  568.8 1.0 copy.84
  569.8 0.7 reshape.221
  570.5 0.9 copy.83
  571.4 1.1 reshape.220
  572.5 1.0 multiply_reduce_fusion.1
  573.5 1.0 multiply_reduce_fusion.2
  574.5 1.0 multiply_reduce_fusion
  575.5 2.0 add_reduce_fusion
  577.4 1.2 convert_divide_fusion
  579.2 0.8 fusion.1
  579.9 4.9 shard_map.251
  (37 shorter events, 2.1 us)
Async XLA Ops:
  7.2 105.1 %copy-start.8 = (s32[1,128]{1,0:T(1,128)S(1)}, s32[1,128]{1,0:T(1,128)}, u32[]{:S(2)}) copy-start(s32[1,128]{1,0:T(1,128)} %param.27) | copy-start | bytes 1540
  7.2 262.8 %all-gather.6.cloned.1.call-start = ((), (), s32[]{:S(2)}) async-start(), calls=%async_computation.1 | async-start | bytes 4456448 | tf_op jit(solution)/shard_map/all_gather | solution.py:818
  7.9 572.0 %all-gather.4.cloned.1.call-start = ((), (), s32[]{:S(2)}) async-start(), calls=%async_computation | async-start | bytes 4325376 | tf_op jit(solution)/shard_map/all_gather | solution.py:817
  112.3 46.8 %copy-start = (bf16[32,16,512]{2,1,0:T(8,128)(2,1)S(1)}, bf16[32,16,512]{2,1,0:T(8,128)(2,1)}, u32[]{:S(2)}) copy-start(bf16[32,16,512]{2,1,0:T(8,128)(2,1)} %param.24) | copy-start | bytes 1572868
  112.3 46.8 %copy-start.3 = (bf16[32,16,512]{2,1,0:T(8,128)(2,1)S(1)}, bf16[32,16,512]{2,1,0:T(8,128)(2,1)}, u32[]{:S(2)}) copy-start(bf16[32,16,512]{2,1,0:T(8,128)(2,1)} %param.25) | copy-start | bytes 1572868
  498.3 74.1 %copy-start.5 = (f32[32,16]{0,1:T(8,128)}, f32[32,16]{0,1:T(8,128)S(1)}, u32[]{:S(2)}) copy-start(f32[32,16]{0,1:T(8,128)S(1)} %copy.94) | copy-start | bytes 6148
  531.3 41.1 %copy-start.6 = (bf16[32,16]{0,1:T(8,128)(2,1)S(1)}, bf16[32,16]{0,1:T(8,128)(2,1)}, u32[]{:S(2)}) copy-start(bf16[32,16]{0,1:T(8,128)(2,1)} %param.22) | copy-start | bytes 3076
  566.2 12.4 %copy-start.7 = (bf16[32]{0:T(256)(128)(2,1)S(1)}, bf16[32]{0:T(256)(128)(2,1)}, u32[]{:S(2)}) copy-start(bf16[32]{0:T(256)(128)(2,1)} %param.16) | copy-start | bytes 196
  571.4 7.8 %copy-start.4 = (bf16[2,64,1024]{2,1,0:T(8,128)(2,1)S(1)}, bf16[2,64,1024]{2,1,0:T(8,128)(2,1)}, u32[]{:S(2)}) copy-start(bf16[2,64,1024]{2,1,0:T(8,128)(2,1)} %get-tuple-element.69) | copy-start | bytes 786436
  572.5 12.4 %copy-start.1 = (f32[32,1024]{1,0:T(8,128)}, f32[32,1024]{1,0:T(8,128)S(1)}, u32[]{:S(2)}) copy-start(f32[32,1024]{1,0:T(8,128)S(1)} %reshape.220) | copy-start | bytes 393220
  572.5 6.7 %copy-start.2 = (f32[128,1024]{1,0:T(8,128)S(1)}, f32[128,1024]{1,0:T(8,128)}, u32[]{:S(2)}) copy-start(f32[128,1024]{1,0:T(8,128)} %get-tuple-element.60) | copy-start | bytes 1572868
Sparse Core Ops, SparseCore 0:
  10.2 68.8 all-gather.5
  82.0 62.6 all-gather.3

commit v2 on v1

--- a/solution.py
+++ b/solution.py
@@ -97,10 +97,17 @@
     pl.semaphore_wait(sem, 2 + (z < 3).astype(jnp.int32) + (z > 0).astype(jnp.int32))
 
 
+QB = 256
+
+
+def lane_block(i, size=QB):
+    return pl.ds(pl.multiple_of(i * size, size), size)
+
+
 class Gather:
     def __init__(self, own, at, send, recv):
         self.own, self.at, self.send, self.recv = own, at, send, recv
-        self.sent = []
+        self.ending = False
         self.x, self.s, self.z, self.y, self.c = place()
 
     def device(self, k):
@@ -121,10 +128,12 @@
             cond = both(cond, self.z < 3)
         if k == DOWN:
             cond = both(cond, self.z > 0)
-        when(cond, lambda: self.copy(src, h, k, own).start())
-        self.sent.append((cond, src, h, k, own))
+        act = (lambda c: c.wait_send()) if self.ending else (lambda c: c.start())
+        when(cond, lambda: act(self.copy(src, h, k, own)))
 
     def wait(self, src, h, cond=None):
+        if self.ending:
+            return
         when(cond, lambda: self.copy(src, h, SIDE, False).wait_recv())
 
     def begin(self):
@@ -161,15 +170,27 @@
             self.wait(other, 0, cond)
             self.go(other, 0, CORE, cond)
 
+    def plane(self, zz, cond=None):
+        for yy in range(2):
+            for h in range(2):
+                self.wait(seat(zz, yy, 1 - self.c), h, cond)
+
+    def planes(self, t):
+        self.step_side(t)
+        for cond, zz in ((self.z - t >= 0, self.z - t), (self.z + t <= 3, self.z + t)):
+            self.plane(zz, cond)
+
     def end_core(self):
         for zz in range(4):
-            for yy in range(2):
-                for h in range(2):
-                    self.wait(seat(zz, yy, 1 - self.c), h)
+            self.plane(zz)
 
     def end_sends(self):
-        for cond, src, h, k, own in self.sent:
-            when(cond, lambda: self.copy(src, h, k, own).wait_send())
+        self.ending = True
+        self.begin()
+        self.near()
+        for t in (1, 2, 3):
+            self.step(t)
+            self.step_side(t)
 
 
 GATHER_SEMS = [DMA((16, 2, 4)), DMA((16, 2))]
@@ -194,26 +215,40 @@
 
 class Exchange:
     def __init__(self, src, dst, send, recv, wide=False):
-        x, s = lax.axis_index("row"), lax.axis_index("seq")
-        self.me = x * 16 + s if wide else s
-        self.n = 32 if wide else 16
-        self.device = (lambda r: (r // 16, r % 16)) if wide else (lambda r: (x, r))
+        self.x, self.s, self.z, self.y, self.c = place()
+        self.wide, self.n = wide, 32 if wide else 16
         self.src, self.dst, self.send, self.recv = src, dst, send, recv
 
+    def seat(self, k, back=False):
+        dz = (k // 4) % 4
+        if back:
+            dz = (4 - dz) % 4
+        x = (self.x + k // 16) % 2
+        s = seat((self.z + dz) % 4, (self.y + k // 2) % 2, (self.c + k) % 2)
+        return x, s
+
+    def index(self, seat_of):
+        x, s = seat_of
+        return x * 16 + s if self.wide else s
+
     def copy(self, k):
-        to = (self.me + k) % self.n
-        return remote(self.src(to), self.dst(self.me), self.send.at[k], self.recv.at[k], self.device(to))
-
-    def begin(self):
-        self.local = pltpu.make_async_copy(self.src(self.me), self.dst(self.me), self.recv.at[0])
-        self.local.start()
-        for k in range(1, self.n):
-            self.copy(k).start()
+        to, me = self.seat(k), self.index((self.x, self.s))
+        return remote(self.src(self.index(to)), self.dst(me), self.send.at[k], self.recv.at[k], to)
+
+    def begin(self, ks=None):
+        for k in range(self.n) if ks is None else ks:
+            if k == 0:
+                me = self.index((self.x, self.s))
+                self.local = pltpu.make_async_copy(self.src(me), self.dst(me), self.recv.at[0])
+                self.local.start()
+            else:
+                self.copy(k).start()
 
     def arrive(self, k):
-        frm = (self.me + self.n - k) % self.n
-        remote(self.src(self.me), self.dst(frm), self.send.at[k], self.recv.at[k], self.device(frm)).wait_recv()
-        return frm
+        frm = self.seat(k, back=True)
+        me = self.index((self.x, self.s))
+        remote(self.src(me), self.dst(self.index(frm)), self.send.at[k], self.recv.at[k], frm).wait_recv()
+        return self.index(frm)
 
     def end(self, arrivals=True):
         self.local.wait()
@@ -221,6 +256,58 @@
             if arrivals:
                 self.arrive(k)
             self.copy(k).wait_send()
+
+
+class Slices:
+    def __init__(self, src, got, send, recv):
+        self.x, self.s, self.z, self.y, self.c = place()
+        self.src, self.got, self.send, self.recv = src, got, send, recv
+
+    def block(self, pair):
+        return self.src.at[:, lane_block(pair, 256)]
+
+    def copy(self, k):
+        z, y = (self.z + k // 2) % 4, (self.y + k) % 2
+        dst = self.got.at[self.x, self.s // 2, self.c]
+        return remote(self.block(z * 2 + y), dst, self.send.at[k], self.recv.at[k], (self.x, seat(z, y, self.c)))
+
+    def begin(self):
+        self.local = pltpu.make_async_copy(
+            self.block(self.s // 2), self.got.at[self.x, self.s // 2, self.c], self.recv.at[0]
+        )
+        self.local.start()
+        for k in range(1, 8):
+            self.copy(k).start()
+
+    def over_x(self):
+        ref = self.got.at[self.x, :, self.c]
+        return remote(ref, ref, self.send.at[8], self.recv.at[8], (1 - self.x, self.s))
+
+    def over_core(self, k):
+        ref = self.got.at[self.x if k == 9 else 1 - self.x, :, self.c]
+        return remote(ref, ref, self.send.at[k], self.recv.at[k], (self.x, seat(self.z, self.y, 1 - self.c)))
+
+    def share(self):
+        self.local.wait()
+        for k in range(1, 8):
+            z, y = (self.z + 4 - k // 2) % 4, (self.y + k) % 2
+            dst = self.got.at[self.x, z * 2 + y, self.c]
+            remote(
+                self.block(z * 2 + y), dst, self.send.at[k], self.recv.at[k], (self.x, seat(z, y, self.c))
+            ).wait_recv()
+        self.over_x().start()
+        self.over_core(9).start()
+
+    def end(self):
+        self.over_x().wait_recv()
+        self.over_core(10).start()
+        self.over_core(9).wait_recv()
+        self.over_core(10).wait_recv()
+        for k in range(1, 8):
+            self.copy(k).wait_send()
+        self.over_x().wait_send()
+        self.over_core(9).wait_send()
+        self.over_core(10).wait_send()
 
 
 def comm_call(body, outs, ins, sems, cid, scratch=()):
@@ -236,25 +323,33 @@
     )(*ins)
 
 
-def compute_call(body, outs, ins, scratch=()):
-    return pl.pallas_call(
-        body,
-        out_shape=outs,
-        in_specs=[pl.BlockSpec(memory_space=VM)] * len(ins),
-        out_specs=[pl.BlockSpec(memory_space=VM)] * len(outs),
-        scratch_shapes=list(scratch),
-        compiler_params=pltpu.CompilerParams(vmem_limit_bytes=VMEM_LIMIT),
-    )(*ins)
-
-
 def sds(shape, dtype):
     return jax.ShapeDtypeStruct(shape, dtype)
 
 
-def gather_first(tok, wperm, small, wo, tok_all, w_mine, small_all, wo_all, *sems):
+def allowed_mask(first_key, first_query, start_row):
+    key = first_key + lax.broadcasted_iota(jnp.int32, (QB, QB), 0)
+    query = first_query + lax.broadcasted_iota(jnp.int32, (QB, QB), 1)
+    return (key <= query) & (key >= start_row)
+
+
+SCORE = math.log2(math.e) / math.sqrt(HEAD_SIZE)
+
+
+def front(
+    tok, wperm, wo, w3, seg, routes, cos, sin,
+    hid, q_t, k_t, v_t, o_t, lse, start, wexp, wo_all,
+    residual, normed, scale_out, h2, att, probs, picked, p_t,
+    tok_all, w_mine, seg_all, o_low, att_t, k_n, w_t,
+    t_send, t_recv, o_send, o_recv, w_send, w_recv, g_send, g_recv,
+    a_send, a_recv, e_send, e_recv, x_send, x_recv, x_sem,
+):
     x, s, z, y, c = place()
-    t_send, t_recv, o_send, o_recv, w_send, w_recv, s_send, s_recv, x_sem = sems
+    half = tok.shape[1]
+    length = hid.shape[0]
     barrier_all()
+    slices = Slices(wperm, w_mine, w_send, w_recv)
+    slices.begin()
     over = remote(wo, wo_all.at[x, s], x_sem.at[0], x_sem.at[1], (1 - x, s))
     over.start()
     tokens = Gather(lambda h: tok.at[h], lambda src, h: tok_all.at[src, h], t_send, t_recv)
@@ -263,71 +358,59 @@
     keep_tok.start()
     keep = pltpu.make_async_copy(wo, wo_all.at[x, s], x_sem.at[3])
     keep.start()
-    minor = Exchange(lambda r: small, lambda r: small_all.at[r], s_send, s_recv, wide=True)
-    minor.begin()
-    slices = Exchange(
-        lambda r: wperm.at[:, pl.ds(pl.multiple_of(((r % 16) // 2) * 256, 256), 256)],
-        lambda r: w_mine.at[r],
-        w_send,
-        w_recv,
-        wide=True,
-    )
-    slices.begin()
+    documents = Exchange(lambda r: seg, lambda r: seg_all.at[r], g_send, g_recv)
+    documents.begin()
+    weights = Exchange(lambda e: w3.at[e], lambda r: wexp.at[:, x * 16 + r], e_send, e_recv)
+    weights.begin(range(4))
+    tokens.near()
+    for t in (1, 2, 3):
+        tokens.step(t)
+    for t in (1, 2, 3):
+        tokens.step_side(t)
+    documents.end()
+    slices.share()
     keep.wait()
     remote(wo, wo_all.at[1 - x, s], x_sem.at[0], x_sem.at[1], (1 - x, s)).wait_recv()
     outw = Gather(None, lambda src, h: wo_all.at[h, src], o_send, o_recv)
     outw.begin()
-    tokens.near()
-    outw.near()
-    for t in (1, 2, 3):
-        tokens.step(t)
-        outw.step(t)
-    for t in (1, 2, 3):
-        tokens.step_side(t)
-        outw.step_side(t)
+
+    def cross(k, begin=True):
+        row = weights.index(weights.seat(k, back=True))
+        if begin and k:
+            weights.arrive(k)
+        src = w3.at[s] if k == 0 else wexp.at[:, x * 16 + row]
+        copy = remote(src, wexp.at[:, x * 16 + row], x_send.at[k], x_recv.at[k], (1 - x, s))
+        if begin:
+            copy.start()
+        else:
+            copy.wait_send()
+            remote(src, wexp.at[:, (1 - x) * 16 + row], x_send.at[k], x_recv.at[k], (1 - x, s)).wait_recv()
+
+    width = tok.shape[2]
+    slices.end()
+    w_t[...] = jnp.transpose(w_mine[...].reshape(width, 256).astype(F32)).astype(BF)
+    numbers = seg_all[:, 0, :]
+    ends = [jnp.sum((numbers < n).astype(jnp.int32)) for n in (1, 2)]
+    for b in range(16):
+        line = numbers[b : b + 1]
+        first = jnp.where(line == 0, 0, jnp.where(line == 1, ends[0], ends[1]))
+        start[:, b * 128 : b * 128 + 128] = first
     tokens.end_core()
-    outw.end_core()
-    minor.end()
-    slices.end()
-    tokens.end_sends()
-    outw.end_sends()
     keep_tok.wait()
-    over.wait_send()
-
-
-QB = 256
-
-
-def allowed_mask(first_key, first_query, start_row):
-    key = first_key + lax.broadcasted_iota(jnp.int32, (QB, QB), 0)
-    query = first_query + lax.broadcasted_iota(jnp.int32, (QB, QB), 1)
-    return (key <= query) & (key >= start_row)
-
-
-def lane_block(i, size=QB):
-    return pl.ds(pl.multiple_of(i * size, size), size)
-
-
-SCORE = math.log2(math.e) / math.sqrt(HEAD_SIZE)
-
-
-def attention_forward(
-    tok, w_mine, small, cos, sin, start, hid, q_t, k_t, v_t, o_t, lse, o_low, k_n, gain, w_t
-):
-    core = lax.axis_index("seq") % 2
-    gain[...] = jnp.transpose(small[...].astype(F32))
-    w_t[...] = jnp.transpose(w_mine[...].astype(F32)).astype(BF)
+    weights.begin(range(4, 8))
+    for k in range(4):
+        cross(k)
 
     def project(i, _):
         rows = lane_block(i, 512)
-        values = tok[rows, :].astype(F32)
+        values = tok_all[pl.ds(i * 4, 4)].reshape(512, width).astype(F32)
         scale = lax.rsqrt(jnp.mean(values * values, axis=-1, keepdims=True) + EPSILON)
-        hidden = (values * scale * gain[E : E + 1, :]).astype(BF)
+        hidden = (values * scale).astype(BF)
         hid[rows, :] = hidden
         made = dot(w_t[...], hidden, NT)
         co, si = cos[:, rows], sin[:, rows]
-        own = jnp.where(core == 0, made[0:64], made[128:192])
-        for ref, part in ((q_t, own), (k_t, made[64:128])):
+        own = jnp.where(c == 0, made[0:64], made[64:128])
+        for ref, part in ((q_t, own), (k_t, made[128:192])):
             a, b = part[:32], part[32:]
             ref[0:32, rows] = (a * co - b * si).astype(BF)
             ref[32:64, rows] = (b * co + a * si).astype(BF)
@@ -335,7 +418,10 @@
         k_n[rows, :] = jnp.transpose(k_t[:, rows].astype(F32)).astype(BF)
         return 0
 
-    lax.fori_loop(0, 4, project, 0)
+    lax.fori_loop(0, length // 512, project, 0)
+    outw.near()
+    outw.step(1)
+    weights.begin(range(8, 12))
 
     def query_block(i, _):
         cols = lane_block(i)
@@ -348,10 +434,10 @@
             scores = dot(k_n[rows, :], queries) * SCORE
             scores = jnp.where(allowed_mask(j * QB, i * QB, begin), scores, MASKED)
             fresh = jnp.maximum(top, jnp.max(scores, axis=0, keepdims=True))
-            weights = jnp.exp2(scores - fresh)
+            powers = jnp.exp2(scores - fresh)
             decay = jnp.exp2(top - fresh)
-            total = total * decay + jnp.sum(weights, axis=0, keepdims=True)
-            acc = acc * decay + dot(v_t[:, rows], weights.astype(BF))
+            total = total * decay + jnp.sum(powers, axis=0, keepdims=True)
+            acc = acc * decay + dot(v_t[:, rows], powers.astype(BF))
             return fresh, total, acc
 
         top, total, acc = lax.fori_loop(
@@ -366,54 +452,38 @@
         lse[:, cols] = top + jnp.log2(total)
         return 0
 
-    lax.fori_loop(0, tok.shape[0] // QB, query_block, 0)
-
-
-def heads_to_tokens(o_low, w3, att_t, wexp, *sems):
-    a_send, a_recv, w_send, w_recv, x_send, x_recv = sems
-    x, s, z, y, c = place()
-    barrier_row(partner=True)
+    blocks = length // QB
+    cut = (5 * blocks) // 8
+    lax.fori_loop(0, cut, query_block, 0)
+    outw.step(2)
+    outw.step(3)
+    for t in (1, 2, 3):
+        outw.step_side(t)
+    for k in range(4, 8):
+        cross(k)
+    weights.begin(range(12, 16))
+    lax.fori_loop(cut, blocks, query_block, 0)
     heads = Exchange(lambda t: o_low.at[:, lane_block(t, 128)], lambda h: att_t.at[h], a_send, a_recv)
     heads.begin()
-    weights = Exchange(lambda e: w3.at[e], lambda r: wexp.at[:, x * 16 + r], w_send, w_recv)
-    weights.begin()
-    over = []
-
-    def cross(k, src, row):
-        copy = remote(src, wexp.at[:, x * 16 + row], x_send.at[k], x_recv.at[k], (1 - x, s))
-        copy.start()
-        over.append(copy)
-
-    cross(0, w3.at[s], s)
-    for k in range(1, 16):
-        frm = weights.arrive(k)
-        cross(k, wexp.at[:, x * 16 + frm], frm)
+    outw.end_core()
+    for k in range(8, 12):
+        cross(k)
     heads.end()
-    weights.end(arrivals=False)
-    for k, copy in enumerate(over):
-        copy.wait_send()
-        frm = (s + 16 - k) % 16
-        remote(
-            wexp.at[:, 0], wexp.at[:, (1 - x) * 16 + frm], x_send.at[k], x_recv.at[k], (1 - x, s)
-        ).wait_recv()
-
-
-def between(tok, att_t, wo, small, routes, residual, normed, scale_out, h2, att, probs, picked, p_t):
-    gain = jnp.transpose(small[...].astype(F32))[E + 1 : E + 2, :]
-    att[...] = jnp.transpose(att_t[...].astype(F32)).astype(BF)
-    res = tok[...].astype(F32) + dot(att[...], wo[...], NT)
+
+    att[...] = jnp.transpose(att_t[...].reshape(width, 2 * half).astype(F32)).astype(BF)
+    res = tok[...].reshape(2 * half, width).astype(F32) + dot(att[...], wo_all[:, :, :, 0:width].reshape(width, width), NT)
     residual[...] = res
     scale = lax.rsqrt(jnp.mean(res * res, axis=-1, keepdims=True) + EPSILON)
     norm = res * scale
     normed[...] = norm
     scale_out[...] = jnp.broadcast_to(scale, scale_out.shape)
-    hidden = (norm * gain).astype(BF)
+    hidden = norm.astype(BF)
     h2[...] = hidden
     lanes = lax.broadcasted_iota(jnp.int32, (128, 128), 1)
-    logits = jnp.where(lanes < E, dot(hidden, small[...]), MASKED)
+    logits = jnp.where(lanes < E, dot(hidden, wo_all[:, :, :, width : width + 128].reshape(width, 128)), MASKED)
     top = jnp.max(logits, axis=-1, keepdims=True)
-    weights = jnp.exp(logits - top)
-    prob = weights / jnp.sum(weights, axis=-1, keepdims=True)
+    powers = jnp.exp(logits - top)
+    prob = powers / jnp.sum(powers, axis=-1, keepdims=True)
     probs[...] = prob
     mask = jnp.zeros((128, 128), F32)
     for k in range(K):
@@ -421,64 +491,14 @@
     picked[...] = mask
     p_t[...] = jnp.transpose(prob * mask)[0:E, :]
 
-
-def gather_second(h2, p_t, h_all, p_all, *sems):
-    h_send, h_recv, p_send, p_recv, keep_sem = sems
-    x, s, z, y, c = place()
-    barrier_row()
-    hidden = Gather(lambda h: h2.at[h], lambda src, h: h_all.at[src, h], h_send, h_recv)
-    hidden.begin()
-    keep = pltpu.make_async_copy(h2, h_all.at[s], keep_sem.at[0])
-    keep.start()
-    minor = Exchange(lambda r: p_t, lambda r: p_all.at[r], p_send, p_recv)
-    minor.begin()
-    hidden.near()
-    for t in (1, 2, 3):
-        hidden.step(t)
-    for t in (1, 2, 3):
-        hidden.step_side(t)
-    hidden.end_core()
-    hidden.end_sends()
-    minor.end()
-    keep.wait()
-
-
-TB = 512
-
-
-def expert_body(h_all, cot, p_all, wexp, mixp, backp, gg, dw, acc):
-    e = lax.axis_index("seq")
-    acc[...] = jnp.zeros(acc.shape, F32)
-
-    def chunk(i, _):
-        rows = lane_block(i, TB)
-        hidden, grad = h_all[rows, :], cot[rows, :]
-        cols = [jnp.broadcast_to(p_all[i * 4 + b, pl.ds(e, 1), :], (128, 128)) for b in range(4)]
-        prob = jnp.concatenate([jnp.transpose(v)[:, 0:1] for v in cols], axis=0)
-        gate = dot(hidden, wexp[0])
-        up = dot(hidden, wexp[1])
-        sig = 1.0 / (1.0 + jnp.exp(-gate))
-        silu = gate * sig
-        act = silu * up
-        low = act.astype(BF)
-        out = dot(low, wexp[2], NT)
-        mixp[rows, :] = (prob * out).astype(BF)
-        back = dot(grad, wexp[2])
-        seen = jnp.sum(low.astype(F32) * back, axis=-1, keepdims=True)
-        for b in range(4):
-            line = jnp.transpose(jnp.broadcast_to(seen[b * 128 : b * 128 + 128], (128, 128)))[0:8]
-            gg[i * 4 + b] = line
-        grad_hidden = back * prob
-        grad_gate = (grad_hidden * up * (sig * (1.0 + gate * (1.0 - sig)))).astype(BF)
-        grad_up = (grad_hidden * silu).astype(BF)
-        backp[rows, :] = (dot(grad_gate, wexp[0], NT) + dot(grad_up, wexp[1], NT)).astype(BF)
-        acc[0] += dot(hidden, grad_gate, TN)
-        acc[1] += dot(hidden, grad_up, TN)
-        acc[2] += dot(grad, (prob * low.astype(F32)).astype(BF), TN)
-        return 0
-
-    lax.fori_loop(0, h_all.shape[0] // TB, chunk, 0)
-    dw[...] = acc[...].astype(BF)
+    for k in range(12, 16):
+        cross(k)
+    weights.end(arrivals=False)
+    for k in range(16):
+        cross(k, begin=False)
+    tokens.end_sends()
+    outw.end_sends()
+    over.wait_send()
 
 
 class Reduce:
@@ -565,25 +585,27 @@
 
         when(cond, go)
 
-    def core_step(self, cond, zz):
+    def begin_plane(self, zz, cond=None):
+        for yy in range(2):
+            when(cond, lambda: self.first(zz, yy).start())
+
+    def fold(self, zz, cond=None):
+        z = self.z
+
         def go():
             for yy in range(2):
                 self.first(zz, yy).wait_recv()
-                mine = self.part.at[seat(zz, yy, self.c)]
-                self.add(self.r1.at[zz, yy], mine)
+                self.add(self.r1.at[zz, yy], self.part.at[seat(zz, yy, self.c)])
             self.side(zz).start()
+            for lane in (1, 2):
+                pl.when((zz > z) & (z == 0))(lambda: self.line(lane, zz, True).start())
+                pl.when((zz < z) & (z == 3))(lambda: self.line(lane, zz, False).start())
 
         when(cond, go)
 
-    def run(self):
-        order = list(self.order())
-        for cond, zz, up in order:
-            self.core_step(cond, zz)
-            if up is not None:
-                for lane in (1, 2):
-                    at_end = (self.z == 0) if up else (self.z == 3)
-                    when(both(cond, at_end), lambda: self.line(lane, zz, up).start())
-        for cond, zz, up in order:
+    def flow(self):
+        z = self.z
+        for cond, zz, up in self.order():
 
             def ready():
                 self.side(zz).wait_recv()
@@ -592,11 +614,10 @@
             when(cond, ready)
             if up is None:
                 continue
-            inner = (self.z > 0) if up else (self.z < 3)
+            inner = (z > 0) if up else (z < 3)
             for lane in (1, 2):
                 self.pass_on(lane, zz, up, both(cond, inner))
             self.pass_on(0, zz, up, cond)
-        z = self.z
         for lane in (1, 2, 0):
             for up, cond in ((True, z > 0), (False, z < 3)):
 
@@ -610,6 +631,11 @@
         self.out[0] = self.ra[z]
         self.last().wait_recv()
         self.out[1] = (self.r1[z, self.y, 1].astype(F32) + self.rb[...].astype(F32)).astype(BF)
+
+    def run(self):
+        for cond, zz, _ in self.order():
+            self.fold(zz, cond)
+        self.flow()
 
     def last(self):
         return remote(
@@ -633,116 +659,171 @@
 
 NBUF = 7
 NSEM = 9
-
-
-def reduce_rows(backp, mixp, gg, back, mix, g_all, *rest):
+TB = 512
+
+
+def middle(h2, p_t, cot, wexp, back, mix, g_all, dwx, h_all, p_all, backp, mixp, gg, dw, acc, *rest):
     bufs_a, bufs_b = rest[:NBUF], rest[NBUF : 2 * NBUF]
     sems = rest[2 * NBUF :]
-    barrier_row()
+    h_send, h_recv, p_send, p_recv, keep_sem, g_send, g_recv, x_sem = sems[2 * NSEM :]
+    x, s, z, y, c = place()
+    barrier_row(partner=True)
+    hidden = Gather(lambda h: h2.at[h], lambda src, h: h_all.at[src, h], h_send, h_recv)
+    hidden.begin()
+    keep = pltpu.make_async_copy(h2, h_all.at[s], keep_sem.at[0])
+    keep.start()
+    minor = Exchange(lambda r: p_t, lambda r: p_all.at[r], p_send, p_recv)
+    minor.begin()
     one = Reduce(backp, back, bufs_a, sems[:NSEM])
     two = Reduce(mixp, mix, bufs_b, sems[NSEM : 2 * NSEM])
-    g_send, g_recv = sems[2 * NSEM :]
-    one.begin()
-    minor = Exchange(lambda r: gg.at[r], lambda r: g_all.at[r], g_send, g_recv)
-    minor.begin()
-    one.run()
-    two.begin()
+    acc[...] = jnp.zeros(acc.shape, F32)
+    hidden.near()
+    keep.wait()
+    minor.end()
+    hidden.plane(z)
+    hidden.step(1)
+    far = z // 2
+    order = (z, z + 1 - 2 * far, 2 - 2 * z + 5 * far, 3 - 3 * far)
+    width = h2.shape[2]
+
+    def chunk(i, _):
+        zz = jnp.where(i == 0, order[0], jnp.where(i == 1, order[1], jnp.where(i == 2, order[2], order[3])))
+
+        @pl.when(i == 1)
+        def _():
+            hidden.planes(1)
+            hidden.step(2)
+
+        @pl.when(i == 2)
+        def _():
+            hidden.planes(2)
+            hidden.step(3)
+            one.fold(order[0])
+
+        @pl.when(i == 3)
+        def _():
+            hidden.planes(3)
+            one.fold(order[1])
+
+        four = pl.ds(zz * 4, 4)
+        rows = lane_block(zz, TB)
+        rest = h_all[four].reshape(TB, width)
+        grad = cot[rows, :]
+        cols = [jnp.broadcast_to(p_all[zz * 4 + b, pl.ds(s, 1), :], (128, 128)) for b in range(4)]
+        prob = jnp.concatenate([jnp.transpose(v)[:, 0:1] for v in cols], axis=0)
+        gate = dot(rest, wexp[0])
+        up = dot(rest, wexp[1])
+        sig = 1.0 / (1.0 + jnp.exp(-gate))
+        silu = gate * sig
+        low = (silu * up).astype(BF)
+        out = dot(low, wexp[2], NT)
+        mixp[four] = (prob * out).astype(BF).reshape(4, 2, TB // 8, width)
+        moved = dot(grad, wexp[2])
+        seen = jnp.sum(low.astype(F32) * moved, axis=-1, keepdims=True)
+        for b in range(4):
+            line = jnp.transpose(jnp.broadcast_to(seen[b * 128 : b * 128 + 128], (128, 128)))[0:8]
+            gg[zz * 4 + b] = line
+        grad_hidden = moved * prob
+        grad_gate = (grad_hidden * up * (sig * (1.0 + gate * (1.0 - sig)))).astype(BF)
+        grad_up = (grad_hidden * silu).astype(BF)
+        below = dot(grad_gate, wexp[0], NT) + dot(grad_up, wexp[1], NT)
+        backp[four] = below.astype(BF).reshape(4, 2, TB // 8, width)
+        one.begin_plane(zz)
+        two.begin_plane(zz)
+        acc[0] += dot(rest, grad_gate, TN)
+        acc[1] += dot(rest, grad_up, TN)
+        acc[2] += dot(grad, (prob * low.astype(F32)).astype(BF), TN)
+        return 0
+
+    lax.fori_loop(0, 4, chunk, 0)
+    seen_out = Exchange(lambda r: gg.at[r], lambda r: g_all.at[r], g_send, g_recv)
+    seen_out.begin()
+    one.fold(order[2])
+    one.fold(order[3])
+    dw[...] = acc[...].astype(BF).reshape(dw.shape)
+    over = remote(dw.at[:, 1 - x], dwx, x_sem.at[0], x_sem.at[1], (1 - x, s))
+    over.start()
+    one.flow()
     two.run()
+    hidden.end_sends()
+    seen_out.end()
     one.end()
     two.end()
-    minor.end()
-
-
-def back_between(
-    back, g_all, cot, probs, picked, normed, scale, small, wo, att, h2, g_res, ga_t, dwo
+    over.wait()
+    dwx[...] = (dwx[...].astype(F32) + dw[:, x].astype(F32)).astype(BF)
+
+
+def rear(
+    back, g_all, cot, probs, picked, normed, scale, wo, att, h2, dwx, q_t, k_t, v_t, lse, o_t, start, hid, cos, sin,
+    wp, tok,
+    grad_tokens, dw_all, dwo_sum, wg_all,
+    g_res, ga_t, dwo, dwo_x, go_t, gq_t, gkv, k_n, v_n, delta, got, g_t, wg, g_mine,
+    *rest,
 ):
-    gain = jnp.transpose(small[...].astype(F32))[E + 1 : E + 2, :]
+    bufs = rest[:NBUF]
+    sems = rest[NBUF:]
+    a_send, a_recv, w_send, w_recv, b_send, b_recv, v_send, v_recv, x_sem = sems[NSEM:]
+    x, s, z, y, c = place()
+    width = att.shape[1]
+    length = hid.shape[0]
+    barrier_all()
+
     seen = jnp.concatenate([g_all[e, 0:1, :] for e in range(E)] + [jnp.zeros((128 - E, 128), F32)], axis=0)
     grad_probs = jnp.transpose(seen) * picked[...]
     prob = probs[...]
     grad_logits = (prob * (grad_probs - jnp.sum(prob * grad_probs, axis=-1, keepdims=True))).astype(BF)
-    grad_second = back[...].astype(F32) + dot(grad_logits, small[...], NT)
-    u = grad_second * gain
+    u = back[...].astype(F32) + dot(grad_logits, wo[:, width : width + 128], NT)
     norm = normed[...]
     grad = cot[...].astype(F32) + scale[:, 0:1] * (u - norm * jnp.mean(u * norm, axis=-1, keepdims=True))
     g_res[...] = grad
     branch = grad.astype(BF)
-    ga_t[...] = jnp.transpose(dot(branch, wo[...])).astype(BF)
-    dwo[:, 0:1024] = dot(jnp.transpose(grad).astype(BF), att[...]).astype(BF)
-    dwo[:, 1024:1152] = dot(h2[...], grad_logits, TN).astype(BF)
-
-
-def grads_out(ga_t, dw, dwo, go_t, dw_all, dwo_sum, *rest):
-    bufs = rest[:NBUF]
-    dwx, dwo_x = rest[NBUF : NBUF + 2]
-    sems = rest[NBUF + 2 :]
-    a_send, a_recv, w_send, w_recv, x_sem = sems[NSEM:]
-    x, s, z, y, c = place()
-    barrier_row(partner=True)
+    ga_t[...] = jnp.transpose(dot(branch, wo[:, 0:width])).astype(BF).reshape(ga_t.shape)
     heads = Exchange(lambda h: ga_t.at[h], lambda t: go_t.at[:, lane_block(t, 128)], a_send, a_recv)
     heads.begin()
-    over = remote(dw.at[:, 1 - x], dwx, x_sem.at[0], x_sem.at[1], (1 - x, s))
-    over.start()
-    over_o = remote(dwo.at[1 - x], dwo_x, x_sem.at[2], x_sem.at[3], (1 - x, s))
+    dwo[:, :, :, :, 0:width] = dot(jnp.transpose(grad).astype(BF), att[...]).astype(BF).reshape(2, 16, 2, 16, width)
+    dwo[:, :, :, :, width : width + 128] = dot(h2[...], grad_logits, TN).astype(BF).reshape(2, 16, 2, 16, 128)
+    over_o = remote(dwo.at[1 - x], dwo_x, x_sem.at[0], x_sem.at[1], (1 - x, s))
     over_o.start()
+    k_n[...] = jnp.transpose(k_t[...].astype(F32)).astype(BF)
+    v_n[...] = jnp.transpose(v_t[...].astype(F32)).astype(BF)
+    gkv[...] = jnp.zeros(gkv.shape, F32)
+    weights = Exchange(lambda r: dwx.at[:, r], lambda e: dw_all.at[e], w_send, w_recv)
+    heads.end()
+    weights.begin(range(8))
+    delta[...] = jnp.sum(go_t[...].astype(F32) * o_t[...], axis=0, keepdims=True)
+
+    def query_block(i, _):
+        cols = lane_block(i)
+        queries, grads = q_t[:, cols], go_t[:, cols]
+        begin, log_total, shift = start[:, cols], lse[:, cols], delta[:, cols]
+
+        def key_block(j, sofar):
+            rows = lane_block(j)
+            scores = dot(k_n[rows, :], queries) * SCORE
+            powers = jnp.where(allowed_mask(j * QB, i * QB, begin), jnp.exp2(scores - log_total), 0.0)
+            moved = dot(v_n[rows, :], grads)
+            grad_scores = (powers * (moved - shift)).astype(BF)
+            gkv[0, :, rows] += dot(queries, grad_scores, NT)
+            gkv[1, :, rows] += dot(grads, powers.astype(BF), NT)
+            return sofar + dot(k_t[:, rows], grad_scores)
+
+        gq_t[:, cols] = lax.fori_loop(0, i + 1, key_block, jnp.zeros((HEAD_SIZE, QB), F32))
+        return 0
+
+    blocks = length // QB
+    cut = (5 * blocks) // 8
+    lax.fori_loop(0, cut, query_block, 0)
     over_o.wait_recv()
     dwo_x[...] = (dwo_x[...].astype(F32) + dwo[x].astype(F32)).astype(BF)
     out = Reduce(dwo_x, dwo_sum, bufs, sems[:NSEM])
     out.begin()
-    out.run()
-    over.wait_recv()
-    dwx[...] = (dwx[...].astype(F32) + dw[:, x].astype(F32)).astype(BF)
-    weights = Exchange(lambda r: dwx.at[:, r], lambda e: dw_all.at[e], w_send, w_recv)
-    weights.begin()
-    weights.end()
-    heads.end()
-    out.end()
-    over.wait_send()
-    over_o.wait_send()
-
-
-def attention_backward(q_t, k_t, v_t, lse, o_t, go_t, start, gq_t, gkv_t, k_n, v_n, delta):
-    k_n[...] = jnp.transpose(k_t[...].astype(F32)).astype(BF)
-    v_n[...] = jnp.transpose(v_t[...].astype(F32)).astype(BF)
-    gkv_t[...] = jnp.zeros(gkv_t.shape, F32)
-    delta[...] = jnp.sum(go_t[...].astype(F32) * o_t[...], axis=0, keepdims=True)
-
-    def query_block(i, _):
-        cols = lane_block(i)
-        queries, grads = q_t[:, cols], go_t[:, cols]
-        begin, log_total, shift = start[:, cols], lse[:, cols], delta[:, cols]
-
-        def key_block(j, acc):
-            rows = lane_block(j)
-            scores = dot(k_n[rows, :], queries) * SCORE
-            weights = jnp.where(
-                allowed_mask(j * QB, i * QB, begin), jnp.exp2(scores - log_total), 0.0
-            )
-            moved = dot(v_n[rows, :], grads)
-            grad_scores = (weights * (moved - shift)).astype(BF)
-            gkv_t[0:64, rows] += dot(queries, grad_scores, NT)
-            gkv_t[64:128, rows] += dot(grads, weights.astype(BF), NT)
-            return acc + dot(k_t[:, rows], grad_scores)
-
-        gq_t[:, cols] = lax.fori_loop(0, i + 1, key_block, jnp.zeros((HEAD_SIZE, QB), F32))
-        return 0
-
-    lax.fori_loop(0, q_t.shape[1] // QB, query_block, 0)
-
-
-def share_pair(gkv, got, send, recv):
-    x, s, z, y, c = place()
-    sem = pltpu.get_barrier_semaphore()
-    mate = (x, seat(z, y, 1 - c))
-    pl.semaphore_signal(sem, inc=1, device_id=mate, device_id_type=MESH)
-    pl.semaphore_wait(sem, 1)
-    copy = remote(gkv.at[1 - c], got, send, recv, mate)
-    copy.start()
-    copy.wait()
-
-
-def back_projection(gq_t, gkv, got, hid, cos, sin, g_t, wg):
-    core = lax.axis_index("seq") % 2
+    weights.begin(range(8, 16))
+    lax.fori_loop(cut, blocks, query_block, 0)
+
+    pair = remote(gkv.at[1 - c], got, x_sem.at[2], x_sem.at[3], (x, seat(z, y, 1 - c)))
+    pair.start()
+    for cond, zz, _ in out.order():
+        out.fold(zz, cond)
     scaling = 1.0 / math.sqrt(HEAD_SIZE)
     co, si = cos[...], sin[...]
 
@@ -750,31 +831,28 @@
         a, b = part[:32], part[32:]
         return jnp.concatenate([a * co + b * si, b * co - a * si], axis=0)
 
-    g_t[0:64, :] = unturn(gq_t[...] * scaling).astype(BF)
-    mine = gkv[core] + got[...]
-    g_t[64:128, :] = jnp.where(core == 0, unturn(mine * scaling), mine).astype(BF)
-    wg[...] = jnp.transpose(dot(g_t[...], hid[...])).astype(BF)
-
-
-def last_exchange(g_t, wg, g_mine, wg_all, *sems):
-    a_send, a_recv, w_send, w_recv = sems
-    barrier_all()
-    heads = Exchange(lambda t: g_t.at[:, lane_block(t, 128)], lambda h: g_mine.at[h], a_send, a_recv)
-    heads.begin()
-    weights = Exchange(lambda r: wg.at[r], lambda r: wg_all.at[r], w_send, w_recv, wide=True)
-    weights.begin()
-    heads.end()
+    g_t[0] = unturn(gq_t[...] * scaling).astype(BF)
+    pair.wait()
+    mine = gkv[c] + got[...]
+    g_t[1] = jnp.where(c == 0, unturn(mine * scaling), mine).astype(BF)
+    tokens = Exchange(
+        lambda t: g_t.at[:, :, lane_block(t, 128)], lambda h: g_mine.at[h // 2, :, h % 2], b_send, b_recv
+    )
+    tokens.begin()
+    wg[...] = jnp.transpose(dot(g_t[...].reshape(128, length), hid[...])).astype(BF).reshape(wg.shape)
+    columns = Exchange(lambda r: wg.at[r], lambda r: wg_all.at[r], v_send, v_recv, wide=True)
+    columns.begin()
+    tokens.end()
+    w = jnp.transpose(dot(wp[...], g_mine[...].reshape(2 * width, 128)))
+    values = tok[...].astype(F32)
+    scale_first = lax.rsqrt(jnp.mean(values * values, axis=-1, keepdims=True) + EPSILON)
+    norm = values * scale_first
+    grad_tokens[...] = g_res[...] + scale_first * (w - norm * jnp.mean(w * norm, axis=-1, keepdims=True))
+    out.flow()
+    out.end()
+    columns.end()
     weights.end()
-
-
-def last_rows(g_mine, wp, tok, small, g_res, grad_tokens):
-    gain = jnp.transpose(small[...].astype(F32))[E : E + 1, :]
-    first = jnp.transpose(dot(wp[...], g_mine[...]))
-    values = tok[...].astype(F32)
-    scale = lax.rsqrt(jnp.mean(values * values, axis=-1, keepdims=True) + EPSILON)
-    norm = values * scale
-    w = first * gain
-    grad_tokens[...] = g_res[...] + scale * (w - norm * jnp.mean(w * norm, axis=-1, keepdims=True))
+    over_o.wait_send()
 
 
 def frequencies(head_dim):
@@ -802,91 +880,88 @@
     D = MODEL_WIDTH
     rows = tokens.shape[1]
     length = 16 * rows
-    pair = jnp.stack([key_matrix.reshape(32, 8, 64), value_matrix.reshape(32, 8, 64)], axis=2).reshape(32, 16, 64)
-    wperm = jnp.concatenate([query_weight.reshape(32, 16, 64), pair], axis=2).reshape(32, 2048)
-    small = jnp.concatenate(
-        [router_weight, attention_gain[:, None], expert_gain[:, None], jnp.zeros((32, 128 - E - 2), BF)], axis=1
-    )
-    w3 = jnp.stack([gate_weight, up_weight, down_weight]).transpose(2, 0, 1, 3)
+    gain_first, gain_second = attention_gain.astype(F32)[:, None], expert_gain.astype(F32)[:, None]
+    scaled_query = (query_weight.astype(F32) * gain_first).astype(BF).reshape(32, 8, 128)
+    scaled_key = (key_matrix.astype(F32) * gain_first).astype(BF).reshape(32, 8, 64)
+    scaled_value = (value_matrix.astype(F32) * gain_first).astype(BF).reshape(32, 8, 64)
+    wperm = jnp.concatenate([scaled_query, scaled_key, scaled_value], axis=2).reshape(32, 2048)
+    scaled_router = (router_weight.astype(F32) * gain_second).astype(BF)
+    wo_router = jnp.concatenate([output_weight, scaled_router, jnp.zeros((32, 128 - E), BF)], axis=1)
+    w3 = jnp.stack(
+        [
+            (gate_weight.astype(F32) * gain_second[..., None]).astype(BF),
+            (up_weight.astype(F32) * gain_second[..., None]).astype(BF),
+            down_weight,
+        ]
+    ).transpose(2, 0, 1, 3)
     angle = (
         jnp.arange(length, dtype=F32)[None, :] / jnp.power(2.0, rope_index.astype(F32))[:, None]
     ) * frequencies(HEAD_SIZE)[:, None]
     cos, sin = jnp.cos(angle), jnp.sin(angle)
-    segment_all = lax.all_gather(segments.astype(jnp.int32), "seq", axis=1, tiled=True)
-    start = jnp.sum((segment_all[:, None, :] < segment_all[:, :, None]).astype(jnp.int32), axis=-1, dtype=jnp.int32)
     wp_all = lax.all_gather(wperm, ("row", "seq"), axis=0, tiled=True)
     cot_all = lax.all_gather(cotangent[0], "seq", axis=0, tiled=True)
 
-    tok_all, w_mine, small_all, wo_all = comm_call(
-        gather_first,
-        [sds((16, 2, rows // 2, D), BF), sds((32, 32, 256), BF), sds((32, 32, 128), BF), sds((2, 16, 32, D), BF)],
-        [tokens.reshape(2, rows // 2, D), wperm, small, output_weight],
-        GATHER_SEMS * 2 + [DMA((32,))] * 4 + [DMA((4,))],
+    tok_mine = tokens.reshape(rows, D)
+    (
+        hid, q_t, k_t, v_t, o_t, lse, start, wexp, wo_all,
+        residual, normed, scale, h2, att, probs, picked, p_t,
+    ) = comm_call(
+        front,
+        [sds((length, D), BF)]
+        + [sds((64, length), BF)] * 3
+        + [sds((64, length), F32), sds((1, length), F32), sds((1, length), jnp.int32)]
+        + [sds((3, 32, 32, F), BF), sds((2, 16, 32, D + 128), BF)]
+        + [sds((rows, D), F32), sds((rows, D), F32), sds((rows, 128), F32), sds((rows, D), BF), sds((rows, D), BF)]
+        + [sds((rows, 128), F32), sds((rows, 128), F32), sds((E, rows), F32)],
+        [
+            tokens.reshape(2, rows // 2, D),
+            wperm,
+            wo_router,
+            w3,
+            jnp.broadcast_to(segments.astype(jnp.int32), (8, rows)),
+            routes.reshape(rows, K),
+            cos,
+            sin,
+        ],
+        GATHER_SEMS * 2 + [DMA((16,))] * 10 + [DMA((4,))],
         0,
-    )
-    small_all = small_all.reshape(D, 128)
-    wo_all = wo_all.reshape(D, D)
-    hid, q_t, k_t, v_t, o_t, lse, o_low = compute_call(
-        attention_forward,
         [
-            sds((length, D), BF),
-            sds((64, length), BF),
-            sds((64, length), BF),
-            sds((64, length), BF),
-            sds((64, length), F32),
-            sds((1, length), F32),
-            sds((64, length), BF),
+            VM((16, 2, rows // 2, D), BF),
+            VM((2, 8, 2, 32, 256), BF),
+            VM((16, 8, rows), jnp.int32),
+            VM((64, length), BF),
+            VM((16, 64, rows), BF),
+            VM((length, 64), BF),
+            VM((256, D), BF),
         ],
-        [tok_all.reshape(length, D), w_mine.reshape(D, 256), small_all, cos, sin, start],
-        [VM((length, 64), BF), VM((128, D), F32), VM((256, D), BF)],
-    )
-    att_t, wexp = comm_call(
-        heads_to_tokens,
-        [sds((16, 64, rows), BF), sds((3, 32, 32, F), BF)],
-        [o_low, w3],
-        [DMA((16,))] * 6,
+    )
+    wo_all = wo_all.reshape(D, D + 128)
+    back, mix, g_all, dwx = comm_call(
+        middle,
+        [
+            sds((2, rows // 2, D), BF),
+            sds((2, rows // 2, D), BF),
+            sds((16, 8, rows), F32),
+            sds((3, 16, 32, F), BF),
+        ],
+        [h2.reshape(2, rows // 2, D), p_t, cot_all, wexp.reshape(3, D, F)],
+        Reduce.SEMS * 2 + GATHER_SEMS + [DMA((16,))] * 2 + [DMA((1,))] + [DMA((16,))] * 2 + [DMA((2,))],
         1,
-    )
-    tok_mine = tokens.reshape(rows, D)
-    residual, normed, scale, h2, att, probs, picked, p_t = compute_call(
-        between,
         [
-            sds((rows, D), F32),
-            sds((rows, D), F32),
-            sds((rows, 128), F32),
-            sds((rows, D), BF),
-            sds((rows, D), BF),
-            sds((rows, 128), F32),
-            sds((rows, 128), F32),
-            sds((E, rows), F32),
-        ],
-        [tok_mine, att_t.reshape(D, rows), wo_all, small_all, routes.reshape(rows, K)],
-    )
-    h_all, p_all = comm_call(
-        gather_second,
-        [sds((16, 2, rows // 2, D), BF), sds((16, E, rows), F32)],
-        [h2.reshape(2, rows // 2, D), p_t],
-        GATHER_SEMS + [DMA((16,))] * 2 + [DMA((1,))],
-        2,
-    )
-    mixp, backp, gg, dw = compute_call(
-        expert_body,
-        [sds((length, D), BF), sds((length, D), BF), sds((16, 8, 128), F32), sds((3, D, F), BF)],
-        [h_all.reshape(length, D), cot_all, p_all, wexp.reshape(3, D, F)],
-        [VM((3, D, F), F32)],
-    )
-    back, mix, g_all = comm_call(
-        reduce_rows,
-        [sds((2, rows // 2, D), BF), sds((2, rows // 2, D), BF), sds((16, 8, 128), F32)],
-        [backp.reshape(16, 2, rows // 2, D), mixp.reshape(16, 2, rows // 2, D), gg],
-        Reduce.SEMS * 2 + [DMA((16,))] * 2,
-        3,
-        Reduce.bufs(rows // 2, D) * 2,
+            VM((16, 2, rows // 2, D), BF),
+            VM((16, E, rows), F32),
+            VM((16, 2, rows // 2, D), BF),
+            VM((16, 2, rows // 2, D), BF),
+            VM((16, 8, rows), F32),
+            VM((3, 2, 16, 32, F), BF),
+            VM((3, D, F), F32),
+        ]
+        + Reduce.bufs(rows // 2, D) * 2,
     )
     mixed = (residual + mix.reshape(rows, D).astype(F32)).astype(BF)
-    g_res, ga_t, dwo = compute_call(
-        back_between,
-        [sds((rows, D), F32), sds((D, rows), BF), sds((D, D + 128), BF)],
+    grad_tokens, dw_all, dwo_sum, wg_all = comm_call(
+        rear,
+        [sds((rows, D), F32), sds((16, 3, 32, F), BF), sds((2, 16, D + 128), BF), sds((32, 32, 128), BF)],
         [
             back.reshape(rows, D),
             g_all,
@@ -895,71 +970,71 @@
             picked,
             normed,
             scale,
-            small_all,
             wo_all,
             att,
             h2,
+            dwx,
+            q_t,
+            k_t,
+            v_t,
+            lse,
+            o_t,
+            start,
+            hid,
+            cos,
+            sin,
+            wp_all,
+            tok_mine,
         ],
-    )
-    go_t, dw_all, dwo_sum = comm_call(
-        grads_out,
-        [sds((64, length), BF), sds((16, 3, 32, F), BF), sds((2, 16, D + 128), BF)],
-        [ga_t.reshape(16, 64, rows), dw.reshape(3, 2, 16, 32, F), dwo.reshape(2, 16, 2, 16, D + 128)],
-        Reduce.SEMS + [DMA((16,))] * 4 + [DMA((4,))],
-        4,
-        Reduce.bufs(16, D + 128) + [VM((3, 16, 32, F), BF), VM((16, 2, 16, D + 128), BF)],
-    )
-    gq_t, gkv_t = compute_call(
-        attention_backward,
-        [sds((64, length), F32), sds((128, length), F32)],
-        [q_t, k_t, v_t, lse, o_t, go_t, start],
-        [VM((length, 64), BF), VM((length, 64), BF), VM((1, length), F32)],
-    )
-    gkv = gkv_t.reshape(2, 64, length)
-    (got,) = comm_call(share_pair, [sds((64, length), F32)], [gkv], [DMA, DMA], 5)
-    g_t, wg = compute_call(
-        back_projection, [sds((128, length), BF), sds((D, 128), BF)], [gq_t, gkv, got, hid, cos, sin]
-    )
-    g_mine, wg_all = comm_call(
-        last_exchange,
-        [sds((16, 128, rows), BF), sds((32, 32, 128), BF)],
-        [g_t, wg.reshape(32, 32, 128)],
-        [DMA((16,))] * 2 + [DMA((32,))] * 2,
-        6,
-    )
-    (grad_tokens,) = compute_call(
-        last_rows, [sds((rows, D), F32)], [g_mine.reshape(2 * D, rows), wp_all, tok_mine, small_all, g_res]
+        Reduce.SEMS + [DMA((16,))] * 6 + [DMA((32,))] * 2 + [DMA((4,))],
+        2,
+        [
+            VM((rows, D), F32),
+            VM((16, 64, rows), BF),
+            VM((2, 16, 2, 16, D + 128), BF),
+            VM((16, 2, 16, D + 128), BF),
+            VM((64, length), BF),
+            VM((64, length), F32),
+            VM((2, 64, length), F32),
+            VM((length, 64), BF),
+            VM((length, 64), BF),
+            VM((1, length), F32),
+            VM((64, length), F32),
+            VM((2, 64, length), BF),
+            VM((32, 32, 128), BF),
+            VM((8, 2, 2, 64, rows), BF),
+        ]
+        + Reduce.bufs(16, D + 128),
     )
     wg_sum = wg_all.reshape(2, 16, 32, 128).astype(F32).sum(axis=0).transpose(1, 0, 2)
-    grad_query_weight = wg_sum[:, :, :64].reshape(32, D)
-    grad_key_weight = wg_sum[:, 0::2, 64:].reshape(32, 512)
-    grad_value_weight = wg_sum[:, 1::2, 64:].reshape(32, 512)
+    plain_query = wg_sum[:, :, :64].reshape(32, D)
+    plain_key = wg_sum[:, 0::2, 64:].reshape(32, 512)
+    plain_value = wg_sum[:, 1::2, 64:].reshape(32, 512)
     own_o = dwo_sum.reshape(32, D + 128).astype(F32)
-    grad_output_weight, grad_router_weight = own_o[:, :D], own_o[:, D : D + E]
+    plain_router = own_o[:, D : D + E]
     expert_grads = dw_all.transpose(1, 2, 0, 3).astype(F32)
-    grad_gate_weight, grad_up_weight, grad_down_weight = expert_grads[0], expert_grads[1], expert_grads[2]
+    plain_gate, plain_up = expert_grads[0], expert_grads[1]
     grad_attention_gain = (
-        jnp.sum(grad_query_weight * query_weight.astype(F32), axis=1)
-        + jnp.sum(grad_key_weight * key_matrix.astype(F32), axis=1)
-        + jnp.sum(grad_value_weight * value_matrix.astype(F32), axis=1)
-    ) / attention_gain.astype(F32)
-    grad_expert_gain = (
-        jnp.sum(grad_gate_weight * gate_weight.astype(F32) + grad_up_weight * up_weight.astype(F32), axis=(1, 2))
-        + jnp.sum(grad_router_weight * router_weight.astype(F32), axis=1)
-    ) / expert_gain.astype(F32)
+        jnp.sum(plain_query * query_weight.astype(F32), axis=1)
+        + jnp.sum(plain_key * key_matrix.astype(F32), axis=1)
+        + jnp.sum(plain_value * value_matrix.astype(F32), axis=1)
+    )
+    grad_expert_gain = jnp.sum(
+        plain_gate * gate_weight.astype(F32) + plain_up * up_weight.astype(F32), axis=(1, 2)
+    ) + jnp.sum(plain_router * router_weight.astype(F32), axis=1)
     return (
         mixed.reshape(tokens.shape),
         grad_tokens.reshape(tokens.shape),
         grad_attention_gain,
         grad_expert_gain,
-        grad_query_weight,
-        grad_key_weight,
-        grad_value_weight,
-        grad_output_weight,
-        grad_router_weight,
-        grad_gate_weight,
-        grad_up_weight,
-        grad_down_weight,
+        plain_query * gain_first,
+        plain_key * gain_first,
+        plain_value * gain_first,
+        own_o[:, :D],
+        plain_router * gain_second,
+        plain_gate * gain_second[..., None],
+        plain_up * gain_second[..., None],
+        expert_grads[2],
     )
 
 

time: 593 us -> 413 us (0.70)
  Pallas kernels: 518 us -> 370 us
  blocking collectives: 19.5 us -> 0 us
  local copies, waits for them, and re-layouts: 20.3 us -> 13.1 us
    pallas_call x7 -> x0, Pallas kernels: 87 us -> none  [compute_call(): pl.pallas_call(body, out_shape=outs, in_specs=[pl.BlockSpec(memory_space=...]
    pallas_call x7 -> x3, Pallas kernels: 431 us -> 370 us  [comm_call(): pl.pallas_call(body, out_shape=outs, in_specs=[pl.BlockSpec(memory_space=...]
    all_gather x1 -> x0, blocking collectives: 19.5 us -> none  [sixteen_seats(): lax.all_gather(segments.astype(jnp.int32), 'seq', axis=1, tiled=True)]
    reduce_sum x6 -> x0, other arithmetic: 7.58 us -> none  [the longest x1 2.63 us: sixteen_seats(): jnp.sum((segment_all[:, None, :] < segment_all[:, :, None]).astype(jnp.in...]
  transfers between devices with their start and end apart: 2 -> 2, of which waited for: 0 -> 0; matrix products, arithmetic and copies ran while one was open for 6% -> 3% of each run, Pallas kernels for 87% -> 67%
where the time goes in v2:
time: 413 us; the launch traced here: 412 us
  Pallas kernels  370 us (90%)
  between operations  15.1 us (4%)
  local copies, waits for them, and re-layouts  13.1 us (3%)
  other arithmetic  12.8 us (3%)
    pallas_call x3, Pallas kernels, comm_call(): pl.pallas_call(body, out_shape=outs, in_specs=[pl.BlockSpec(memory_space=...  370 us
    unnamed x40, local copies, waits for them, and re-layouts  8.88 us
  transfers between devices with their start and end apart: 2, of which 0 were waited for; matrix products, arithmetic and copies ran while one was open for 3% of the time, Pallas kernels for 67%

profile of v2, /device:TPU:0, one launch (start us, length us, event | category | flops | bytes accessed | tf_op | source)
XLA Modules:
  0.0 412.1 jit_solution(10912445663147895318)
XLA Ops:
  7.2 0.0 all-gather.6.cloned.1.call-start
  7.3 0.7 all-gather.6.cloned.1.call-update
  8.0 0.0 all-gather.4.cloned.1.call-start
  8.0 0.7 convert_element_type.79
  8.7 0.9 fusion.12
  9.5 0.1 reshape.101
  9.6 0.1 reshape.102
  9.7 0.9 fusion.16
  10.7 0.1 pad_maximum_fusion
  10.8 0.7 copy.65
  11.4 0.0 all-gather.4.cloned.1.call-update
  11.5 0.3 copy.71
  11.8 0.6 fusion.7
  12.5 0.2 maximum_bitcast_fusion
  12.7 1.3 copy.54.w3
  14.0 0.1 copy.49
  14.7 0.7 copy.53
  15.5 0.1 fusion.17
  15.6 0.7 concatenate.7.wo
  16.3 1.8 multiply_sine_fusion
  18.1 0.6 broadcast_in_dim.8.seg
  18.7 152.4 %shard_map.238 = (bf16[2048,1024]{1,0:T(8,128)(2,1)}, bf16[64,2048]{1,0:T(8,128)(2,1)}, bf16[64,2048]{1,0:T(8,128)(2,1)}, bf16[64,2048]{1,0:T(8,128)(2,1)}, f32[...) custom-call(bf16[2,64,1024]{2,1,0:T(8,128)(2,1)} %bitcast.64, ...), custom_call_target="tpu_custom_call" | custom-call | tf_op jit(solution)/shard_map/pallas_call | solution.py:314
  171.1 0.0 all-gather.6.cloned.1.call-done
  171.2 123.7 %shard_map.239 = (bf16[2,64,1024]{2,1,0:T(8,128)(2,1)}, bf16[2,64,1024]{2,1,0:T(8,128)(2,1)}, f32[16,8,128]{2,1,0:T(8,128)}, bf16[3,16,32,512]{3,2,1,0:T(8,128)(2,1)}) custom-call(bf16[2,64,1024]{2,1,0:T(8,128)(2,1)} %bitcast.66, f32[16,128]{1,0:T(8,128)} %get-tuple-element.39.p_t, bf16[2048,1024]{1,0:T(8,128)(2,1)} %bitcast.56, bf16[3,1024,512]{2,1,0:T(8,128)(2,1)} %bitcast.57), custom_call_target="tpu_custom_call" | custom-call | tf_op jit(solution)/shard_map/pallas_call | solution.py:314
  294.8 1.7 fusion.9
  296.6 94.2 %shard_map.240 = (f32[128,1024]{1,0:T(8,128)}, bf16[16,3,32,512]{3,2,1,0:T(8,128)(2,1)}, bf16[2,16,1152]{2,1,0:T(8,128)(2,1)}, bf16[32,32,128]{2,1,0:T(8,128)(2,1)}) custom-call(bf16[128,1024]{1,0:T(8,128)(2,1)} %bitcast.70, f32[16,8,128]{2,1,0:T(8,128)} %get-tuple-element.43.g_all, bf16[128,1024]{1,0:T(8,128)(2,1)} %bitcast.67, ...), custom_call_target="tpu_custom_call" | custom-call | tf_op jit(solution)/shard_map/pallas_call | solution.py:314
  390.7 1.8 convert_bitcast_fusion
  392.6 1.2 fusion.5
  393.8 0.1 slice_bitcast_fusion
  393.8 0.8 copy-done.9
  394.7 0.1 slice_multiply_fusion
  394.8 0.7 slice.36
  395.4 1.6 copy.60
  397.0 1.6 copy.61
  398.6 1.6 copy.62
  400.2 0.1 fusion.19
  400.4 0.1 copy.56
  400.5 0.1 reshape.113
  400.6 0.1 copy.57
  400.6 0.1 reshape.114
  400.7 0.2 copy.55
  400.9 0.1 reshape.112
  401.0 0.8 broadcast_multiply_fusion
  401.9 0.7 copy.59
  402.5 0.5 add.19
  403.1 0.8 broadcast_multiply_fusion.1
  403.9 0.5 add_add_fusion
  404.4 0.8 copy.74
  (37 shorter events, 0.2 us)
Async XLA Ops:
  7.2 4.3 %copy-start.14 = (bf16[32]{0:T(256)(128)(2,1)S(1)}, bf16[32]{0:T(256)(128)(2,1)}, u32[]{:S(2)}) copy-start(bf16[32]{0:T(256)(128)(2,1)} %param.17) | copy-start | bytes 196
  7.2 4.3 %copy-start.2 = (bf16[32,16,512]{2,1,0:T(8,128)(2,1)S(1)}, bf16[32,16,512]{2,1,0:T(8,128)(2,1)}, u32[]{:S(2)}) copy-start(bf16[32,16,512]{2,1,0:T(8,128)(2,1)} %param.25) | copy-start | bytes 1572868
  7.2 4.6 %copy-start = (bf16[32,16,512]{2,1,0:T(8,128)(2,1)S(1)}, bf16[32,16,512]{2,1,0:T(8,128)(2,1)}, u32[]{:S(2)}) copy-start(bf16[32,16,512]{2,1,0:T(8,128)(2,1)} %param.23) | copy-start | bytes 1572868
  7.2 4.6 %copy-start.1 = (bf16[32,16,512]{2,1,0:T(8,128)(2,1)S(1)}, bf16[32,16,512]{2,1,0:T(8,128)(2,1)}, u32[]{:S(2)}) copy-start(bf16[32,16,512]{2,1,0:T(8,128)(2,1)} %param.24) | copy-start | bytes 1572868
  7.2 163.9 %all-gather.6.cloned.1.call-start = ((), (), s32[]{:S(2)}) async-start(), calls=%async_computation.1 | async-start | bytes 4456448 | tf_op jit(solution)/shard_map/all_gather | solution.py:902
  8.0 288.6 %all-gather.4.cloned.1.call-start = ((), (), s32[]{:S(2)}) async-start(), calls=%async_computation | async-start | bytes 4325376 | tf_op jit(solution)/shard_map/all_gather | solution.py:901
  12.6 1.3 copy-start.11
  12.7 2.0 copy-start.12
  12.7 2.9 copy-start.10
  12.7 5.4 %copy-start.13 = (s32[1,128]{1,0:T(1,128)S(1)}, s32[1,128]{1,0:T(1,128)}, u32[]{:S(2)}) copy-start(s32[1,128]{1,0:T(1,128)} %param.27) | copy-start | bytes 1540
  171.1 123.7 %copy-start.4 = (f32[128,1024]{1,0:T(8,128)S(1)}, f32[128,1024]{1,0:T(8,128)}, u32[]{:S(2)}) copy-start(f32[128,1024]{1,0:T(8,128)} %get-tuple-element.37) | copy-start | bytes 1572868
  393.7 0.9 copy-start.9
  398.6 1.6 copy-start.6
  400.2 0.8 copy-start.5
  400.2 2.9 copy-start.7
  400.2 2.9 copy-start.8
  400.2 4.2 %copy-start.3 = (f32[128,1024]{1,0:T(8,128)S(1)}, f32[128,1024]{1,0:T(8,128)}, u32[]{:S(2)}) copy-start(f32[128,1024]{1,0:T(8,128)} %get-tuple-element.58) | copy-start | bytes 1572868
Sparse Core Ops, SparseCore 0:
  10.2 65.1 all-gather.5
  78.9 90.3 all-gather.3

commit v3 on v2

--- a/solution.py
+++ b/solution.py
@@ -119,98 +119,60 @@
             CORE: (x, seat(z, y, 1 - c)),
         }[k]
 
-    def copy(self, src, h, k, own):
-        ref = self.own(h) if own else self.at(src, h)
-        return remote(ref, self.at(src, h), self.send.at[src, h, k], self.recv.at[src, h], self.device(k))
-
-    def go(self, src, h, k, cond=None, own=False):
+    def copy(self, src, k, own=False):
+        ref = self.own if own else self.at(src)
+        return remote(ref, self.at(src), self.send.at[src, k], self.recv.at[src], self.device(k))
+
+    def go(self, src, k, cond=None, own=False):
         if k == UP:
             cond = both(cond, self.z < 3)
         if k == DOWN:
             cond = both(cond, self.z > 0)
         act = (lambda c: c.wait_send()) if self.ending else (lambda c: c.start())
-        when(cond, lambda: act(self.copy(src, h, k, own)))
-
-    def wait(self, src, h, cond=None):
+        when(cond, lambda: act(self.copy(src, k, own)))
+
+    def wait(self, src, cond=None):
         if self.ending:
             return
-        when(cond, lambda: self.copy(src, h, SIDE, False).wait_recv())
+        when(cond, lambda: self.copy(src, SIDE).wait_recv())
+
+    def sides(self, t):
+        if t == 0:
+            return ((None, self.z, None),)
+        return ((self.z - t >= 0, self.z - t, UP), (self.z + t <= 3, self.z + t, DOWN))
 
     def begin(self):
-        own = self.own is not None
-        for h, k in ((0, UP), (0, DOWN), (1, SIDE), (0, SIDE), (1, UP), (1, DOWN), (0, CORE), (1, CORE)):
-            self.go(self.s, h, k, own=own)
-
-    def near(self):
-        src = seat(self.z, 1 - self.y, self.c)
-        self.wait(src, 1)
-        for k in (UP, DOWN, CORE):
-            self.go(src, 1, k)
-        self.wait(src, 0)
-        self.go(src, 0, CORE)
-
-    def step(self, t):
-        z, y, c = self.z, self.y, self.c
-        for cond, zz, k in ((z - t >= 0, z - t, UP), (z + t <= 3, z + t, DOWN)):
-            mine, other = seat(zz, y, c), seat(zz, 1 - y, c)
-            self.wait(mine, 0, cond)
+        for k in (UP, DOWN, SIDE, CORE):
+            self.go(self.s, k, own=self.own is not None)
+
+    def line(self, t):
+        for cond, zz, k in self.sides(t):
+            src = seat(zz, self.y, self.c)
+            self.wait(src, cond)
             for way in (k, SIDE, CORE):
-                self.go(mine, 0, way, cond)
-            self.wait(mine, 1, cond)
-            for way in (k, CORE):
-                self.go(mine, 1, way, cond)
-            self.wait(other, 1, cond)
-            for way in (k, CORE):
-                self.go(other, 1, way, cond)
-
-    def step_side(self, t):
-        z, y, c = self.z, self.y, self.c
-        for cond, zz in ((z - t >= 0, z - t), (z + t <= 3, z + t)):
-            other = seat(zz, 1 - y, c)
-            self.wait(other, 0, cond)
-            self.go(other, 0, CORE, cond)
-
-    def plane(self, zz, cond=None):
-        for yy in range(2):
-            for h in range(2):
-                self.wait(seat(zz, yy, 1 - self.c), h, cond)
-
-    def planes(self, t):
-        self.step_side(t)
-        for cond, zz in ((self.z - t >= 0, self.z - t), (self.z + t <= 3, self.z + t)):
-            self.plane(zz, cond)
-
-    def end_core(self):
-        for zz in range(4):
-            self.plane(zz)
-
-    def end_sends(self):
+                self.go(src, way, cond)
+
+    def over(self, t):
+        for cond, zz, _ in self.sides(t):
+            src = seat(zz, 1 - self.y, self.c)
+            self.wait(src, cond)
+            self.go(src, CORE, cond)
+
+    def done(self, t):
+        for cond, zz, _ in self.sides(t):
+            for yy in range(2):
+                self.wait(seat(zz, yy, 1 - self.c), cond)
+
+    def end(self):
         self.ending = True
         self.begin()
-        self.near()
-        for t in (1, 2, 3):
-            self.step(t)
-            self.step_side(t)
-
-
-GATHER_SEMS = [DMA((16, 2, 4)), DMA((16, 2))]
-
-
-def run_gathers(gathers):
-    for g in gathers:
-        g.begin()
-    for g in gathers:
-        g.near()
-    for t in (1, 2, 3):
-        for g in gathers:
-            g.step(t)
-    for t in (1, 2, 3):
-        for g in gathers:
-            g.step_side(t)
-    for g in gathers:
-        g.end_core()
-    for g in gathers:
-        g.end_sends()
+        for t in range(4):
+            if t:
+                self.line(t)
+            self.over(t)
+
+
+GATHER_SEMS = [DMA((16, 4)), DMA((16,))]
 
 
 class Exchange:
@@ -310,12 +272,16 @@
         self.over_core(10).wait_send()
 
 
-def comm_call(body, outs, ins, sems, cid, scratch=()):
+ANY = pl.ANY
+SM = pltpu.SMEM
+
+
+def comm_call(body, outs, ins, sems, cid, scratch=(), out_spaces=None, in_spaces=None):
     return pl.pallas_call(
         body,
         out_shape=outs,
-        in_specs=[pl.BlockSpec(memory_space=VM)] * len(ins),
-        out_specs=[pl.BlockSpec(memory_space=VM)] * len(outs),
+        in_specs=[pl.BlockSpec(memory_space=m) for m in in_spaces or [VM] * len(ins)],
+        out_specs=[pl.BlockSpec(memory_space=m) for m in out_spaces or [VM] * len(outs)],
         scratch_shapes=list(scratch) + list(sems),
         compiler_params=pltpu.CompilerParams(
             collective_id=cid, has_side_effects=True, vmem_limit_bytes=VMEM_LIMIT
@@ -336,44 +302,56 @@
 SCORE = math.log2(math.e) / math.sqrt(HEAD_SIZE)
 
 
+def column(line):
+    n = line.shape[1]
+    same = lax.broadcasted_iota(jnp.int32, (n, n), 0) == lax.broadcasted_iota(jnp.int32, (n, n), 1)
+    return jnp.sum(jnp.where(same, jnp.broadcast_to(line.astype(F32), (n, n)), 0.0), axis=1, keepdims=True)
+
+
 def front(
-    tok, wperm, wo, w3, seg, routes, cos, sin,
-    hid, q_t, k_t, v_t, o_t, lse, start, wexp, wo_all,
-    residual, normed, scale_out, h2, att, probs, picked, p_t,
-    tok_all, w_mine, seg_all, o_low, att_t, k_n, w_t,
-    t_send, t_recv, o_send, o_recv, w_send, w_recv, g_send, g_recv,
+    tok, query_w, key_w, value_w, out_w, router_w, gate_w, up_w, down_w, gain_a, gain_e, seg, routes, cot, rope, freq,
+    hid, wexp, wo_all, cot_all, q_t, k_t, v_t, o_t, lse, start, cos, sin,
+    residual, normed, scale_out, h2, att, probs, picked, p_t, wperm,
+    wo, w3, spread, seg_mine, tok_all, w_mine, seg_all, o_low, att_t, k_n, w_t, hid_v, wo_v,
+    t_send, t_recv, o_send, o_recv, c_send, c_recv, w_send, w_recv, g_send, g_recv,
     a_send, a_recv, e_send, e_recv, x_send, x_recv, x_sem,
 ):
     x, s, z, y, c = place()
-    half = tok.shape[1]
+    rows, width = tok.shape
     length = hid.shape[0]
     barrier_all()
-    slices = Slices(wperm, w_mine, w_send, w_recv)
-    slices.begin()
-    over = remote(wo, wo_all.at[x, s], x_sem.at[0], x_sem.at[1], (1 - x, s))
-    over.start()
-    tokens = Gather(lambda h: tok.at[h], lambda src, h: tok_all.at[src, h], t_send, t_recv)
+    tokens = Gather(tok, lambda src: tok_all.at[src], t_send, t_recv)
     tokens.begin()
     keep_tok = pltpu.make_async_copy(tok, tok_all.at[s], x_sem.at[2])
     keep_tok.start()
-    keep = pltpu.make_async_copy(wo, wo_all.at[x, s], x_sem.at[3])
+    seg_mine[...] = jnp.broadcast_to(seg[...], seg_mine.shape)
+    documents = Exchange(lambda r: seg_mine, lambda r: seg_all.at[r], g_send, g_recv)
+    documents.begin()
+    by_first = column(gain_a[...])
+    for j in range(8):
+        wperm[:, 256 * j : 256 * j + 128] = (query_w[:, 128 * j : 128 * j + 128].astype(F32) * by_first).astype(BF)
+        pair = [ref[:, 64 * j : 64 * j + 64].astype(F32) for ref in (key_w, value_w)]
+        wperm[:, 256 * j + 128 : 256 * j + 256] = (jnp.concatenate(pair, axis=1) * by_first).astype(BF)
+    slices = Slices(wperm, w_mine, w_send, w_recv)
+    slices.begin()
+    by_second = column(gain_e[...])
+    wo[:, 0:width] = out_w[...]
+    router = (router_w[...].astype(F32) * by_second).astype(F32)
+    wo[:, width : width + 128] = jnp.concatenate([router, jnp.zeros((32, 128 - E), F32)], axis=1).astype(BF)
+    over = remote(wo, wo_v.at[x, s], x_sem.at[0], x_sem.at[1], (1 - x, s))
+    over.start()
+    keep = pltpu.make_async_copy(wo, wo_v.at[x, s], x_sem.at[3])
     keep.start()
-    documents = Exchange(lambda r: seg, lambda r: seg_all.at[r], g_send, g_recv)
-    documents.begin()
+    for m, ref in enumerate((gate_w, up_w, down_w)):
+        plain = ref[...].astype(F32).reshape(32 * E, F)
+        for b in range(F // 128):
+            lanes = slice(b * 128, b * 128 + 128)
+            spread[b] = plain[:, lanes]
+            for e in range(E):
+                part = spread[b, pl.ds(e, 32, stride=E), :]
+                w3[e, m, :, lanes] = (part * by_second if m < 2 else part).astype(BF)
     weights = Exchange(lambda e: w3.at[e], lambda r: wexp.at[:, x * 16 + r], e_send, e_recv)
     weights.begin(range(4))
-    tokens.near()
-    for t in (1, 2, 3):
-        tokens.step(t)
-    for t in (1, 2, 3):
-        tokens.step_side(t)
-    documents.end()
-    slices.share()
-    keep.wait()
-    remote(wo, wo_all.at[1 - x, s], x_sem.at[0], x_sem.at[1], (1 - x, s)).wait_recv()
-    outw = Gather(None, lambda src, h: wo_all.at[h, src], o_send, o_recv)
-    outw.begin()
-
     def cross(k, begin=True):
         row = weights.index(weights.seat(k, back=True))
         if begin and k:
@@ -386,41 +364,65 @@
             copy.wait_send()
             remote(src, wexp.at[:, (1 - x) * 16 + row], x_send.at[k], x_recv.at[k], (1 - x, s)).wait_recv()
 
-    width = tok.shape[2]
+    factor = jnp.exp2(rope[0].astype(F32))
+    for b in range(length // 128):
+        position = (b * 128 + lax.broadcasted_iota(jnp.int32, (32, 128), 1)).astype(F32)
+        angle = position / factor * freq[...]
+        cos[:, b * 128 : b * 128 + 128] = jnp.cos(angle)
+        sin[:, b * 128 : b * 128 + 128] = jnp.sin(angle)
+    tokens.over(0)
+    tokens.line(1)
+    slices.share()
+    tokens.over(1)
+    tokens.line(2)
+    keep.wait()
+    remote(wo, wo_v.at[1 - x, s], x_sem.at[0], x_sem.at[1], (1 - x, s)).wait_recv()
+    outw = Gather(None, lambda src: wo_v.at[:, src], o_send, o_recv)
+    outw.begin()
+    for k in range(4):
+        cross(k)
     slices.end()
     w_t[...] = jnp.transpose(w_mine[...].reshape(width, 256).astype(F32)).astype(BF)
+    tokens.over(2)
+    tokens.line(3)
+    outw.over(0)
+    outw.line(1)
+    documents.end()
     numbers = seg_all[:, 0, :]
     ends = [jnp.sum((numbers < n).astype(jnp.int32)) for n in (1, 2)]
     for b in range(16):
         line = numbers[b : b + 1]
-        first = jnp.where(line == 0, 0, jnp.where(line == 1, ends[0], ends[1]))
-        start[:, b * 128 : b * 128 + 128] = first
-    tokens.end_core()
+        start[:, b * 128 : b * 128 + 128] = jnp.where(line == 0, 0, jnp.where(line == 1, ends[0], ends[1]))
+    tokens.over(3)
+    outw.over(1)
+    outw.line(2)
+    weights.begin(range(4, 8))
+    for t in range(4):
+        tokens.done(t)
     keep_tok.wait()
-    weights.begin(range(4, 8))
-    for k in range(4):
-        cross(k)
 
     def project(i, _):
-        rows = lane_block(i, 512)
+        cols = lane_block(i, 512)
         values = tok_all[pl.ds(i * 4, 4)].reshape(512, width).astype(F32)
         scale = lax.rsqrt(jnp.mean(values * values, axis=-1, keepdims=True) + EPSILON)
         hidden = (values * scale).astype(BF)
-        hid[rows, :] = hidden
+        hid_v[cols, :] = hidden
         made = dot(w_t[...], hidden, NT)
-        co, si = cos[:, rows], sin[:, rows]
+        co, si = cos[:, cols], sin[:, cols]
         own = jnp.where(c == 0, made[0:64], made[64:128])
         for ref, part in ((q_t, own), (k_t, made[128:192])):
             a, b = part[:32], part[32:]
-            ref[0:32, rows] = (a * co - b * si).astype(BF)
-            ref[32:64, rows] = (b * co + a * si).astype(BF)
-        v_t[:, rows] = made[192:256].astype(BF)
-        k_n[rows, :] = jnp.transpose(k_t[:, rows].astype(F32)).astype(BF)
+            ref[0:32, cols] = (a * co - b * si).astype(BF)
+            ref[32:64, cols] = (b * co + a * si).astype(BF)
+        v_t[:, cols] = made[192:256].astype(BF)
+        k_n[cols, :] = jnp.transpose(k_t[:, cols].astype(F32)).astype(BF)
         return 0
 
     lax.fori_loop(0, length // 512, project, 0)
-    outw.near()
-    outw.step(1)
+    keep_hid = pltpu.make_async_copy(hid_v, hid, x_sem.at[4])
+    keep_hid.start()
+    outw.over(2)
+    outw.line(3)
     weights.begin(range(8, 12))
 
     def query_block(i, _):
@@ -430,14 +432,14 @@
 
         def key_block(j, carried):
             top, total, acc = carried
-            rows = lane_block(j)
-            scores = dot(k_n[rows, :], queries) * SCORE
+            keys = lane_block(j)
+            scores = dot(k_n[keys, :], queries) * SCORE
             scores = jnp.where(allowed_mask(j * QB, i * QB, begin), scores, MASKED)
             fresh = jnp.maximum(top, jnp.max(scores, axis=0, keepdims=True))
             powers = jnp.exp2(scores - fresh)
             decay = jnp.exp2(top - fresh)
             total = total * decay + jnp.sum(powers, axis=0, keepdims=True)
-            acc = acc * decay + dot(v_t[:, rows], powers.astype(BF))
+            acc = acc * decay + dot(v_t[:, keys], powers.astype(BF))
             return fresh, total, acc
 
         top, total, acc = lax.fori_loop(
@@ -455,23 +457,29 @@
     blocks = length // QB
     cut = (5 * blocks) // 8
     lax.fori_loop(0, cut, query_block, 0)
-    outw.step(2)
-    outw.step(3)
-    for t in (1, 2, 3):
-        outw.step_side(t)
+    outw.over(3)
     for k in range(4, 8):
         cross(k)
-    weights.begin(range(12, 16))
     lax.fori_loop(cut, blocks, query_block, 0)
     heads = Exchange(lambda t: o_low.at[:, lane_block(t, 128)], lambda h: att_t.at[h], a_send, a_recv)
     heads.begin()
-    outw.end_core()
+    weights.begin(range(12, 16))
+    cots = Gather(cot, lambda src: cot_all.at[src], c_send, c_recv)
+    cots.begin()
+    keep_cot = pltpu.make_async_copy(cot, cot_all.at[s], x_sem.at[6])
+    keep_cot.start()
+    for t in range(4):
+        outw.done(t)
+    keep_wo = pltpu.make_async_copy(wo_v, wo_all, x_sem.at[5])
+    keep_wo.start()
     for k in range(8, 12):
         cross(k)
     heads.end()
-
-    att[...] = jnp.transpose(att_t[...].reshape(width, 2 * half).astype(F32)).astype(BF)
-    res = tok[...].reshape(2 * half, width).astype(F32) + dot(att[...], wo_all[:, :, :, 0:width].reshape(width, width), NT)
+    cots.over(0)
+    cots.line(1)
+
+    att[...] = jnp.transpose(att_t[...].reshape(width, rows).astype(F32)).astype(BF)
+    res = tok[...].astype(F32) + dot(att[...], wo_v[:, :, :, 0:width].reshape(width, width), NT)
     residual[...] = res
     scale = lax.rsqrt(jnp.mean(res * res, axis=-1, keepdims=True) + EPSILON)
     norm = res * scale
@@ -480,7 +488,7 @@
     hidden = norm.astype(BF)
     h2[...] = hidden
     lanes = lax.broadcasted_iota(jnp.int32, (128, 128), 1)
-    logits = jnp.where(lanes < E, dot(hidden, wo_all[:, :, :, width : width + 128].reshape(width, 128)), MASKED)
+    logits = jnp.where(lanes < E, dot(hidden, wo_v[:, :, :, width : width + 128].reshape(width, 128)), MASKED)
     top = jnp.max(logits, axis=-1, keepdims=True)
     powers = jnp.exp(logits - top)
     prob = powers / jnp.sum(powers, axis=-1, keepdims=True)
@@ -491,38 +499,37 @@
     picked[...] = mask
     p_t[...] = jnp.transpose(prob * mask)[0:E, :]
 
+    cots.over(1)
+    cots.line(2)
     for k in range(12, 16):
         cross(k)
+    cots.over(2)
+    cots.line(3)
+    cots.over(3)
+    for t in range(4):
+        cots.done(t)
     weights.end(arrivals=False)
     for k in range(16):
         cross(k, begin=False)
-    tokens.end_sends()
-    outw.end_sends()
+    for g in (tokens, outw, cots):
+        g.end()
     over.wait_send()
+    for copy in (keep_hid, keep_wo, keep_cot):
+        copy.wait()
 
 
 class Reduce:
     def __init__(self, part, out, bufs, sems):
         self.part, self.out = part, out
-        self.r1, self.ra, self.ua, self.da, self.ub, self.db, self.rb = bufs
-        (self.s1, self.q1, self.sa, self.qa, self.su, self.qu, self.sd, self.qd, self.sb) = sems
+        self.r1, self.ra, self.ua, self.da = bufs
+        self.s1, self.q1, self.sa, self.qa, self.su, self.qu, self.sd, self.qd = sems
         self.x, self.s, self.z, self.y, self.c = place()
-        self.pending = []
 
     @staticmethod
     def bufs(rows, width):
-        b = (rows, width)
-        return [
-            VM((4, 2, 2) + b, BF),
-            VM((4,) + b, BF),
-            VM((4,) + b, BF),
-            VM((4,) + b, BF),
-            VM((2, 4) + b, BF),
-            VM((2, 4) + b, BF),
-            VM(b, BF),
-        ]
-
-    SEMS = [DMA((4, 2)), DMA((4, 2)), DMA((4,)), DMA((4,)), DMA((3, 4)), DMA((3, 4)), DMA((3, 4)), DMA((3, 4)), DMA((2,))]
+        return [VM((4, 2, rows, width), BF)] + [VM((4, rows, width), BF)] * 3
+
+    SEMS = [DMA((4, 2))] * 2 + [DMA((4,))] * 6
 
     def add(self, dst, src):
         dst[...] = (dst[...].astype(F32) + src[...].astype(F32)).astype(BF)
@@ -538,29 +545,18 @@
 
     def side(self, zz):
         return remote(
-            self.r1.at[zz, 1 - self.y, 0],
+            self.r1.at[zz, 1 - self.y],
             self.ra.at[zz],
             self.sa.at[zz],
             self.qa.at[zz],
             (self.x, seat(self.z, 1 - self.y, self.c)),
         )
 
-    def line(self, lane, zz, up):
+    def line(self, zz, up):
         z, y, c = self.z, self.y, self.c
-        src = self.ra.at[zz] if lane == 0 else self.r1.at[zz, lane - 1, 1]
         if up:
-            dst = self.ua.at[zz] if lane == 0 else self.ub.at[lane - 1, zz]
-            return remote(src, dst, self.su.at[lane, zz], self.qu.at[lane, zz], (self.x, seat(z + 1, y, c)))
-        dst = self.da.at[zz] if lane == 0 else self.db.at[lane - 1, zz]
-        return remote(src, dst, self.sd.at[lane, zz], self.qd.at[lane, zz], (self.x, seat(z - 1, y, c)))
-
-    def landed(self, lane, zz, up):
-        if lane == 0:
-            return (self.ua if up else self.da).at[zz]
-        return (self.ub if up else self.db).at[lane - 1, zz]
-
-    def held(self, lane, zz):
-        return self.ra.at[zz] if lane == 0 else self.r1.at[zz, lane - 1, 1]
+            return remote(self.ra.at[zz], self.ua.at[zz], self.su.at[zz], self.qu.at[zz], (self.x, seat(z + 1, y, c)))
+        return remote(self.ra.at[zz], self.da.at[zz], self.sd.at[zz], self.qd.at[zz], (self.x, seat(z - 1, y, c)))
 
     def order(self):
         z = self.z
@@ -569,37 +565,20 @@
             yield z - t >= 0, z - t, False
         yield None, z, None
 
-    def begin(self):
-        for cond, zz, _ in self.order():
-            for yy in range(2):
-                when(cond, lambda: self.first(zz, yy).start())
-
-    def pass_on(self, lane, zz, up, cond):
-        def go():
-            def add():
-                self.line(lane, zz, up).wait_recv()
-                self.add(self.held(lane, zz), self.landed(lane, zz, up))
-
-            pl.when(self.z > 0 if up else self.z < 3)(add)
-            self.line(lane, zz, up).start()
-
-        when(cond, go)
-
     def begin_plane(self, zz, cond=None):
         for yy in range(2):
             when(cond, lambda: self.first(zz, yy).start())
 
+    def begin(self):
+        for cond, zz, _ in self.order():
+            self.begin_plane(zz, cond)
+
     def fold(self, zz, cond=None):
-        z = self.z
-
         def go():
             for yy in range(2):
                 self.first(zz, yy).wait_recv()
                 self.add(self.r1.at[zz, yy], self.part.at[seat(zz, yy, self.c)])
             self.side(zz).start()
-            for lane in (1, 2):
-                pl.when((zz > z) & (z == 0))(lambda: self.line(lane, zz, True).start())
-                pl.when((zz < z) & (z == 3))(lambda: self.line(lane, zz, False).start())
 
         when(cond, go)
 
@@ -607,44 +586,33 @@
         z = self.z
         for cond, zz, up in self.order():
 
-            def ready():
+            def go():
                 self.side(zz).wait_recv()
-                self.add(self.ra.at[zz], self.r1.at[zz, self.y, 0])
-
-            when(cond, ready)
-            if up is None:
-                continue
-            inner = (z > 0) if up else (z < 3)
-            for lane in (1, 2):
-                self.pass_on(lane, zz, up, both(cond, inner))
-            self.pass_on(0, zz, up, cond)
-        for lane in (1, 2, 0):
-            for up, cond in ((True, z > 0), (False, z < 3)):
+                self.add(self.ra.at[zz], self.r1.at[zz, self.y])
+                if up is None:
+                    return
 
                 def take():
-                    self.line(lane, z, up).wait_recv()
-                    self.add(self.held(lane, z), self.landed(lane, z, up))
-
-                when(cond, take)
-            if lane == 2:
-                self.last().start()
-        self.out[0] = self.ra[z]
-        self.last().wait_recv()
-        self.out[1] = (self.r1[z, self.y, 1].astype(F32) + self.rb[...].astype(F32)).astype(BF)
+                    self.line(zz, up).wait_recv()
+                    self.add(self.ra.at[zz], (self.ua if up else self.da).at[zz])
+
+                pl.when(z > 0 if up else z < 3)(take)
+                self.line(zz, up).start()
+
+            when(cond, go)
+        for up, cond in ((True, z > 0), (False, z < 3)):
+
+            def take():
+                self.line(z, up).wait_recv()
+                self.add(self.ra.at[z], (self.ua if up else self.da).at[z])
+
+            when(cond, take)
+        self.out[...] = self.ra[z]
 
     def run(self):
         for cond, zz, _ in self.order():
             self.fold(zz, cond)
         self.flow()
-
-    def last(self):
-        return remote(
-            self.r1.at[self.z, 1 - self.y, 1],
-            self.rb,
-            self.sb.at[0],
-            self.sb.at[1],
-            (self.x, seat(self.z, 1 - self.y, self.c)),
-        )
 
     def end(self):
         for cond, zz, up in self.order():
@@ -652,72 +620,85 @@
                 when(cond, lambda: self.first(zz, yy).wait_send())
             when(cond, lambda: self.side(zz).wait_send())
             if up is not None:
-                for lane in range(3):
-                    when(cond, lambda: self.line(lane, zz, up).wait_send())
-        self.last().wait_send()
-
-
-NBUF = 7
-NSEM = 9
+                when(cond, lambda: self.line(zz, up).wait_send())
+
+
+NBUF = 4
+NSEM = 8
 TB = 512
 
 
-def middle(h2, p_t, cot, wexp, back, mix, g_all, dwx, h_all, p_all, backp, mixp, gg, dw, acc, *rest):
+def middle(
+    h2, p_t, cot_in, wexp_in, residual,
+    back, mixed, g_all, dwx,
+    h_all, p_all, cot, wexp, backp, mixp, mix, gg, dw, acc,
+    *rest,
+):
     bufs_a, bufs_b = rest[:NBUF], rest[NBUF : 2 * NBUF]
     sems = rest[2 * NBUF :]
-    h_send, h_recv, p_send, p_recv, keep_sem, g_send, g_recv, x_sem = sems[2 * NSEM :]
+    h_send, h_recv, p_send, p_recv, g_send, g_recv, x_sem = sems[2 * NSEM :]
     x, s, z, y, c = place()
+    loads = [
+        pltpu.make_async_copy(wexp_in, wexp, x_sem.at[2]),
+        pltpu.make_async_copy(cot_in, cot, x_sem.at[3]),
+    ]
+    for copy in loads:
+        copy.start()
     barrier_row(partner=True)
-    hidden = Gather(lambda h: h2.at[h], lambda src, h: h_all.at[src, h], h_send, h_recv)
+    hidden = Gather(h2, lambda src: h_all.at[src], h_send, h_recv)
     hidden.begin()
-    keep = pltpu.make_async_copy(h2, h_all.at[s], keep_sem.at[0])
+    keep = pltpu.make_async_copy(h2, h_all.at[s], x_sem.at[4])
     keep.start()
     minor = Exchange(lambda r: p_t, lambda r: p_all.at[r], p_send, p_recv)
     minor.begin()
     one = Reduce(backp, back, bufs_a, sems[:NSEM])
     two = Reduce(mixp, mix, bufs_b, sems[NSEM : 2 * NSEM])
     acc[...] = jnp.zeros(acc.shape, F32)
-    hidden.near()
+    hidden.over(0)
     keep.wait()
     minor.end()
-    hidden.plane(z)
-    hidden.step(1)
+    for copy in loads:
+        copy.wait()
+    hidden.done(0)
+    hidden.line(1)
     far = z // 2
     order = (z, z + 1 - 2 * far, 2 - 2 * z + 5 * far, 3 - 3 * far)
-    width = h2.shape[2]
+    width = h2.shape[1]
+    rows = h2.shape[0]
 
     def chunk(i, _):
         zz = jnp.where(i == 0, order[0], jnp.where(i == 1, order[1], jnp.where(i == 2, order[2], order[3])))
 
         @pl.when(i == 1)
         def _():
-            hidden.planes(1)
-            hidden.step(2)
+            hidden.over(1)
+            hidden.done(1)
+            hidden.line(2)
+            one.fold(order[0])
 
         @pl.when(i == 2)
         def _():
-            hidden.planes(2)
-            hidden.step(3)
-            one.fold(order[0])
+            hidden.over(2)
+            hidden.done(2)
+            hidden.line(3)
+            one.fold(order[1])
 
         @pl.when(i == 3)
         def _():
-            hidden.planes(3)
-            one.fold(order[1])
+            hidden.over(3)
+            hidden.done(3)
+            one.fold(order[2])
 
         four = pl.ds(zz * 4, 4)
-        rows = lane_block(zz, TB)
-        rest = h_all[four].reshape(TB, width)
-        grad = cot[rows, :]
+        some = h_all[four].reshape(4 * rows, width)
+        grad = cot[four].reshape(4 * rows, width)
         cols = [jnp.broadcast_to(p_all[zz * 4 + b, pl.ds(s, 1), :], (128, 128)) for b in range(4)]
         prob = jnp.concatenate([jnp.transpose(v)[:, 0:1] for v in cols], axis=0)
-        gate = dot(rest, wexp[0])
-        up = dot(rest, wexp[1])
+        gate = dot(some, wexp[0])
+        up = dot(some, wexp[1])
         sig = 1.0 / (1.0 + jnp.exp(-gate))
         silu = gate * sig
         low = (silu * up).astype(BF)
-        out = dot(low, wexp[2], NT)
-        mixp[four] = (prob * out).astype(BF).reshape(4, 2, TB // 8, width)
         moved = dot(grad, wexp[2])
         seen = jnp.sum(low.astype(F32) * moved, axis=-1, keepdims=True)
         for b in range(4):
@@ -727,25 +708,27 @@
         grad_gate = (grad_hidden * up * (sig * (1.0 + gate * (1.0 - sig)))).astype(BF)
         grad_up = (grad_hidden * silu).astype(BF)
         below = dot(grad_gate, wexp[0], NT) + dot(grad_up, wexp[1], NT)
-        backp[four] = below.astype(BF).reshape(4, 2, TB // 8, width)
+        backp[four] = below.astype(BF).reshape(4, rows, width)
         one.begin_plane(zz)
+        out = dot(low, wexp[2], NT)
+        mixp[four] = (prob * out).astype(BF).reshape(4, rows, width)
         two.begin_plane(zz)
-        acc[0] += dot(rest, grad_gate, TN)
-        acc[1] += dot(rest, grad_up, TN)
+        acc[0] += dot(some, grad_gate, TN)
+        acc[1] += dot(some, grad_up, TN)
         acc[2] += dot(grad, (prob * low.astype(F32)).astype(BF), TN)
         return 0
 
     lax.fori_loop(0, 4, chunk, 0)
+    one.fold(order[3])
     seen_out = Exchange(lambda r: gg.at[r], lambda r: g_all.at[r], g_send, g_recv)
     seen_out.begin()
-    one.fold(order[2])
-    one.fold(order[3])
     dw[...] = acc[...].astype(BF).reshape(dw.shape)
     over = remote(dw.at[:, 1 - x], dwx, x_sem.at[0], x_sem.at[1], (1 - x, s))
     over.start()
     one.flow()
     two.run()
-    hidden.end_sends()
+    mixed[...] = (residual[...] + mix[...].astype(F32)).astype(BF)
+    hidden.end()
     seen_out.end()
     one.end()
     two.end()
@@ -755,18 +738,22 @@
 
 def rear(
     back, g_all, cot, probs, picked, normed, scale, wo, att, h2, dwx, q_t, k_t, v_t, lse, o_t, start, hid, cos, sin,
-    wp, tok,
+    wperm, tok,
     grad_tokens, dw_all, dwo_sum, wg_all,
-    g_res, ga_t, dwo, dwo_x, go_t, gq_t, gkv, k_n, v_n, delta, got, g_t, wg, g_mine,
+    g_res, ga_t, dwo, dwo_x, go_t, gq_t, gkv, k_n, v_n, delta, got, g_t, wg, g_mine, wp,
     *rest,
 ):
     bufs = rest[:NBUF]
     sems = rest[NBUF:]
-    a_send, a_recv, w_send, w_recv, b_send, b_recv, v_send, v_recv, x_sem = sems[NSEM:]
+    a_send, a_recv, w_send, w_recv, b_send, b_recv, v_send, v_recv, p_send, p_recv, x_sem = sems[NSEM:]
     x, s, z, y, c = place()
     width = att.shape[1]
     length = hid.shape[0]
     barrier_all()
+    over_w = remote(wperm, wp.at[x, s], x_sem.at[4], x_sem.at[5], (1 - x, s))
+    over_w.start()
+    keep_w = pltpu.make_async_copy(wperm, wp.at[x, s], x_sem.at[6])
+    keep_w.start()
 
     seen = jnp.concatenate([g_all[e, 0:1, :] for e in range(E)] + [jnp.zeros((128 - E, 128), F32)], axis=0)
     grad_probs = jnp.transpose(seen) * picked[...]
@@ -780,8 +767,8 @@
     ga_t[...] = jnp.transpose(dot(branch, wo[:, 0:width])).astype(BF).reshape(ga_t.shape)
     heads = Exchange(lambda h: ga_t.at[h], lambda t: go_t.at[:, lane_block(t, 128)], a_send, a_recv)
     heads.begin()
-    dwo[:, :, :, :, 0:width] = dot(jnp.transpose(grad).astype(BF), att[...]).astype(BF).reshape(2, 16, 2, 16, width)
-    dwo[:, :, :, :, width : width + 128] = dot(h2[...], grad_logits, TN).astype(BF).reshape(2, 16, 2, 16, 128)
+    dwo[:, :, :, 0:width] = dot(jnp.transpose(grad).astype(BF), att[...]).astype(BF).reshape(2, 16, 32, width)
+    dwo[:, :, :, width : width + 128] = dot(h2[...], grad_logits, TN).astype(BF).reshape(2, 16, 32, 128)
     over_o = remote(dwo.at[1 - x], dwo_x, x_sem.at[0], x_sem.at[1], (1 - x, s))
     over_o.start()
     k_n[...] = jnp.transpose(k_t[...].astype(F32)).astype(BF)
@@ -789,6 +776,10 @@
     gkv[...] = jnp.zeros(gkv.shape, F32)
     weights = Exchange(lambda r: dwx.at[:, r], lambda e: dw_all.at[e], w_send, w_recv)
     heads.end()
+    keep_w.wait()
+    remote(wperm, wp.at[1 - x, s], x_sem.at[4], x_sem.at[5], (1 - x, s)).wait_recv()
+    columns_all = Gather(None, lambda src: wp.at[:, src], p_send, p_recv)
+    columns_all.begin()
     weights.begin(range(8))
     delta[...] = jnp.sum(go_t[...].astype(F32) * o_t[...], axis=0, keepdims=True)
 
@@ -813,6 +804,8 @@
     blocks = length // QB
     cut = (5 * blocks) // 8
     lax.fori_loop(0, cut, query_block, 0)
+    columns_all.over(0)
+    columns_all.line(1)
     over_o.wait_recv()
     dwo_x[...] = (dwo_x[...].astype(F32) + dwo[x].astype(F32)).astype(BF)
     out = Reduce(dwo_x, dwo_sum, bufs, sems[:NSEM])
@@ -822,6 +815,8 @@
 
     pair = remote(gkv.at[1 - c], got, x_sem.at[2], x_sem.at[3], (x, seat(z, y, 1 - c)))
     pair.start()
+    columns_all.over(1)
+    columns_all.line(2)
     for cond, zz, _ in out.order():
         out.fold(zz, cond)
     scaling = 1.0 / math.sqrt(HEAD_SIZE)
@@ -842,8 +837,13 @@
     wg[...] = jnp.transpose(dot(g_t[...].reshape(128, length), hid[...])).astype(BF).reshape(wg.shape)
     columns = Exchange(lambda r: wg.at[r], lambda r: wg_all.at[r], v_send, v_recv, wide=True)
     columns.begin()
+    columns_all.over(2)
+    columns_all.line(3)
+    columns_all.over(3)
+    for t in range(4):
+        columns_all.done(t)
     tokens.end()
-    w = jnp.transpose(dot(wp[...], g_mine[...].reshape(2 * width, 128)))
+    w = jnp.transpose(dot(wp[...].reshape(width, 2 * width), g_mine[...].reshape(2 * width, 128)))
     values = tok[...].astype(F32)
     scale_first = lax.rsqrt(jnp.mean(values * values, axis=-1, keepdims=True) + EPSILON)
     norm = values * scale_first
@@ -853,6 +853,8 @@
     columns.end()
     weights.end()
     over_o.wait_send()
+    over_w.wait_send()
+    columns_all.end()
 
 
 def frequencies(head_dim):
@@ -881,91 +883,88 @@
     rows = tokens.shape[1]
     length = 16 * rows
     gain_first, gain_second = attention_gain.astype(F32)[:, None], expert_gain.astype(F32)[:, None]
-    scaled_query = (query_weight.astype(F32) * gain_first).astype(BF).reshape(32, 8, 128)
-    scaled_key = (key_matrix.astype(F32) * gain_first).astype(BF).reshape(32, 8, 64)
-    scaled_value = (value_matrix.astype(F32) * gain_first).astype(BF).reshape(32, 8, 64)
-    wperm = jnp.concatenate([scaled_query, scaled_key, scaled_value], axis=2).reshape(32, 2048)
-    scaled_router = (router_weight.astype(F32) * gain_second).astype(BF)
-    wo_router = jnp.concatenate([output_weight, scaled_router, jnp.zeros((32, 128 - E), BF)], axis=1)
-    w3 = jnp.stack(
-        [
-            (gate_weight.astype(F32) * gain_second[..., None]).astype(BF),
-            (up_weight.astype(F32) * gain_second[..., None]).astype(BF),
-            down_weight,
-        ]
-    ).transpose(2, 0, 1, 3)
-    angle = (
-        jnp.arange(length, dtype=F32)[None, :] / jnp.power(2.0, rope_index.astype(F32))[:, None]
-    ) * frequencies(HEAD_SIZE)[:, None]
-    cos, sin = jnp.cos(angle), jnp.sin(angle)
-    wp_all = lax.all_gather(wperm, ("row", "seq"), axis=0, tiled=True)
-    cot_all = lax.all_gather(cotangent[0], "seq", axis=0, tiled=True)
-
     tok_mine = tokens.reshape(rows, D)
+    cot_mine = cotangent.reshape(rows, D)
+    freq = jnp.broadcast_to(frequencies(HEAD_SIZE)[:, None], (32, 128))
     (
-        hid, q_t, k_t, v_t, o_t, lse, start, wexp, wo_all,
-        residual, normed, scale, h2, att, probs, picked, p_t,
+        hid, wexp, wo_all, cot_all, q_t, k_t, v_t, o_t, lse, start, cos, sin,
+        residual, normed, scale, h2, att, probs, picked, p_t, wperm,
     ) = comm_call(
         front,
-        [sds((length, D), BF)]
+        [sds((length, D), BF), sds((3, 32, 32, F), BF), sds((2, 16, 32, D + 128), BF), sds((16, rows, D), BF)]
         + [sds((64, length), BF)] * 3
         + [sds((64, length), F32), sds((1, length), F32), sds((1, length), jnp.int32)]
-        + [sds((3, 32, 32, F), BF), sds((2, 16, 32, D + 128), BF)]
+        + [sds((32, length), F32)] * 2
         + [sds((rows, D), F32), sds((rows, D), F32), sds((rows, 128), F32), sds((rows, D), BF), sds((rows, D), BF)]
-        + [sds((rows, 128), F32), sds((rows, 128), F32), sds((E, rows), F32)],
+        + [sds((rows, 128), F32), sds((rows, 128), F32), sds((E, rows), F32), sds((32, 2 * D), BF)],
         [
-            tokens.reshape(2, rows // 2, D),
-            wperm,
-            wo_router,
-            w3,
-            jnp.broadcast_to(segments.astype(jnp.int32), (8, rows)),
+            tok_mine,
+            query_weight,
+            key_matrix,
+            value_matrix,
+            output_weight,
+            router_weight,
+            gate_weight,
+            up_weight,
+            down_weight,
+            attention_gain.reshape(1, 32),
+            expert_gain.reshape(1, 32),
+            segments.astype(jnp.int32),
             routes.reshape(rows, K),
-            cos,
-            sin,
+            cot_mine,
+            rope_index.astype(jnp.int32),
+            freq,
         ],
-        GATHER_SEMS * 2 + [DMA((16,))] * 10 + [DMA((4,))],
+        GATHER_SEMS * 3 + [DMA((16,))] * 10 + [DMA((8,))],
         0,
         [
-            VM((16, 2, rows // 2, D), BF),
+            VM((32, D + 128), BF),
+            VM((E, 3, 32, F), BF),
+            VM((F // 128, 32 * E, 128), F32),
+            VM((8, rows), jnp.int32),
+            VM((16, rows, D), BF),
             VM((2, 8, 2, 32, 256), BF),
             VM((16, 8, rows), jnp.int32),
             VM((64, length), BF),
             VM((16, 64, rows), BF),
             VM((length, 64), BF),
             VM((256, D), BF),
+            VM((length, D), BF),
+            VM((2, 16, 32, D + 128), BF),
         ],
+        [ANY] * 4 + [VM] * 17,
+        [VM] * 14 + [SM, VM],
     )
     wo_all = wo_all.reshape(D, D + 128)
-    back, mix, g_all, dwx = comm_call(
+    back, mixed, g_all, dwx = comm_call(
         middle,
-        [
-            sds((2, rows // 2, D), BF),
-            sds((2, rows // 2, D), BF),
-            sds((16, 8, rows), F32),
-            sds((3, 16, 32, F), BF),
-        ],
-        [h2.reshape(2, rows // 2, D), p_t, cot_all, wexp.reshape(3, D, F)],
-        Reduce.SEMS * 2 + GATHER_SEMS + [DMA((16,))] * 2 + [DMA((1,))] + [DMA((16,))] * 2 + [DMA((2,))],
+        [sds((rows, D), BF), sds((rows, D), BF), sds((16, 8, rows), F32), sds((3, 16, 32, F), BF)],
+        [h2, p_t, cot_all, wexp.reshape(3, D, F), residual],
+        Reduce.SEMS * 2 + GATHER_SEMS + [DMA((16,))] * 4 + [DMA((8,))],
         1,
         [
-            VM((16, 2, rows // 2, D), BF),
+            VM((16, rows, D), BF),
             VM((16, E, rows), F32),
-            VM((16, 2, rows // 2, D), BF),
-            VM((16, 2, rows // 2, D), BF),
+            VM((16, rows, D), BF),
+            VM((3, D, F), BF),
+            VM((16, rows, D), BF),
+            VM((16, rows, D), BF),
+            VM((rows, D), BF),
             VM((16, 8, rows), F32),
             VM((3, 2, 16, 32, F), BF),
             VM((3, D, F), F32),
         ]
-        + Reduce.bufs(rows // 2, D) * 2,
-    )
-    mixed = (residual + mix.reshape(rows, D).astype(F32)).astype(BF)
+        + Reduce.bufs(rows, D) * 2,
+        None,
+        [VM, VM, ANY, ANY, VM],
+    )
     grad_tokens, dw_all, dwo_sum, wg_all = comm_call(
         rear,
-        [sds((rows, D), F32), sds((16, 3, 32, F), BF), sds((2, 16, D + 128), BF), sds((32, 32, 128), BF)],
+        [sds((rows, D), F32), sds((16, 3, 32, F), BF), sds((32, D + 128), BF), sds((32, 32, 128), BF)],
         [
-            back.reshape(rows, D),
+            back,
             g_all,
-            cotangent.reshape(rows, D),
+            cot_mine,
             probs,
             picked,
             normed,
@@ -983,16 +982,16 @@
             hid,
             cos,
             sin,
-            wp_all,
+            wperm,
             tok_mine,
         ],
-        Reduce.SEMS + [DMA((16,))] * 6 + [DMA((32,))] * 2 + [DMA((4,))],
+        Reduce.SEMS + [DMA((16,))] * 6 + [DMA((32,))] * 2 + GATHER_SEMS + [DMA((8,))],
         2,
         [
             VM((rows, D), F32),
             VM((16, 64, rows), BF),
-            VM((2, 16, 2, 16, D + 128), BF),
-            VM((16, 2, 16, D + 128), BF),
+            VM((2, 16, 32, D + 128), BF),
+            VM((16, 32, D + 128), BF),
             VM((64, length), BF),
             VM((64, length), F32),
             VM((2, 64, length), F32),
@@ -1003,14 +1002,15 @@
             VM((2, 64, length), BF),
             VM((32, 32, 128), BF),
             VM((8, 2, 2, 64, rows), BF),
+            VM((2, 16, 32, 2 * D), BF),
         ]
-        + Reduce.bufs(16, D + 128),
+        + Reduce.bufs(32, D + 128),
     )
     wg_sum = wg_all.reshape(2, 16, 32, 128).astype(F32).sum(axis=0).transpose(1, 0, 2)
     plain_query = wg_sum[:, :, :64].reshape(32, D)
     plain_key = wg_sum[:, 0::2, 64:].reshape(32, 512)
     plain_value = wg_sum[:, 1::2, 64:].reshape(32, 512)
-    own_o = dwo_sum.reshape(32, D + 128).astype(F32)
+    own_o = dwo_sum.astype(F32)
     plain_router = own_o[:, D : D + E]
     expert_grads = dw_all.transpose(1, 2, 0, 3).astype(F32)
     plain_gate, plain_up = expert_grads[0], expert_grads[1]

time: 413 us -> 361 us (0.87)
  Pallas kernels: 370 us -> 342 us
  between operations: 15.1 us -> 1.53 us
  other arithmetic: 12.8 us -> 5.9 us
    pallas_call x3, Pallas kernels: 370 us -> 342 us  [comm_call(): pl.pallas_call(body, out_shape=outs, in_specs=[pl.BlockSpec(memory_space=...]
    unnamed x40 -> x32, local copies, waits for them, and re-layouts: 8.88 us -> 9.74 us
  transfers between devices with their start and end apart: 2 -> 0, of which waited for: 0 -> 0; matrix products, arithmetic and copies ran while one was open for 3% -> 0% of each run, Pallas kernels for 67% -> 0%
where the time goes in v3:
time: 361 us
  Pallas kernels  342 us (95%)
  local copies, waits for them, and re-layouts  11.9 us (3%)
  other arithmetic  5.9 us (2%)
    pallas_call x3, Pallas kernels, comm_call(): pl.pallas_call(body, out_shape=outs, in_specs=[pl.BlockSpec(memory_space=...  342 us
    unnamed x32, local copies, waits for them, and re-layouts  9.74 us

profile of v3, /device:TPU:0, one launch (start us, length us, event | category | flops | bytes accessed | tf_op | source)
XLA Modules:
  0.0 361.1 jit_solution(3475730639490276769)
XLA Ops:
  0.6 1.4 copy.48.router_w
  2.0 1.4 copy.47
  3.4 0.7 broadcast_in_dim.2.freq
  4.8 129.4 %shard_map.238 = (bf16[2048,1024]{1,0:T(8,128)(2,1)}, bf16[3,32,32,512]{3,2,1,0:T(8,128)(2,1)}, bf16[2,16,32,1152]{3,2,1,0:T(8,128)(2,1)}, bf16[16,128,1024]{2,1...) custom-call(bf16[128,1024]{1,0:T(8,128)(2,1)} %bitcast.35, ...), custom_call_target="tpu_custom_call" | custom-call | tf_op jit(solution)/shard_map/pallas_call | solution.py:280
  134.1 111.4 %shard_map.239 = (bf16[128,1024]{1,0:T(8,128)(2,1)}, bf16[128,1024]{1,0:T(8,128)(2,1)}, f32[16,8,128]{2,1,0:T(8,128)}, bf16[3,16,32,512]{3,2,1,0:T(8,128)(2,1)}) custom-call(bf16[128,1024]{1,0:T(8,128)(2,1)} %get-tuple-element.41.h2, f32[16,128]{1,0:T(8,128)} %get-tuple-element.42.p_t, bf16[16,128,1024]{2,1,0:T(8,128)(2,1)} %get-tuple-element.43.cot_in, ...), custom_call_target="tpu_custom_call" | custom-call | tf_op jit(solution)/shard_map/pallas_call | solution.py:280
  245.5 101.0 %shard_map.240 = (f32[128,1024]{1,0:T(8,128)}, bf16[16,3,32,512]{3,2,1,0:T(8,128)(2,1)}, bf16[32,1152]{1,0:T(8,128)(2,1)}, bf16[32,32,128]{2,1,0:T(8,128)(2,1)}) custom-call(bf16[128,1024]{1,0:T(8,128)(2,1)} %get-tuple-element.47.back, f32[16,8,128]{2,1,0:T(8,128)} %get-tuple-element.48.g_all, bf16[128,1024]{1,0:T(8,128)(2,1)} %bitcast.38, ...), custom_call_target="tpu_custom_call" | custom-call | tf_op jit(solution)/shard_map/pallas_call | solution.py:280
  346.6 0.0 copy-start.10
  346.6 0.0 copy-start
  346.6 0.0 copy-start.1
  346.6 1.9 convert_bitcast_fusion
  348.5 0.0 copy-done.10
  348.5 0.0 copy-start.2
  348.5 0.0 copy-start.9
  348.6 0.0 copy-done
  348.6 0.0 copy-done.1
  348.6 1.1 fusion.1
  349.7 0.0 copy-done.2
  349.7 0.0 copy-done.9
  349.7 0.1 slice_multiply_fusion
  349.8 0.5 add.15
  350.4 1.6 copy.57
  351.9 1.6 copy.58
  353.5 0.1 slice_bitcast_fusion
  353.6 0.0 copy-start.4
  353.6 0.0 copy-start.5
  353.6 0.0 copy-start.3
  353.6 1.6 copy.59
  355.2 0.0 copy-done.6
  355.3 0.1 fusion.2
  355.4 0.1 copy.50
  355.5 0.1 reshape.82
  355.6 0.1 copy.51
  355.7 0.1 reshape.83
  355.7 0.0 copy-done.11
  355.8 0.0 copy-done.7
  355.8 0.0 copy-done.8
  355.8 0.8 broadcast_multiply_fusion.1
  356.6 0.2 copy.49
  356.8 0.1 reshape.81
  356.9 0.0 copy-done.4
  356.9 0.8 broadcast_multiply_fusion
  357.8 0.5 add_add_fusion
  358.3 0.7 copy.56
  359.0 0.7 slice.36
  359.6 0.0 copy-done.5
  359.6 0.7 copy.66
  360.3 0.0 copy-done.3
  360.3 0.8 copy.67
  (9 shorter events, 0.1 us)
Async XLA Ops:
  346.6 2.0 copy-start.10
  346.6 2.0 copy-start
  346.6 2.0 copy-start.1
  348.5 1.2 copy-start.2
  348.5 1.2 copy-start.9
  351.9 3.3 copy-start.6
  353.5 2.2 copy-start.11
  353.5 2.2 copy-start.7
  353.5 2.2 copy-start.8
  353.6 3.3 copy-start.4
  353.6 6.0 %copy-start.5 = (bf16[128,1024]{1,0:T(8,128)(2,1)S(1)}, bf16[128,1024]{1,0:T(8,128)(2,1)}, u32[]{:S(2)}) copy-start(bf16[128,1024]{1,0:T(8,128)(2,1)} %get-tuple-element.46) | copy-start | bytes 786436
  353.6 6.7 %copy-start.3 = (f32[128,1024]{1,0:T(8,128)S(1)}, f32[128,1024]{1,0:T(8,128)}, u32[]{:S(2)}) copy-start(f32[128,1024]{1,0:T(8,128)} %get-tuple-element.66) | copy-start | bytes 1572868

commit v4 on v3

--- a/solution.py
+++ b/solution.py
@@ -3,6 +3,7 @@
 
 import jax
 import jax.numpy as jnp
+import numpy as np
 from jax import lax
 from jax.experimental import pallas as pl
 from jax.experimental.pallas import tpu as pltpu
@@ -25,7 +26,7 @@
 BF = jnp.bfloat16
 F32 = jnp.float32
 DMA = pltpu.SemaphoreType.DMA
-UP, DOWN, SIDE, CORE = range(4)
+UP, DOWN, SIDE, CORE, ACROSS = range(5)
 VMEM_LIMIT = 60 * 1024 * 1024
 
 NN = (((1,), (0,)), ((), ()))
@@ -175,6 +176,59 @@
 GATHER_SEMS = [DMA((16, 4)), DMA((16,))]
 
 
+class GatherAll(Gather):
+    def device(self, k):
+        return (1 - self.x, self.s) if k == ACROSS else Gather.device(self, k)
+
+    def copy(self, src, k, own=False, x=None):
+        x = self.x if x is None else x
+        ref = self.own if own else self.at(x, src)
+        return remote(ref, self.at(x, src), self.send.at[x, src, k], self.recv.at[x, src], self.device(k))
+
+    def begin(self):
+        for k in (UP, DOWN, SIDE, ACROSS, CORE):
+            self.go(self.s, k, own=True)
+
+    def line(self, t):
+        for cond, zz, k in self.sides(t):
+            src = seat(zz, self.y, self.c)
+            self.wait(src, cond)
+            for way in (k, SIDE, ACROSS, CORE):
+                self.go(src, way, cond)
+
+    def over(self, t):
+        for cond, zz, _ in self.sides(t):
+            src = seat(zz, 1 - self.y, self.c)
+            self.wait(src, cond)
+            for way in (ACROSS, CORE):
+                self.go(src, way, cond)
+
+    def across(self, t):
+        x = 1 - self.x
+        for cond, zz, _ in self.sides(t):
+            for yy in range(2):
+                src = seat(zz, yy, self.c)
+                if not self.ending:
+                    when(cond, lambda: self.copy(src, SIDE, x=x).wait_recv())
+                act = (lambda c: c.wait_send()) if self.ending else (lambda c: c.start())
+                when(cond, lambda: act(self.copy(src, CORE, x=x)))
+
+    def done(self, t):
+        for cond, zz, _ in self.sides(t):
+            for yy in range(2):
+                src = seat(zz, yy, 1 - self.c)
+                for x in (self.x, 1 - self.x):
+                    when(cond, lambda: self.copy(src, SIDE, x=x).wait_recv())
+
+    def end(self):
+        Gather.end(self)
+        for t in range(4):
+            self.across(t)
+
+
+GATHER_ALL_SEMS = [DMA((2, 16, 5)), DMA((2, 16))]
+
+
 class Exchange:
     def __init__(self, src, dst, send, recv, wide=False):
         self.x, self.s, self.z, self.y, self.c = place()
@@ -197,12 +251,14 @@
         to, me = self.seat(k), self.index((self.x, self.s))
         return remote(self.src(self.index(to)), self.dst(me), self.send.at[k], self.recv.at[k], to)
 
+    def keep(self):
+        me = self.index((self.x, self.s))
+        return pltpu.make_async_copy(self.src(me), self.dst(me), self.recv.at[0])
+
     def begin(self, ks=None):
         for k in range(self.n) if ks is None else ks:
             if k == 0:
-                me = self.index((self.x, self.s))
-                self.local = pltpu.make_async_copy(self.src(me), self.dst(me), self.recv.at[0])
-                self.local.start()
+                self.keep().start()
             else:
                 self.copy(k).start()
 
@@ -212,11 +268,14 @@
         remote(self.src(me), self.dst(self.index(frm)), self.send.at[k], self.recv.at[k], frm).wait_recv()
         return self.index(frm)
 
-    def end(self, arrivals=True):
-        self.local.wait()
+    def end(self):
+        self.keep().wait()
         for k in range(1, self.n):
-            if arrivals:
-                self.arrive(k)
+            self.arrive(k)
+        self.end_sends()
+
+    def end_sends(self):
+        for k in range(1, self.n):
             self.copy(k).wait_send()
 
 
@@ -293,6 +352,125 @@
     return jax.ShapeDtypeStruct(shape, dtype)
 
 
+class Reduce:
+    def __init__(self, part, out, bufs, sems):
+        self.part, self.out = part, out
+        self.r1, self.ra, self.ua, self.da = bufs
+        self.s1, self.q1, self.sa, self.qa, self.su, self.qu, self.sd, self.qd = sems
+        self.x, self.s, self.z, self.y, self.c = place()
+
+    @staticmethod
+    def bufs(rows, width):
+        return [VM((4, 2, rows, width), BF)] + [VM((4, rows, width), BF)] * 3
+
+    SEMS = [DMA((4, 2))] * 8
+
+    def add(self, dst, src):
+        dst[...] = (dst[...].astype(F32) + src[...].astype(F32)).astype(BF)
+
+    def piece(self, p):
+        rows = self.ra.shape[1] // 2
+        return slice(p * rows, p * rows + rows)
+
+    def first(self, zz, yy):
+        return remote(
+            self.part.at[seat(zz, yy, 1 - self.c)],
+            self.r1.at[zz, yy],
+            self.s1.at[zz, yy],
+            self.q1.at[zz, yy],
+            (self.x, seat(self.z, self.y, 1 - self.c)),
+        )
+
+    def side(self, zz, p):
+        part = self.piece(p)
+        return remote(
+            self.r1.at[zz, 1 - self.y, part],
+            self.ra.at[zz, part],
+            self.sa.at[zz, p],
+            self.qa.at[zz, p],
+            (self.x, seat(self.z, 1 - self.y, self.c)),
+        )
+
+    def line(self, zz, p, up):
+        z, y, c = self.z, self.y, self.c
+        src = self.ra.at[zz, self.piece(p)]
+        dst = (self.ua if up else self.da).at[zz, self.piece(p)]
+        send, recv = (self.su, self.qu) if up else (self.sd, self.qd)
+        return remote(src, dst, send.at[zz, p], recv.at[zz, p], (self.x, seat(z + 1 if up else z - 1, y, c)))
+
+    def order(self):
+        z = self.z
+        for t in (3, 2, 1):
+            yield z + t <= 3, z + t, True
+            yield z - t >= 0, z - t, False
+        yield None, z, None
+
+    def begin_plane(self, zz, cond=None):
+        for yy in range(2):
+            when(cond, lambda: self.first(zz, yy).start())
+
+    def begin(self):
+        for cond, zz, _ in self.order():
+            self.begin_plane(zz, cond)
+
+    def fold(self, zz, cond=None):
+        def go():
+            for yy in range(2):
+                self.first(zz, yy).wait_recv()
+                self.add(self.r1.at[zz, yy], self.part.at[seat(zz, yy, self.c)])
+            for p in range(2):
+                self.side(zz, p).start()
+
+        when(cond, go)
+
+    def take(self, zz, p, up):
+        self.line(zz, p, up).wait_recv()
+        part = self.piece(p)
+        self.add(self.ra.at[zz, part], (self.ua if up else self.da).at[zz, part])
+
+    def flow_plane(self, cond, zz, up):
+        z = self.z
+
+        def go():
+            for p in range(2):
+                part = self.piece(p)
+                self.side(zz, p).wait_recv()
+                self.add(self.ra.at[zz, part], self.r1.at[zz, self.y, part])
+                if up is not None:
+                    pl.when(z > 0 if up else z < 3)(lambda: self.take(zz, p, up))
+                    self.line(zz, p, up).start()
+
+        when(cond, go)
+
+    def flow(self):
+        z = self.z
+        for cond, zz, up in self.order():
+            self.flow_plane(cond, zz, up)
+        for up, cond in ((True, z > 0), (False, z < 3)):
+            for p in range(2):
+                when(cond, lambda: self.take(z, p, up))
+        self.out[...] = self.ra[z]
+
+    def run(self):
+        for cond, zz, _ in self.order():
+            self.fold(zz, cond)
+        self.flow()
+
+    def end(self):
+        for cond, zz, up in self.order():
+            for yy in range(2):
+                when(cond, lambda: self.first(zz, yy).wait_send())
+            for p in range(2):
+                when(cond, lambda: self.side(zz, p).wait_send())
+                if up is not None:
+                    when(cond, lambda: self.line(zz, p, up).wait_send())
+
+
+NBUF = 4
+NSEM = 8
+TB = 512
+
+
 def allowed_mask(first_key, first_query, start_row):
     key = first_key + lax.broadcasted_iota(jnp.int32, (QB, QB), 0)
     query = first_query + lax.broadcasted_iota(jnp.int32, (QB, QB), 1)
@@ -302,6 +480,12 @@
 SCORE = math.log2(math.e) / math.sqrt(HEAD_SIZE)
 
 
+def as_row(col):
+    n = col.shape[0]
+    same = lax.broadcasted_iota(jnp.int32, (n, n), 0) == lax.broadcasted_iota(jnp.int32, (n, n), 1)
+    return jnp.sum(jnp.where(same, jnp.broadcast_to(col, (n, n)), 0.0), axis=0, keepdims=True)
+
+
 def column(line):
     n = line.shape[1]
     same = lax.broadcasted_iota(jnp.int32, (n, n), 0) == lax.broadcasted_iota(jnp.int32, (n, n), 1)
@@ -310,19 +494,24 @@
 
 def front(
     tok, query_w, key_w, value_w, out_w, router_w, gate_w, up_w, down_w, gain_a, gain_e, seg, routes, cot, rope, freq,
-    hid, wexp, wo_all, cot_all, q_t, k_t, v_t, o_t, lse, start, cos, sin,
-    residual, normed, scale_out, h2, att, probs, picked, p_t, wperm,
-    wo, w3, spread, seg_mine, tok_all, w_mine, seg_all, o_low, att_t, k_n, w_t, hid_v, wo_v,
-    t_send, t_recv, o_send, o_recv, c_send, c_recv, w_send, w_recv, g_send, g_recv,
-    a_send, a_recv, e_send, e_recv, x_send, x_recv, x_sem,
+    hid, wo_all, mixp, q_t, k_t, v_t, o_t, lse, start, cos, sin,
+    residual, normed, scale_out, h2, att, probs, picked, wperm, back, g_all, dw,
+    wo, w3, spread, seg_mine, row_all, w_mine, seg_all, o_low, att_t, k_n, w_t, wo_v,
+    wexp, cot_all, p_t, p_all, backp, mix_v, gg, acc,
+    *rest,
 ):
+    bufs, sems = rest[:NBUF], rest[NBUF:]
+    (
+        t_send, t_recv, o_send, o_recv, c_send, c_recv, h_send, h_recv, w_send, w_recv, g_send, g_recv,
+        a_send, a_recv, e_send, e_recv, x_send, x_recv, p_send, p_recv, y_send, y_recv, x_sem,
+    ) = sems[NSEM:]
     x, s, z, y, c = place()
     rows, width = tok.shape
-    length = hid.shape[0]
+    length = 16 * rows
     barrier_all()
-    tokens = Gather(tok, lambda src: tok_all.at[src], t_send, t_recv)
+    tokens = Gather(tok, lambda src: row_all.at[src], t_send, t_recv)
     tokens.begin()
-    keep_tok = pltpu.make_async_copy(tok, tok_all.at[s], x_sem.at[2])
+    keep_tok = pltpu.make_async_copy(tok, row_all.at[s], x_sem.at[2])
     keep_tok.start()
     seg_mine[...] = jnp.broadcast_to(seg[...], seg_mine.shape)
     documents = Exchange(lambda r: seg_mine, lambda r: seg_all.at[r], g_send, g_recv)
@@ -336,10 +525,10 @@
     slices.begin()
     by_second = column(gain_e[...])
     wo[:, 0:width] = out_w[...]
-    router = (router_w[...].astype(F32) * by_second).astype(F32)
-    wo[:, width : width + 128] = jnp.concatenate([router, jnp.zeros((32, 128 - E), F32)], axis=1).astype(BF)
-    over = remote(wo, wo_v.at[x, s], x_sem.at[0], x_sem.at[1], (1 - x, s))
-    over.start()
+    router = router_w[...].astype(F32) * gain_e[...].astype(F32)
+    router = jnp.concatenate([jnp.concatenate([router, jnp.zeros((128 - E, 32), F32)], axis=0), jnp.zeros((128, 96), F32)], axis=1)
+    wo[:, width : width + 128] = jnp.transpose(router)[0:32].astype(BF)
+    outw = GatherAll(wo, lambda x, src: wo_v.at[x, src], o_send, o_recv)
     keep = pltpu.make_async_copy(wo, wo_v.at[x, s], x_sem.at[3])
     keep.start()
     for m, ref in enumerate((gate_w, up_w, down_w)):
@@ -351,7 +540,8 @@
                 part = spread[b, pl.ds(e, 32, stride=E), :]
                 w3[e, m, :, lanes] = (part * by_second if m < 2 else part).astype(BF)
     weights = Exchange(lambda e: w3.at[e], lambda r: wexp.at[:, x * 16 + r], e_send, e_recv)
-    weights.begin(range(4))
+    cots = Gather(cot, lambda src: cot_all.at[src], c_send, c_recv)
+
     def cross(k, begin=True):
         row = weights.index(weights.seat(k, back=True))
         if begin and k:
@@ -375,18 +565,17 @@
     slices.share()
     tokens.over(1)
     tokens.line(2)
-    keep.wait()
-    remote(wo, wo_v.at[1 - x, s], x_sem.at[0], x_sem.at[1], (1 - x, s)).wait_recv()
-    outw = Gather(None, lambda src: wo_v.at[:, src], o_send, o_recv)
     outw.begin()
-    for k in range(4):
-        cross(k)
+    weights.begin(range(8))
     slices.end()
     w_t[...] = jnp.transpose(w_mine[...].reshape(width, 256).astype(F32)).astype(BF)
     tokens.over(2)
     tokens.line(3)
     outw.over(0)
     outw.line(1)
+    weights.begin(range(8, 12))
+    for k in range(4):
+        cross(k)
     documents.end()
     numbers = seg_all[:, 0, :]
     ends = [jnp.sum((numbers < n).astype(jnp.int32)) for n in (1, 2)]
@@ -394,19 +583,18 @@
         line = numbers[b : b + 1]
         start[:, b * 128 : b * 128 + 128] = jnp.where(line == 0, 0, jnp.where(line == 1, ends[0], ends[1]))
     tokens.over(3)
-    outw.over(1)
-    outw.line(2)
-    weights.begin(range(4, 8))
     for t in range(4):
         tokens.done(t)
     keep_tok.wait()
+    tokens.end()
+    acc[...] = jnp.zeros(acc.shape, F32)
 
     def project(i, _):
         cols = lane_block(i, 512)
-        values = tok_all[pl.ds(i * 4, 4)].reshape(512, width).astype(F32)
+        values = row_all[pl.ds(i * 4, 4)].reshape(512, width).astype(F32)
         scale = lax.rsqrt(jnp.mean(values * values, axis=-1, keepdims=True) + EPSILON)
         hidden = (values * scale).astype(BF)
-        hid_v[cols, :] = hidden
+        row_all[pl.ds(i * 4, 4)] = hidden.reshape(4, rows, width)
         made = dot(w_t[...], hidden, NT)
         co, si = cos[:, cols], sin[:, cols]
         own = jnp.where(c == 0, made[0:64], made[64:128])
@@ -419,13 +607,30 @@
         return 0
 
     lax.fori_loop(0, length // 512, project, 0)
-    keep_hid = pltpu.make_async_copy(hid_v, hid, x_sem.at[4])
+    keep_hid = pltpu.make_async_copy(row_all, hid, x_sem.at[4])
     keep_hid.start()
-    outw.over(2)
-    outw.line(3)
-    weights.begin(range(8, 12))
 
     def query_block(i, _):
+        @pl.when(i == 2)
+        def _():
+            outw.over(1)
+            outw.line(2)
+
+        @pl.when(i == 5)
+        def _():
+            outw.over(2)
+            outw.line(3)
+            for k in range(4, 8):
+                cross(k)
+
+        @pl.when(i == 6)
+        def _():
+            cots.begin()
+
+        @pl.when(i == 7)
+        def _():
+            outw.over(3)
+
         cols = lane_block(i)
         queries = q_t[:, cols]
         begin = start[:, cols]
@@ -454,29 +659,26 @@
         lse[:, cols] = top + jnp.log2(total)
         return 0
 
-    blocks = length // QB
-    cut = (5 * blocks) // 8
-    lax.fori_loop(0, cut, query_block, 0)
-    outw.over(3)
-    for k in range(4, 8):
-        cross(k)
-    lax.fori_loop(cut, blocks, query_block, 0)
+    lax.fori_loop(0, length // QB, query_block, 0)
+    keep_hid.wait()
     heads = Exchange(lambda t: o_low.at[:, lane_block(t, 128)], lambda h: att_t.at[h], a_send, a_recv)
     heads.begin()
-    weights.begin(range(12, 16))
-    cots = Gather(cot, lambda src: cot_all.at[src], c_send, c_recv)
-    cots.begin()
     keep_cot = pltpu.make_async_copy(cot, cot_all.at[s], x_sem.at[6])
     keep_cot.start()
+    cots.over(0)
+    cots.line(1)
+    for t in range(4):
+        outw.across(t)
     for t in range(4):
         outw.done(t)
+    keep.wait()
     keep_wo = pltpu.make_async_copy(wo_v, wo_all, x_sem.at[5])
     keep_wo.start()
+    weights.begin(range(12, 16))
+    heads.end()
+    cots.over(1)
     for k in range(8, 12):
         cross(k)
-    heads.end()
-    cots.over(0)
-    cots.line(1)
 
     att[...] = jnp.transpose(att_t[...].reshape(width, rows).astype(F32)).astype(BF)
     res = tok[...].astype(F32) + dot(att[...], wo_v[:, :, :, 0:width].reshape(width, width), NT)
@@ -493,213 +695,75 @@
     powers = jnp.exp(logits - top)
     prob = powers / jnp.sum(powers, axis=-1, keepdims=True)
     probs[...] = prob
+    names = lax.broadcasted_iota(jnp.int32, (128, 128), 0)
     mask = jnp.zeros((128, 128), F32)
     for k in range(K):
-        mask = mask + jnp.where(lanes == routes[:, k : k + 1], 1.0, 0.0)
+        mask = mask + jnp.where(names == routes[k : k + 1, :], 1.0, 0.0)
+    mask = jnp.transpose(mask)
     picked[...] = mask
     p_t[...] = jnp.transpose(prob * mask)[0:E, :]
 
-    cots.over(1)
-    cots.line(2)
-    for k in range(12, 16):
-        cross(k)
-    cots.over(2)
-    cots.line(3)
-    cots.over(3)
-    for t in range(4):
-        cots.done(t)
-    weights.end(arrivals=False)
-    for k in range(16):
-        cross(k, begin=False)
-    for g in (tokens, outw, cots):
-        g.end()
-    over.wait_send()
-    for copy in (keep_hid, keep_wo, keep_cot):
-        copy.wait()
-
-
-class Reduce:
-    def __init__(self, part, out, bufs, sems):
-        self.part, self.out = part, out
-        self.r1, self.ra, self.ua, self.da = bufs
-        self.s1, self.q1, self.sa, self.qa, self.su, self.qu, self.sd, self.qd = sems
-        self.x, self.s, self.z, self.y, self.c = place()
-
-    @staticmethod
-    def bufs(rows, width):
-        return [VM((4, 2, rows, width), BF)] + [VM((4, rows, width), BF)] * 3
-
-    SEMS = [DMA((4, 2))] * 2 + [DMA((4,))] * 6
-
-    def add(self, dst, src):
-        dst[...] = (dst[...].astype(F32) + src[...].astype(F32)).astype(BF)
-
-    def first(self, zz, yy):
-        return remote(
-            self.part.at[seat(zz, yy, 1 - self.c)],
-            self.r1.at[zz, yy],
-            self.s1.at[zz, yy],
-            self.q1.at[zz, yy],
-            (self.x, seat(self.z, self.y, 1 - self.c)),
-        )
-
-    def side(self, zz):
-        return remote(
-            self.r1.at[zz, 1 - self.y],
-            self.ra.at[zz],
-            self.sa.at[zz],
-            self.qa.at[zz],
-            (self.x, seat(self.z, 1 - self.y, self.c)),
-        )
-
-    def line(self, zz, up):
-        z, y, c = self.z, self.y, self.c
-        if up:
-            return remote(self.ra.at[zz], self.ua.at[zz], self.su.at[zz], self.qu.at[zz], (self.x, seat(z + 1, y, c)))
-        return remote(self.ra.at[zz], self.da.at[zz], self.sd.at[zz], self.qd.at[zz], (self.x, seat(z - 1, y, c)))
-
-    def order(self):
-        z = self.z
-        for t in (3, 2, 1):
-            yield z + t <= 3, z + t, True
-            yield z - t >= 0, z - t, False
-        yield None, z, None
-
-    def begin_plane(self, zz, cond=None):
-        for yy in range(2):
-            when(cond, lambda: self.first(zz, yy).start())
-
-    def begin(self):
-        for cond, zz, _ in self.order():
-            self.begin_plane(zz, cond)
-
-    def fold(self, zz, cond=None):
-        def go():
-            for yy in range(2):
-                self.first(zz, yy).wait_recv()
-                self.add(self.r1.at[zz, yy], self.part.at[seat(zz, yy, self.c)])
-            self.side(zz).start()
-
-        when(cond, go)
-
-    def flow(self):
-        z = self.z
-        for cond, zz, up in self.order():
-
-            def go():
-                self.side(zz).wait_recv()
-                self.add(self.ra.at[zz], self.r1.at[zz, self.y])
-                if up is None:
-                    return
-
-                def take():
-                    self.line(zz, up).wait_recv()
-                    self.add(self.ra.at[zz], (self.ua if up else self.da).at[zz])
-
-                pl.when(z > 0 if up else z < 3)(take)
-                self.line(zz, up).start()
-
-            when(cond, go)
-        for up, cond in ((True, z > 0), (False, z < 3)):
-
-            def take():
-                self.line(z, up).wait_recv()
-                self.add(self.ra.at[z], (self.ua if up else self.da).at[z])
-
-            when(cond, take)
-        self.out[...] = self.ra[z]
-
-    def run(self):
-        for cond, zz, _ in self.order():
-            self.fold(zz, cond)
-        self.flow()
-
-    def end(self):
-        for cond, zz, up in self.order():
-            for yy in range(2):
-                when(cond, lambda: self.first(zz, yy).wait_send())
-            when(cond, lambda: self.side(zz).wait_send())
-            if up is not None:
-                when(cond, lambda: self.line(zz, up).wait_send())
-
-
-NBUF = 4
-NSEM = 8
-TB = 512
-
-
-def middle(
-    h2, p_t, cot_in, wexp_in, residual,
-    back, mixed, g_all, dwx,
-    h_all, p_all, cot, wexp, backp, mixp, mix, gg, dw, acc,
-    *rest,
-):
-    bufs_a, bufs_b = rest[:NBUF], rest[NBUF : 2 * NBUF]
-    sems = rest[2 * NBUF :]
-    h_send, h_recv, p_send, p_recv, g_send, g_recv, x_sem = sems[2 * NSEM :]
-    x, s, z, y, c = place()
-    loads = [
-        pltpu.make_async_copy(wexp_in, wexp, x_sem.at[2]),
-        pltpu.make_async_copy(cot_in, cot, x_sem.at[3]),
-    ]
-    for copy in loads:
-        copy.start()
-    barrier_row(partner=True)
-    hidden = Gather(h2, lambda src: h_all.at[src], h_send, h_recv)
+    hidden = Gather(h2, lambda src: row_all.at[src], h_send, h_recv)
     hidden.begin()
-    keep = pltpu.make_async_copy(h2, h_all.at[s], x_sem.at[4])
+    keep = pltpu.make_async_copy(h2, row_all.at[s], x_sem.at[8])
     keep.start()
     minor = Exchange(lambda r: p_t, lambda r: p_all.at[r], p_send, p_recv)
     minor.begin()
-    one = Reduce(backp, back, bufs_a, sems[:NSEM])
-    two = Reduce(mixp, mix, bufs_b, sems[NSEM : 2 * NSEM])
-    acc[...] = jnp.zeros(acc.shape, F32)
+    one = Reduce(backp, back, bufs, sems[:NSEM])
+    cots.line(2)
     hidden.over(0)
     keep.wait()
+    keep_cot.wait()
+    for k in range(12, 16):
+        cross(k)
     minor.end()
-    for copy in loads:
-        copy.wait()
+    hidden.line(1)
+    weights.keep().wait()
+    for k in range(16):
+        cross(k, begin=False)
+    cots.done(0)
     hidden.done(0)
-    hidden.line(1)
     far = z // 2
     order = (z, z + 1 - 2 * far, 2 - 2 * z + 5 * far, 3 - 3 * far)
-    width = h2.shape[1]
-    rows = h2.shape[0]
 
     def chunk(i, _):
         zz = jnp.where(i == 0, order[0], jnp.where(i == 1, order[1], jnp.where(i == 2, order[2], order[3])))
 
+        for t in (1, 2, 3):
+
+            @pl.when(i == t)
+            def _():
+                cots.done(t)
+                hidden.done(t)
+
+        four = pl.ds(zz * 4, 4)
+        some = row_all[four].reshape(4 * rows, width)
+        grad = cot_all[four].reshape(4 * rows, width)
+        cols = [jnp.broadcast_to(p_all[zz * 4 + b, pl.ds(s, 1), :], (128, 128)) for b in range(4)]
+        prob = jnp.concatenate([jnp.transpose(v)[:, 0:1] for v in cols], axis=0)
+        gate = dot(some, wexp[0].reshape(width, F))
+        up = dot(some, wexp[1].reshape(width, F))
+
+        @pl.when(i == 0)
+        def _():
+            hidden.over(1)
+            hidden.line(2)
+
         @pl.when(i == 1)
         def _():
-            hidden.over(1)
-            hidden.done(1)
-            hidden.line(2)
-            one.fold(order[0])
+            hidden.over(2)
+            hidden.line(3)
 
         @pl.when(i == 2)
         def _():
-            hidden.over(2)
-            hidden.done(2)
-            hidden.line(3)
+            one.fold(order[0])
             one.fold(order[1])
-
-        @pl.when(i == 3)
-        def _():
             hidden.over(3)
-            hidden.done(3)
-            one.fold(order[2])
-
-        four = pl.ds(zz * 4, 4)
-        some = h_all[four].reshape(4 * rows, width)
-        grad = cot[four].reshape(4 * rows, width)
-        cols = [jnp.broadcast_to(p_all[zz * 4 + b, pl.ds(s, 1), :], (128, 128)) for b in range(4)]
-        prob = jnp.concatenate([jnp.transpose(v)[:, 0:1] for v in cols], axis=0)
-        gate = dot(some, wexp[0])
-        up = dot(some, wexp[1])
+
         sig = 1.0 / (1.0 + jnp.exp(-gate))
         silu = gate * sig
         low = (silu * up).astype(BF)
-        moved = dot(grad, wexp[2])
+        moved = dot(grad, wexp[2].reshape(width, F))
         seen = jnp.sum(low.astype(F32) * moved, axis=-1, keepdims=True)
         for b in range(4):
             line = jnp.transpose(jnp.broadcast_to(seen[b * 128 : b * 128 + 128], (128, 128)))[0:8]
@@ -707,53 +771,99 @@
         grad_hidden = moved * prob
         grad_gate = (grad_hidden * up * (sig * (1.0 + gate * (1.0 - sig)))).astype(BF)
         grad_up = (grad_hidden * silu).astype(BF)
-        below = dot(grad_gate, wexp[0], NT) + dot(grad_up, wexp[1], NT)
+        below = dot(grad_gate, wexp[0].reshape(width, F), NT) + dot(
+            grad_up, wexp[1].reshape(width, F), NT
+        )
         backp[four] = below.astype(BF).reshape(4, rows, width)
         one.begin_plane(zz)
-        out = dot(low, wexp[2], NT)
-        mixp[four] = (prob * out).astype(BF).reshape(4, rows, width)
-        two.begin_plane(zz)
+
+        @pl.when(i == 0)
+        def _():
+            cots.over(2)
+
+        @pl.when(i == 3)
+        def _():
+            one.fold(order[2])
+
+        out = dot(low, wexp[2].reshape(width, F), NT)
+        keep_mix = pltpu.make_async_copy(mix_v, mixp.at[four], x_sem.at[7])
+        pl.when(i > 0)(lambda: keep_mix.wait())
+        mix_v[...] = (prob * out).astype(BF).reshape(4, rows, width)
+        keep_mix.start()
         acc[0] += dot(some, grad_gate, TN)
         acc[1] += dot(some, grad_up, TN)
         acc[2] += dot(grad, (prob * low.astype(F32)).astype(BF), TN)
+
+        @pl.when(i == 0)
+        def _():
+            cots.line(3)
+
+        @pl.when(i == 1)
+        def _():
+            cots.over(3)
+
         return 0
 
     lax.fori_loop(0, 4, chunk, 0)
     one.fold(order[3])
-    seen_out = Exchange(lambda r: gg.at[r], lambda r: g_all.at[r], g_send, g_recv)
+    seen_out = Exchange(lambda r: gg.at[r], lambda r: g_all.at[r], y_send, y_recv)
     seen_out.begin()
     dw[...] = acc[...].astype(BF).reshape(dw.shape)
-    over = remote(dw.at[:, 1 - x], dwx, x_sem.at[0], x_sem.at[1], (1 - x, s))
-    over.start()
     one.flow()
-    two.run()
-    mixed[...] = (residual[...] + mix[...].astype(F32)).astype(BF)
-    hidden.end()
+    weights.end_sends()
+    for g in (outw, cots, hidden):
+        g.end()
+    keep_wo.wait()
+    pltpu.make_async_copy(mix_v, mixp.at[pl.ds(0, 4)], x_sem.at[7]).wait()
     seen_out.end()
     one.end()
-    two.end()
-    over.wait()
-    dwx[...] = (dwx[...].astype(F32) + dw[:, x].astype(F32)).astype(BF)
 
 
 def rear(
-    back, g_all, cot, probs, picked, normed, scale, wo, att, h2, dwx, q_t, k_t, v_t, lse, o_t, start, hid, cos, sin,
+    back, g_all, cot, probs, picked, normed, scale, wo, att, h2, dw, mixp, q_t, k_t, v_t, lse, o_t, start, hid_in, cos, sin,
     wperm, tok,
-    grad_tokens, dw_all, dwo_sum, wg_all,
-    g_res, ga_t, dwo, dwo_x, go_t, gq_t, gkv, k_n, v_n, delta, got, g_t, wg, g_mine, wp,
+    grad_tokens, dw_all, dwo_sum, wg_all, mix,
+    g_res, ga_t, dwo, dwo_x, go_t, gq_t, gkv, k_n, v_n, delta, got, g_t, wg, g_mine, wp, hid, dwx,
     *rest,
 ):
-    bufs = rest[:NBUF]
-    sems = rest[NBUF:]
-    a_send, a_recv, w_send, w_recv, b_send, b_recv, v_send, v_recv, p_send, p_recv, x_sem = sems[NSEM:]
+    bufs, bufs_b = rest[:NBUF], rest[NBUF : 2 * NBUF]
+    sems = rest[2 * NBUF :]
+    (
+        a_send, a_recv, b_send, b_recv, w0s, w0r, w1s, w1r, w2s, w2r, v_send, v_recv, p_send, p_recv, d_sem, x_sem,
+    ) = sems[2 * NSEM :]
     x, s, z, y, c = place()
     width = att.shape[1]
-    length = hid.shape[0]
+    length = q_t.shape[1]
     barrier_all()
-    over_w = remote(wperm, wp.at[x, s], x_sem.at[4], x_sem.at[5], (1 - x, s))
-    over_w.start()
-    keep_w = pltpu.make_async_copy(wperm, wp.at[x, s], x_sem.at[6])
-    keep_w.start()
+    two = Reduce(mixp, mix, bufs_b, sems[NSEM : 2 * NSEM])
+    two.begin()
+    columns_all = GatherAll(wperm, lambda x, src: wp.at[x, src], p_send, p_recv)
+    columns_all.begin()
+    loads = [
+        pltpu.make_async_copy(wperm, wp.at[x, s], x_sem.at[6]),
+        pltpu.make_async_copy(hid_in, hid, x_sem.at[4]),
+    ]
+    for copy in loads:
+        copy.start()
+    owners = [
+        Exchange(
+            lambda r, m=m: dwx.at[m, r],
+            lambda e, m=m: dw_all.at[e, m],
+            (w0s, w1s, w2s)[m],
+            (w0r, w1r, w2r)[m],
+        )
+        for m in range(3)
+    ]
+
+    def over_d(m):
+        return remote(dw.at[m, 1 - x], dwx.at[m], d_sem.at[0, m], d_sem.at[1, m], (1 - x, s))
+
+    def to_owners(m):
+        over_d(m).wait()
+        dwx[m] = (dwx[m].astype(F32) + dw[m, x].astype(F32)).astype(BF)
+        owners[m].begin()
+
+    over_d(0).start()
 
     seen = jnp.concatenate([g_all[e, 0:1, :] for e in range(E)] + [jnp.zeros((128 - E, 128), F32)], axis=0)
     grad_probs = jnp.transpose(seen) * picked[...]
@@ -767,23 +877,25 @@
     ga_t[...] = jnp.transpose(dot(branch, wo[:, 0:width])).astype(BF).reshape(ga_t.shape)
     heads = Exchange(lambda h: ga_t.at[h], lambda t: go_t.at[:, lane_block(t, 128)], a_send, a_recv)
     heads.begin()
+    over_d(1).start()
+    over_d(2).start()
+    for cond, zz, _ in two.order():
+        two.fold(zz, cond)
     dwo[:, :, :, 0:width] = dot(jnp.transpose(grad).astype(BF), att[...]).astype(BF).reshape(2, 16, 32, width)
     dwo[:, :, :, width : width + 128] = dot(h2[...], grad_logits, TN).astype(BF).reshape(2, 16, 32, 128)
     over_o = remote(dwo.at[1 - x], dwo_x, x_sem.at[0], x_sem.at[1], (1 - x, s))
     over_o.start()
+    to_owners(0)
     k_n[...] = jnp.transpose(k_t[...].astype(F32)).astype(BF)
     v_n[...] = jnp.transpose(v_t[...].astype(F32)).astype(BF)
     gkv[...] = jnp.zeros(gkv.shape, F32)
-    weights = Exchange(lambda r: dwx.at[:, r], lambda e: dw_all.at[e], w_send, w_recv)
+    columns_all.over(0)
     heads.end()
-    keep_w.wait()
-    remote(wperm, wp.at[1 - x, s], x_sem.at[4], x_sem.at[5], (1 - x, s)).wait_recv()
-    columns_all = Gather(None, lambda src: wp.at[:, src], p_send, p_recv)
-    columns_all.begin()
-    weights.begin(range(8))
+    columns_all.line(1)
     delta[...] = jnp.sum(go_t[...].astype(F32) * o_t[...], axis=0, keepdims=True)
 
     def query_block(i, _):
+        pl.when(i == 4)(lambda: to_owners(1))
         cols = lane_block(i)
         queries, grads = q_t[:, cols], go_t[:, cols]
         begin, log_total, shift = start[:, cols], lse[:, cols], delta[:, cols]
@@ -801,24 +913,16 @@
         gq_t[:, cols] = lax.fori_loop(0, i + 1, key_block, jnp.zeros((HEAD_SIZE, QB), F32))
         return 0
 
-    blocks = length // QB
-    cut = (5 * blocks) // 8
-    lax.fori_loop(0, cut, query_block, 0)
-    columns_all.over(0)
-    columns_all.line(1)
-    over_o.wait_recv()
-    dwo_x[...] = (dwo_x[...].astype(F32) + dwo[x].astype(F32)).astype(BF)
-    out = Reduce(dwo_x, dwo_sum, bufs, sems[:NSEM])
-    out.begin()
-    weights.begin(range(8, 16))
-    lax.fori_loop(cut, blocks, query_block, 0)
+    lax.fori_loop(0, length // QB, query_block, 0)
+    columns_all.over(1)
+    columns_all.line(2)
+    two.flow()
 
     pair = remote(gkv.at[1 - c], got, x_sem.at[2], x_sem.at[3], (x, seat(z, y, 1 - c)))
     pair.start()
-    columns_all.over(1)
-    columns_all.line(2)
-    for cond, zz, _ in out.order():
-        out.fold(zz, cond)
+    columns_all.over(2)
+    columns_all.line(3)
+    columns_all.over(3)
     scaling = 1.0 / math.sqrt(HEAD_SIZE)
     co, si = cos[...], sin[...]
 
@@ -834,27 +938,78 @@
         lambda t: g_t.at[:, :, lane_block(t, 128)], lambda h: g_mine.at[h // 2, :, h % 2], b_send, b_recv
     )
     tokens.begin()
+    loads[1].wait()
     wg[...] = jnp.transpose(dot(g_t[...].reshape(128, length), hid[...])).astype(BF).reshape(wg.shape)
     columns = Exchange(lambda r: wg.at[r], lambda r: wg_all.at[r], v_send, v_recv, wide=True)
     columns.begin()
-    columns_all.over(2)
-    columns_all.line(3)
-    columns_all.over(3)
+    over_o.wait_recv()
+    dwo_x[...] = (dwo_x[...].astype(F32) + dwo[x].astype(F32)).astype(BF)
+    out = Reduce(dwo_x, dwo_sum, bufs, sems[:NSEM])
+    out.begin()
+    out.run()
+    for t in range(4):
+        columns_all.across(t)
+    tokens.end()
     for t in range(4):
         columns_all.done(t)
-    tokens.end()
+    loads[0].wait()
     w = jnp.transpose(dot(wp[...].reshape(width, 2 * width), g_mine[...].reshape(2 * width, 128)))
     values = tok[...].astype(F32)
     scale_first = lax.rsqrt(jnp.mean(values * values, axis=-1, keepdims=True) + EPSILON)
     norm = values * scale_first
     grad_tokens[...] = g_res[...] + scale_first * (w - norm * jnp.mean(w * norm, axis=-1, keepdims=True))
-    out.flow()
+    to_owners(2)
     out.end()
     columns.end()
-    weights.end()
+    for m in range(3):
+        owners[m].end()
     over_o.wait_send()
-    over_w.wait_send()
+    two.end()
     columns_all.end()
+
+
+def finish(
+    wg_all, dwo_sum, dw_all, query_w, key_w, value_w, router_w, gate_w, up_w, gain_a, gain_e, mix, residual, g_tok,
+    mixed, grad_tokens, grad_a, grad_e, grad_q, grad_k, grad_v, grad_o, grad_r, grad_gate, grad_up, grad_down,
+    spread,
+):
+    width = grad_o.shape[1]
+    mixed[...] = (residual[...] + mix[...].astype(F32)).astype(BF)
+    grad_tokens[...] = g_tok[...]
+    by_first, by_second = column(gain_a[...]), column(gain_e[...])
+    head = [wg_all[h].astype(F32) + wg_all[16 + h].astype(F32) for h in range(16)]
+    total = jnp.zeros((32, 128), F32)
+    for ref, weight, lanes, seats in (
+        (grad_q, query_w, slice(0, 64), range(16)),
+        (grad_k, key_w, slice(64, 128), range(0, 16, 2)),
+        (grad_v, value_w, slice(64, 128), range(1, 16, 2)),
+    ):
+        for j in range(len(seats) // 2):
+            part = jnp.concatenate([head[seats[2 * j]][:, lanes], head[seats[2 * j + 1]][:, lanes]], axis=1)
+            cols = slice(128 * j, 128 * j + 128)
+            ref[:, cols] = part * by_first
+            total = total + part * weight[:, cols].astype(F32)
+    grad_a[...] = as_row(jnp.sum(total, axis=1, keepdims=True))
+    grad_o[...] = dwo_sum[:, 0:width].astype(F32)
+    router = dwo_sum[:, width : width + 128].astype(F32)
+    router = jnp.concatenate([router, jnp.zeros((96, 128), F32)], axis=0)
+    router = jnp.transpose(router)[0:E, 0:32]
+    grad_r[...] = router * gain_e[...].astype(F32)
+    total = jnp.zeros((32 * E, 128), F32)
+    for m, (ref, weight) in enumerate(((grad_gate, gate_w), (grad_up, up_w), (grad_down, None))):
+        for b in range(F // 128):
+            lanes = slice(b * 128, b * 128 + 128)
+            for e in range(E):
+                part = dw_all[e, m, :, lanes].astype(F32)
+                spread[b, pl.ds(e, 32, stride=E), :] = part
+            plain = spread[b]
+            if m == 2:
+                ref[:, :, lanes] = plain.reshape(32, E, 128)
+            else:
+                ref[:, :, lanes] = plain.reshape(32, E, 128) * by_second[:, :, None]
+                total = total + plain * weight[:, :, lanes].astype(F32).reshape(32 * E, 128)
+    sums = jnp.sum(jnp.sum(total.reshape(32, E, 128), axis=1), axis=1, keepdims=True)
+    grad_e[...] = as_row(sums) + jnp.sum(router * router_w[...].astype(F32), axis=0, keepdims=True)
 
 
 def frequencies(head_dim):
@@ -882,40 +1037,41 @@
     D = MODEL_WIDTH
     rows = tokens.shape[1]
     length = 16 * rows
-    gain_first, gain_second = attention_gain.astype(F32)[:, None], expert_gain.astype(F32)[:, None]
     tok_mine = tokens.reshape(rows, D)
     cot_mine = cotangent.reshape(rows, D)
-    freq = jnp.broadcast_to(frequencies(HEAD_SIZE)[:, None], (32, 128))
+    powers = np.power(np.float32(ROPE_BASE), -np.arange(32, dtype=np.float32) * np.float32(2.0 / HEAD_SIZE))
+    freq = jnp.asarray(np.broadcast_to(powers[:, None], (32, 128)).astype(np.float32))
     (
-        hid, wexp, wo_all, cot_all, q_t, k_t, v_t, o_t, lse, start, cos, sin,
-        residual, normed, scale, h2, att, probs, picked, p_t, wperm,
+        hid, wo_all, mixp, q_t, k_t, v_t, o_t, lse, start, cos, sin,
+        residual, normed, scale, h2, att, probs, picked, wperm, back, g_all, dw,
     ) = comm_call(
         front,
-        [sds((length, D), BF), sds((3, 32, 32, F), BF), sds((2, 16, 32, D + 128), BF), sds((16, rows, D), BF)]
+        [sds((16, rows, D), BF), sds((2, 16, 32, D + 128), BF), sds((16, rows, D), BF)]
         + [sds((64, length), BF)] * 3
         + [sds((64, length), F32), sds((1, length), F32), sds((1, length), jnp.int32)]
         + [sds((32, length), F32)] * 2
         + [sds((rows, D), F32), sds((rows, D), F32), sds((rows, 128), F32), sds((rows, D), BF), sds((rows, D), BF)]
-        + [sds((rows, 128), F32), sds((rows, 128), F32), sds((E, rows), F32), sds((32, 2 * D), BF)],
+        + [sds((rows, 128), F32), sds((rows, 128), F32), sds((32, 2 * D), BF)]
+        + [sds((rows, D), BF), sds((16, 8, rows), F32), sds((3, 2, 16, 32, F), BF)],
         [
             tok_mine,
             query_weight,
             key_matrix,
             value_matrix,
             output_weight,
-            router_weight,
+            router_weight.T,
             gate_weight,
             up_weight,
             down_weight,
             attention_gain.reshape(1, 32),
             expert_gain.reshape(1, 32),
             segments.astype(jnp.int32),
-            routes.reshape(rows, K),
+            routes.reshape(rows, K).T,
             cot_mine,
             rope_index.astype(jnp.int32),
             freq,
         ],
-        GATHER_SEMS * 3 + [DMA((16,))] * 10 + [DMA((8,))],
+        Reduce.SEMS + GATHER_SEMS + GATHER_ALL_SEMS + GATHER_SEMS * 2 + [DMA((16,))] * 14 + [DMA((12,))],
         0,
         [
             VM((32, D + 128), BF),
@@ -929,38 +1085,26 @@
             VM((16, 64, rows), BF),
             VM((length, 64), BF),
             VM((256, D), BF),
-            VM((length, D), BF),
             VM((2, 16, 32, D + 128), BF),
-        ],
-        [ANY] * 4 + [VM] * 17,
-        [VM] * 14 + [SM, VM],
-    )
-    wo_all = wo_all.reshape(D, D + 128)
-    back, mixed, g_all, dwx = comm_call(
-        middle,
-        [sds((rows, D), BF), sds((rows, D), BF), sds((16, 8, rows), F32), sds((3, 16, 32, F), BF)],
-        [h2, p_t, cot_all, wexp.reshape(3, D, F), residual],
-        Reduce.SEMS * 2 + GATHER_SEMS + [DMA((16,))] * 4 + [DMA((8,))],
-        1,
-        [
+            VM((3, 32, 32, F), BF),
             VM((16, rows, D), BF),
+            VM((E, rows), F32),
             VM((16, E, rows), F32),
             VM((16, rows, D), BF),
-            VM((3, D, F), BF),
-            VM((16, rows, D), BF),
-            VM((16, rows, D), BF),
-            VM((rows, D), BF),
+            VM((4, rows, D), BF),
             VM((16, 8, rows), F32),
-            VM((3, 2, 16, 32, F), BF),
             VM((3, D, F), F32),
         ]
-        + Reduce.bufs(rows, D) * 2,
-        None,
-        [VM, VM, ANY, ANY, VM],
-    )
-    grad_tokens, dw_all, dwo_sum, wg_all = comm_call(
+        + Reduce.bufs(rows, D),
+        [ANY] * 3 + [VM] * 19,
+        [VM] * 14 + [SM, VM],
+    )
+    wo_all = wo_all.reshape(D, D + 128)
+    hid = hid.reshape(length, D)
+    grad_tokens, dw_all, dwo_sum, wg_all, mix = comm_call(
         rear,
-        [sds((rows, D), F32), sds((16, 3, 32, F), BF), sds((32, D + 128), BF), sds((32, 32, 128), BF)],
+        [sds((rows, D), F32), sds((16, 3, 32, F), BF), sds((32, D + 128), BF), sds((32, 32, 128), BF)]
+        + [sds((rows, D), BF)],
         [
             back,
             g_all,
@@ -972,7 +1116,8 @@
             wo_all,
             att,
             h2,
-            dwx,
+            dw,
+            mixp,
             q_t,
             k_t,
             v_t,
@@ -985,7 +1130,7 @@
             wperm,
             tok_mine,
         ],
-        Reduce.SEMS + [DMA((16,))] * 6 + [DMA((32,))] * 2 + GATHER_SEMS + [DMA((8,))],
+        Reduce.SEMS * 2 + [DMA((16,))] * 10 + [DMA((32,))] * 2 + GATHER_ALL_SEMS + [DMA((2, 3)), DMA((10,))],
         2,
         [
             VM((rows, D), F32),
@@ -1003,38 +1148,53 @@
             VM((32, 32, 128), BF),
             VM((8, 2, 2, 64, rows), BF),
             VM((2, 16, 32, 2 * D), BF),
+            VM((length, D), BF),
+            VM((3, 16, 32, F), BF),
         ]
-        + Reduce.bufs(32, D + 128),
-    )
-    wg_sum = wg_all.reshape(2, 16, 32, 128).astype(F32).sum(axis=0).transpose(1, 0, 2)
-    plain_query = wg_sum[:, :, :64].reshape(32, D)
-    plain_key = wg_sum[:, 0::2, 64:].reshape(32, 512)
-    plain_value = wg_sum[:, 1::2, 64:].reshape(32, 512)
-    own_o = dwo_sum.astype(F32)
-    plain_router = own_o[:, D : D + E]
-    expert_grads = dw_all.transpose(1, 2, 0, 3).astype(F32)
-    plain_gate, plain_up = expert_grads[0], expert_grads[1]
-    grad_attention_gain = (
-        jnp.sum(plain_query * query_weight.astype(F32), axis=1)
-        + jnp.sum(plain_key * key_matrix.astype(F32), axis=1)
-        + jnp.sum(plain_value * value_matrix.astype(F32), axis=1)
-    )
-    grad_expert_gain = jnp.sum(
-        plain_gate * gate_weight.astype(F32) + plain_up * up_weight.astype(F32), axis=(1, 2)
-    ) + jnp.sum(plain_router * router_weight.astype(F32), axis=1)
+        + Reduce.bufs(32, D + 128)
+        + Reduce.bufs(rows, D),
+        None,
+        [VM] * 18 + [ANY] + [VM] * 4,
+    )
+    (
+        mixed, grad_tokens, grad_a, grad_e, grad_q, grad_k, grad_v, grad_o, grad_r, grad_gate, grad_up, grad_down,
+    ) = pl.pallas_call(
+        finish,
+        out_shape=[sds((rows, D), BF), sds((rows, D), F32), sds((1, 32), F32), sds((1, 32), F32)]
+        + [sds((32, n), F32) for n in (D, 512, 512, D)]
+        + [sds((E, 32), F32)]
+        + [sds((32, E, F), F32)] * 3,
+        scratch_shapes=[VM((F // 128, 32 * E, 128), F32)],
+        compiler_params=pltpu.CompilerParams(vmem_limit_bytes=VMEM_LIMIT),
+    )(
+        wg_all,
+        dwo_sum,
+        dw_all,
+        query_weight,
+        key_matrix,
+        value_matrix,
+        router_weight.T,
+        gate_weight,
+        up_weight,
+        attention_gain.reshape(1, 32),
+        expert_gain.reshape(1, 32),
+        mix,
+        residual,
+        grad_tokens,
+    )
     return (
         mixed.reshape(tokens.shape),
         grad_tokens.reshape(tokens.shape),
-        grad_attention_gain,
-        grad_expert_gain,
-        plain_query * gain_first,
-        plain_key * gain_first,
-        plain_value * gain_first,
-        own_o[:, :D],
-        plain_router * gain_second,
-        plain_gate * gain_second[..., None],
-        plain_up * gain_second[..., None],
-        expert_grads[2],
+        grad_a.reshape(32),
+        grad_e.reshape(32),
+        grad_q,
+        grad_k,
+        grad_v,
+        grad_o,
+        grad_r.T,
+        grad_gate,
+        grad_up,
+        grad_down,
     )
 
 

time: 361 us -> 305 us (0.84)
  Pallas kernels: 342 us -> 303 us
  local copies, waits for them, and re-layouts: 11.9 us -> 0 us
  other arithmetic: 5.9 us -> 0 us
    pallas_call x3 -> x2, Pallas kernels: 342 us -> 297 us  [comm_call(): pl.pallas_call(body, out_shape=outs, in_specs=[pl.BlockSpec(memory_space=...]
    unnamed x32 -> x0, local copies, waits for them, and re-layouts: 9.74 us -> none
    pallas_call x0 -> x1, Pallas kernels: none -> 5.3 us  [sixteen_seats(): pl.pallas_call(finish, out_shape=[sds((rows, D), BF), sds((rows, D), F32)...]
where the time goes in v4:
time: 305 us; the launch traced here: 304 us
  Pallas kernels  303 us (99%)
    pallas_call x2, Pallas kernels, comm_call(): pl.pallas_call(body, out_shape=outs, in_specs=[pl.BlockSpec(memory_space=...  297 us

profile of v4, /device:TPU:0, one launch (start us, length us, event | category | flops | bytes accessed | tf_op | source)
XLA Modules:
  0.0 304.0 jit_solution(13048776285122306967)
XLA Ops:
  1.3 183.0 %shard_map.247 = (bf16[16,128,1024]{2,1,0:T(8,128)(2,1)}, bf16[2,16,32,1152]{3,2,1,0:T(8,128)(2,1)}, bf16[16,128,1024]{2,1,0:T(8,128)(2,1)}, bf16[64,2048]{1,0:T...) custom-call(bf16[128,1024]{1,0:T(8,128)(2,1)} %bitcast.17, ...), custom_call_target="tpu_custom_call" | custom-call | tf_op jit(solution)/shard_map/pallas_call | solution.py:339
  184.3 114.4 %shard_map.248 = (f32[128,1024]{1,0:T(8,128)}, bf16[16,3,32,512]{3,2,1,0:T(8,128)(2,1)}, bf16[32,1152]{1,0:T(8,128)(2,1)}, bf16[32,32,128]{2,1,0:T(8,128)(2,1)}, bf16[128,1024]{1,0:T(8,128)(2,1)}) custom-call(bf16[128,1024]{1,0:T(8,128)(2,1)} %get-tuple-element.51.back, f32[16,8,128]{2,1,0:T(8,128)} %get-tuple-element.52.g_all, bf16[128,1024]{1,0:T(8,128)(2,1)} %bitcast.20, ...), custom_call_target="tpu_custom_call" | custom-call | tf_op jit(solution)/shard_map/pallas_call | solution.py:339
  298.7 5.3 %shard_map.249 = (bf16[128,1024]{1,0:T(8,128)(2,1)}, f32[128,1024]{1,0:T(8,128)}, f32[1,32]{1,0:T(1,128)}, f32[1,32]{1,0:T(1,128)}, f32[32,1024]{1,0:T(8,128)}, ...) custom-call(bf16[32,32,128]{2,1,0:T(8,128)(2,1)} %get-tuple-element., ...), custom_call_target="tpu_custom_call" | custom-call | tf_op jit(solution)/shard_map/pallas_call | solution.py:1161

commit v5 on v4

--- a/solution.py
+++ b/solution.py
@@ -99,6 +99,7 @@
 
 
 QB = 256
+TOKENS_CUT, COTS_CUT, HIDDEN_CUT = 112, None, 96
 
 
 def lane_block(i, size=QB):
@@ -106,8 +107,8 @@
 
 
 class Gather:
-    def __init__(self, own, at, send, recv):
-        self.own, self.at, self.send, self.recv = own, at, send, recv
+    def __init__(self, own, at, send, recv, cut=None):
+        self.own, self.at, self.send, self.recv, self.cut = own, at, send, recv, cut
         self.ending = False
         self.x, self.s, self.z, self.y, self.c = place()
 
@@ -120,22 +121,28 @@
             CORE: (x, seat(z, y, 1 - c)),
         }[k]
 
-    def copy(self, src, k, own=False):
+    def part(self, ref, p):
+        if self.cut is None:
+            return ref
+        return ref.at[self.cut : ref.shape[0]] if p else ref.at[0 : self.cut]
+
+    def copy(self, src, k, own=False, p=0):
         ref = self.own if own else self.at(src)
-        return remote(ref, self.at(src), self.send.at[src, k], self.recv.at[src], self.device(k))
-
-    def go(self, src, k, cond=None, own=False):
+        send, recv = self.send.at[src, k, p], self.recv.at[src, p]
+        return remote(self.part(ref, p), self.part(self.at(src), p), send, recv, self.device(k))
+
+    def go(self, src, k, cond=None, own=False, p=0):
         if k == UP:
             cond = both(cond, self.z < 3)
         if k == DOWN:
             cond = both(cond, self.z > 0)
         act = (lambda c: c.wait_send()) if self.ending else (lambda c: c.start())
-        when(cond, lambda: act(self.copy(src, k, own)))
-
-    def wait(self, src, cond=None):
+        when(cond, lambda: act(self.copy(src, k, own, p=p)))
+
+    def wait(self, src, cond=None, p=0):
         if self.ending:
             return
-        when(cond, lambda: self.copy(src, SIDE).wait_recv())
+        when(cond, lambda: self.copy(src, SIDE, p=p).wait_recv())
 
     def sides(self, t):
         if t == 0:
@@ -143,26 +150,38 @@
         return ((self.z - t >= 0, self.z - t, UP), (self.z + t <= 3, self.z + t, DOWN))
 
     def begin(self):
+        if self.cut is not None:
+            self.go(self.s, SIDE, own=True, p=1)
         for k in (UP, DOWN, SIDE, CORE):
-            self.go(self.s, k, own=self.own is not None)
+            self.go(self.s, k, own=True)
+        if self.cut is not None:
+            for k in (UP, DOWN, CORE):
+                self.go(self.s, k, own=True, p=1)
 
     def line(self, t):
         for cond, zz, k in self.sides(t):
-            src = seat(zz, self.y, self.c)
-            self.wait(src, cond)
-            for way in (k, SIDE, CORE):
-                self.go(src, way, cond)
+            mine, other = seat(zz, self.y, self.c), seat(zz, 1 - self.y, self.c)
+            parts = ((mine, 0, (k, SIDE, CORE)), (mine, 1, (k, CORE)), (other, 1, (k, CORE)))
+            for src, p, ways in parts[: 1 if self.cut is None else 3]:
+                self.wait(src, cond, p)
+                for way in ways:
+                    self.go(src, way, cond, p=p)
 
     def over(self, t):
         for cond, zz, _ in self.sides(t):
             src = seat(zz, 1 - self.y, self.c)
+            if t == 0 and self.cut is not None:
+                self.wait(src, cond, 1)
+                for way in (UP, DOWN, CORE):
+                    self.go(src, way, cond, p=1)
             self.wait(src, cond)
             self.go(src, CORE, cond)
 
     def done(self, t):
         for cond, zz, _ in self.sides(t):
             for yy in range(2):
-                self.wait(seat(zz, yy, 1 - self.c), cond)
+                for p in range(1 if self.cut is None else 2):
+                    self.wait(seat(zz, yy, 1 - self.c), cond, p)
 
     def end(self):
         self.ending = True
@@ -173,14 +192,14 @@
             self.over(t)
 
 
-GATHER_SEMS = [DMA((16, 4)), DMA((16,))]
+GATHER_SEMS = [DMA((16, 4, 2)), DMA((16, 2))]
 
 
 class GatherAll(Gather):
     def device(self, k):
         return (1 - self.x, self.s) if k == ACROSS else Gather.device(self, k)
 
-    def copy(self, src, k, own=False, x=None):
+    def copy(self, src, k, own=False, x=None, p=0):
         x = self.x if x is None else x
         ref = self.own if own else self.at(x, src)
         return remote(ref, self.at(x, src), self.send.at[x, src, k], self.recv.at[x, src], self.device(k))
@@ -279,13 +298,37 @@
             self.copy(k).wait_send()
 
 
+class Swap(Exchange):
+    def __init__(self, src, dst, whole, most, send, recv, wide=False):
+        Exchange.__init__(self, src, dst, send, recv, wide)
+        self.whole, self.most = whole, most
+
+    def keep(self):
+        me = self.index((self.x, self.s))
+        return pltpu.make_async_copy(self.src(me), self.dst(me), self.recv.at[0])
+
+    def copy(self, k):
+        to, me = self.seat(k), self.index((self.x, self.s))
+        return remote(self.src(self.index(to)), self.dst(me), self.send.at[0], self.recv.at[0], to)
+
+    def arrived(self):
+        remote(self.whole, self.whole, self.send.at[0], self.recv.at[0], self.seat(1)).wait_recv()
+
+    def sent(self):
+        remote(self.most, self.most, self.send.at[0], self.recv.at[0], self.seat(1)).wait_send()
+
+    def end(self):
+        self.arrived()
+        self.sent()
+
+
 class Slices:
     def __init__(self, src, got, send, recv):
         self.x, self.s, self.z, self.y, self.c = place()
         self.src, self.got, self.send, self.recv = src, got, send, recv
 
     def block(self, pair):
-        return self.src.at[:, lane_block(pair, 256)]
+        return self.src.at[pl.ds((pair // 4) * 32, 32), lane_block(pair % 4, 256)]
 
     def copy(self, k):
         z, y = (self.z + k // 2) % 4, (self.y + k) % 2
@@ -353,8 +396,9 @@
 
 
 class Reduce:
-    def __init__(self, part, out, bufs, sems):
+    def __init__(self, part, out, bufs, sems, near=None):
         self.part, self.out = part, out
+        self.near = part if near is None else near
         self.r1, self.ra, self.ua, self.da = bufs
         self.s1, self.q1, self.sa, self.qa, self.su, self.qu, self.sd, self.qd = sems
         self.x, self.s, self.z, self.y, self.c = place()
@@ -417,7 +461,7 @@
         def go():
             for yy in range(2):
                 self.first(zz, yy).wait_recv()
-                self.add(self.r1.at[zz, yy], self.part.at[seat(zz, yy, self.c)])
+                self.add(self.r1.at[zz, yy], self.near.at[seat(zz, yy, self.c)])
             for p in range(2):
                 self.side(zz, p).start()
 
@@ -492,35 +536,38 @@
     return jnp.sum(jnp.where(same, jnp.broadcast_to(line.astype(F32), (n, n)), 0.0), axis=1, keepdims=True)
 
 
-def front(
+def layer(
     tok, query_w, key_w, value_w, out_w, router_w, gate_w, up_w, down_w, gain_a, gain_e, seg, routes, cot, rope, freq,
-    hid, wo_all, mixp, q_t, k_t, v_t, o_t, lse, start, cos, sin,
-    residual, normed, scale_out, h2, att, probs, picked, wperm, back, g_all, dw,
+    hid, mixp, dw_all, grad_tokens, dwo_sum, wg_all, mix, residual,
+    q_t, k_t, v_t, o_t, lse, start, cos, sin, normed, scale_out, h2, att, probs, picked, wperm, back, g_all,
     wo, w3, spread, seg_mine, row_all, w_mine, seg_all, o_low, att_t, k_n, w_t, wo_v,
     wexp, cot_all, p_t, p_all, backp, mix_v, gg, acc,
+    g_res, grad_t, router_t, dwo, dwo_x, gkv, v_n, delta, got, g_t, wg, g_mine,
     *rest,
 ):
-    bufs, sems = rest[:NBUF], rest[NBUF:]
+    bufs, bufs_o, sems = rest[:NBUF], rest[NBUF : 2 * NBUF], rest[2 * NBUF :]
     (
-        t_send, t_recv, o_send, o_recv, c_send, c_recv, h_send, h_recv, w_send, w_recv, g_send, g_recv,
-        a_send, a_recv, e_send, e_recv, x_send, x_recv, p_send, p_recv, y_send, y_recv, x_sem,
-    ) = sems[NSEM:]
+        t_send, t_recv, o_send, o_recv, c_send, c_recv, h_send, h_recv, q_send, q_recv, w_send, w_recv, e_send, e_recv,
+        x_send, x_recv, g_send, g_recv, a_send, a_recv, p_send, p_recv, y_send, y_recv, b_send, b_recv, r_send, r_recv,
+        v_send, v_recv, w0s, w0r, w1s, w1r, w2s, w2r, d_sem, x_sem, free,
+    ) = sems[3 * NSEM :]
     x, s, z, y, c = place()
     rows, width = tok.shape
     length = 16 * rows
     barrier_all()
-    tokens = Gather(tok, lambda src: row_all.at[src], t_send, t_recv)
+    tokens = Gather(tok, lambda src: row_all.at[src], t_send, t_recv, TOKENS_CUT)
     tokens.begin()
     keep_tok = pltpu.make_async_copy(tok, row_all.at[s], x_sem.at[2])
     keep_tok.start()
     seg_mine[...] = jnp.broadcast_to(seg[...], seg_mine.shape)
-    documents = Exchange(lambda r: seg_mine, lambda r: seg_all.at[r], g_send, g_recv)
+    documents = Swap(lambda r: seg_mine, lambda r: seg_all.at[r], seg_all, seg_all.at[0:15], g_send, g_recv)
     documents.begin()
     by_first = column(gain_a[...])
     for j in range(8):
-        wperm[:, 256 * j : 256 * j + 128] = (query_w[:, 128 * j : 128 * j + 128].astype(F32) * by_first).astype(BF)
+        part, lane = slice(32 * (j // 4), 32 * (j // 4) + 32), 256 * (j % 4)
+        wperm[part, lane : lane + 128] = (query_w[:, 128 * j : 128 * j + 128].astype(F32) * by_first).astype(BF)
         pair = [ref[:, 64 * j : 64 * j + 64].astype(F32) for ref in (key_w, value_w)]
-        wperm[:, 256 * j + 128 : 256 * j + 256] = (jnp.concatenate(pair, axis=1) * by_first).astype(BF)
+        wperm[part, lane + 128 : lane + 256] = (jnp.concatenate(pair, axis=1) * by_first).astype(BF)
     slices = Slices(wperm, w_mine, w_send, w_recv)
     slices.begin()
     by_second = column(gain_e[...])
@@ -535,24 +582,23 @@
         plain = ref[...].astype(F32).reshape(32 * E, F)
         for b in range(F // 128):
             lanes = slice(b * 128, b * 128 + 128)
-            spread[b] = plain[:, lanes]
+            spread[...] = plain[:, lanes]
             for e in range(E):
-                part = spread[b, pl.ds(e, 32, stride=E), :]
+                part = spread[pl.ds(e, 32, stride=E), :]
                 w3[e, m, :, lanes] = (part * by_second if m < 2 else part).astype(BF)
     weights = Exchange(lambda e: w3.at[e], lambda r: wexp.at[:, x * 16 + r], e_send, e_recv)
-    cots = Gather(cot, lambda src: cot_all.at[src], c_send, c_recv)
-
-    def cross(k, begin=True):
+    cots = Gather(cot, lambda src: cot_all.at[src], c_send, c_recv, COTS_CUT)
+
+    def cross_copy(k, back=False):
         row = weights.index(weights.seat(k, back=True))
-        if begin and k:
+        src = w3.at[s] if k == 0 else wexp.at[:, x * 16 + row]
+        dst = wexp.at[:, (1 - x if back else x) * 16 + row]
+        return remote(src, dst, x_send.at[k], x_recv.at[k], (1 - x, s))
+
+    def cross(k):
+        if k:
             weights.arrive(k)
-        src = w3.at[s] if k == 0 else wexp.at[:, x * 16 + row]
-        copy = remote(src, wexp.at[:, x * 16 + row], x_send.at[k], x_recv.at[k], (1 - x, s))
-        if begin:
-            copy.start()
-        else:
-            copy.wait_send()
-            remote(src, wexp.at[:, (1 - x) * 16 + row], x_send.at[k], x_recv.at[k], (1 - x, s)).wait_recv()
+        cross_copy(k).start()
 
     factor = jnp.exp2(rope[0].astype(F32))
     for b in range(length // 128):
@@ -564,8 +610,8 @@
     tokens.line(1)
     slices.share()
     tokens.over(1)
+    outw.begin()
     tokens.line(2)
-    outw.begin()
     weights.begin(range(8))
     slices.end()
     w_t[...] = jnp.transpose(w_mine[...].reshape(width, 256).astype(F32)).astype(BF)
@@ -574,8 +620,6 @@
     outw.over(0)
     outw.line(1)
     weights.begin(range(8, 12))
-    for k in range(4):
-        cross(k)
     documents.end()
     numbers = seg_all[:, 0, :]
     ends = [jnp.sum((numbers < n).astype(jnp.int32)) for n in (1, 2)]
@@ -588,6 +632,8 @@
     keep_tok.wait()
     tokens.end()
     acc[...] = jnp.zeros(acc.shape, F32)
+    for k in range(4):
+        cross(k)
 
     def project(i, _):
         cols = lane_block(i, 512)
@@ -620,8 +666,6 @@
         def _():
             outw.over(2)
             outw.line(3)
-            for k in range(4, 8):
-                cross(k)
 
         @pl.when(i == 6)
         def _():
@@ -660,23 +704,24 @@
         return 0
 
     lax.fori_loop(0, length // QB, query_block, 0)
+    for k in range(4, 8):
+        cross(k)
     keep_hid.wait()
-    heads = Exchange(lambda t: o_low.at[:, lane_block(t, 128)], lambda h: att_t.at[h], a_send, a_recv)
+    heads = Swap(
+        lambda t: o_low.at[:, lane_block(t, 128)], lambda h: att_t.at[h], att_t, att_t.at[0:15], a_send, a_recv
+    )
     heads.begin()
     keep_cot = pltpu.make_async_copy(cot, cot_all.at[s], x_sem.at[6])
     keep_cot.start()
-    cots.over(0)
-    cots.line(1)
     for t in range(4):
         outw.across(t)
     for t in range(4):
         outw.done(t)
     keep.wait()
-    keep_wo = pltpu.make_async_copy(wo_v, wo_all, x_sem.at[5])
-    keep_wo.start()
+    cots.over(0)
+    cots.line(1)
     weights.begin(range(12, 16))
     heads.end()
-    cots.over(1)
     for k in range(8, 12):
         cross(k)
 
@@ -703,24 +748,27 @@
     picked[...] = mask
     p_t[...] = jnp.transpose(prob * mask)[0:E, :]
 
-    hidden = Gather(h2, lambda src: row_all.at[src], h_send, h_recv)
+    hidden = Gather(h2, lambda src: row_all.at[src], h_send, h_recv, HIDDEN_CUT)
     hidden.begin()
     keep = pltpu.make_async_copy(h2, row_all.at[s], x_sem.at[8])
     keep.start()
-    minor = Exchange(lambda r: p_t, lambda r: p_all.at[r], p_send, p_recv)
+    minor = Swap(lambda r: p_t, lambda r: p_all.at[r], p_all, p_all.at[0:15], p_send, p_recv)
     minor.begin()
     one = Reduce(backp, back, bufs, sems[:NSEM])
-    cots.line(2)
     hidden.over(0)
     keep.wait()
     keep_cot.wait()
+    weights.end_sends()
+    weights.keep().wait()
+    cross_copy(0).wait_send()
     for k in range(12, 16):
         cross(k)
     minor.end()
     hidden.line(1)
-    weights.keep().wait()
     for k in range(16):
-        cross(k, begin=False)
+        if k:
+            cross_copy(k).wait_send()
+        cross_copy(k, back=True).wait_recv()
     cots.done(0)
     hidden.done(0)
     far = z // 2
@@ -748,6 +796,7 @@
         def _():
             hidden.over(1)
             hidden.line(2)
+            cots.over(1)
 
         @pl.when(i == 1)
         def _():
@@ -779,7 +828,15 @@
 
         @pl.when(i == 0)
         def _():
+            cots.line(2)
+
+        @pl.when(i == 1)
+        def _():
             cots.over(2)
+
+        @pl.when(i == 2)
+        def _():
+            cots.over(3)
 
         @pl.when(i == 3)
         def _():
@@ -794,110 +851,124 @@
         acc[1] += dot(some, grad_up, TN)
         acc[2] += dot(grad, (prob * low.astype(F32)).astype(BF), TN)
 
-        @pl.when(i == 0)
+        @pl.when(i == 1)
         def _():
             cots.line(3)
 
-        @pl.when(i == 1)
-        def _():
-            cots.over(3)
-
         return 0
 
     lax.fori_loop(0, 4, chunk, 0)
     one.fold(order[3])
-    seen_out = Exchange(lambda r: gg.at[r], lambda r: g_all.at[r], y_send, y_recv)
+    seen_out = Swap(lambda r: gg.at[r], lambda r: g_all.at[r], g_all, g_all.at[0:15], y_send, y_recv)
     seen_out.begin()
-    dw[...] = acc[...].astype(BF).reshape(dw.shape)
-    one.flow()
-    weights.end_sends()
+
+    def over_d(m):
+        part = wexp.at[m, pl.ds((1 - x) * 16, 16)]
+        return remote(part, w3.at[:, m], d_sem.at[0, m], d_sem.at[1, m], (1 - x, s))
+
+    for m in range(3):
+        wexp[m] = acc[m].astype(BF).reshape(wexp.shape[1:])
+        over_d(m).start()
+    owners = [
+        Swap(
+            lambda r, m=m: w3.at[r, m],
+            lambda e, m=m: dw_all.at[m, e],
+            dw_all.at[m],
+            dw_all.at[m, 0:15],
+            (w0s, w1s, w2s)[m],
+            (w0r, w1r, w2r)[m],
+        )
+        for m in range(3)
+    ]
+
+    def to_owners(m):
+        over_d(m).wait()
+        w3[:, m] = (w3[:, m].astype(F32) + wexp[m, pl.ds(x * 16, 16)].astype(F32)).astype(BF)
+        owners[m].begin()
+
     for g in (outw, cots, hidden):
         g.end()
-    keep_wo.wait()
+    one.flow()
+    one.end()
     pltpu.make_async_copy(mix_v, mixp.at[pl.ds(0, 4)], x_sem.at[7]).wait()
-    seen_out.end()
-    one.end()
-
-
-def rear(
-    back, g_all, cot, probs, picked, normed, scale, wo, att, h2, dw, mixp, q_t, k_t, v_t, lse, o_t, start, hid_in, cos, sin,
-    wperm, tok,
-    grad_tokens, dw_all, dwo_sum, wg_all, mix,
-    g_res, ga_t, dwo, dwo_x, go_t, gq_t, gkv, k_n, v_n, delta, got, g_t, wg, g_mine, wp, hid, dwx,
-    *rest,
-):
-    bufs, bufs_b = rest[:NBUF], rest[NBUF : 2 * NBUF]
-    sems = rest[2 * NBUF :]
-    (
-        a_send, a_recv, b_send, b_recv, w0s, w0r, w1s, w1r, w2s, w2r, v_send, v_recv, p_send, p_recv, d_sem, x_sem,
-    ) = sems[2 * NSEM :]
-    x, s, z, y, c = place()
-    width = att.shape[1]
-    length = q_t.shape[1]
-    barrier_all()
-    two = Reduce(mixp, mix, bufs_b, sems[NSEM : 2 * NSEM])
-    two.begin()
-    columns_all = GatherAll(wperm, lambda x, src: wp.at[x, src], p_send, p_recv)
-    columns_all.begin()
+    near = (
+        (z < 3, (x, seat(z + 1, y, c))),
+        (z > 0, (x, seat(z - 1, y, c))),
+        (None, (x, seat(z, 1 - y, c))),
+        (None, (x, seat(z, y, 1 - c))),
+        (None, (1 - x, s)),
+    )
+    for cond, dev in near:
+        when(cond, lambda dev=dev: pl.semaphore_signal(free, inc=1, device_id=dev, device_id_type=MESH))
     loads = [
-        pltpu.make_async_copy(wperm, wp.at[x, s], x_sem.at[6]),
-        pltpu.make_async_copy(hid_in, hid, x_sem.at[4]),
+        pltpu.make_async_copy(hid, row_all, x_sem.at[9]),
+        pltpu.make_async_copy(mixp, backp, x_sem.at[10]),
     ]
     for copy in loads:
         copy.start()
-    owners = [
-        Exchange(
-            lambda r, m=m: dwx.at[m, r],
-            lambda e, m=m: dw_all.at[e, m],
-            (w0s, w1s, w2s)[m],
-            (w0r, w1r, w2r)[m],
-        )
-        for m in range(3)
-    ]
-
-    def over_d(m):
-        return remote(dw.at[m, 1 - x], dwx.at[m], d_sem.at[0, m], d_sem.at[1, m], (1 - x, s))
-
-    def to_owners(m):
-        over_d(m).wait()
-        dwx[m] = (dwx[m].astype(F32) + dw[m, x].astype(F32)).astype(BF)
-        owners[m].begin()
-
-    over_d(0).start()
+    seen_out.end()
+    pl.semaphore_wait(free, 3 + (z < 3).astype(jnp.int32) + (z > 0).astype(jnp.int32))
+    me = x * 16 + s
+    columns_all = GatherAll(
+        wperm, lambda x_, src: cot_all.at[x_ * 8 + src // 2, pl.ds((src % 2) * 64, 64)], q_send, q_recv
+    )
+    columns_all.begin()
+    keep_w = pltpu.make_async_copy(wperm, cot_all.at[me // 2, pl.ds((me % 2) * 64, 64)], x_sem.at[11])
+    keep_w.start()
+    two = Reduce(mixp, mix, bufs, sems[NSEM : 2 * NSEM], backp)
+    two.begin()
 
     seen = jnp.concatenate([g_all[e, 0:1, :] for e in range(E)] + [jnp.zeros((128 - E, 128), F32)], axis=0)
     grad_probs = jnp.transpose(seen) * picked[...]
     prob = probs[...]
     grad_logits = (prob * (grad_probs - jnp.sum(prob * grad_probs, axis=-1, keepdims=True))).astype(BF)
-    u = back[...].astype(F32) + dot(grad_logits, wo[:, width : width + 128], NT)
+    u = back[...].astype(F32) + dot(
+        grad_logits, wo_v[:, :, :, width : width + 128].reshape(width, 128), NT
+    )
     norm = normed[...]
-    grad = cot[...].astype(F32) + scale[:, 0:1] * (u - norm * jnp.mean(u * norm, axis=-1, keepdims=True))
+    grad = cot[...].astype(F32) + scale_out[:, 0:1] * (u - norm * jnp.mean(u * norm, axis=-1, keepdims=True))
     g_res[...] = grad
     branch = grad.astype(BF)
-    ga_t[...] = jnp.transpose(dot(branch, wo[:, 0:width])).astype(BF).reshape(ga_t.shape)
-    heads = Exchange(lambda h: ga_t.at[h], lambda t: go_t.at[:, lane_block(t, 128)], a_send, a_recv)
+    att_t[...] = jnp.transpose(dot(branch, wo_v[:, :, :, 0:width].reshape(width, width))).astype(BF).reshape(att_t.shape)
+    heads = Swap(
+        lambda h: att_t.at[h], lambda t: o_low.at[:, lane_block(t, 128)], o_low, att_t.at[0:15], b_send, b_recv
+    )
     heads.begin()
-    over_d(1).start()
-    over_d(2).start()
+    columns_all.over(0)
+    columns_all.line(1)
+    loads[1].wait()
     for cond, zz, _ in two.order():
         two.fold(zz, cond)
-    dwo[:, :, :, 0:width] = dot(jnp.transpose(grad).astype(BF), att[...]).astype(BF).reshape(2, 16, 32, width)
-    dwo[:, :, :, width : width + 128] = dot(h2[...], grad_logits, TN).astype(BF).reshape(2, 16, 32, 128)
-    over_o = remote(dwo.at[1 - x], dwo_x, x_sem.at[0], x_sem.at[1], (1 - x, s))
+    grad_t[...] = jnp.transpose(grad).astype(BF)
+    other = pl.ds((1 - x) * (width // 2), width // 2)
+    router_t[...] = dot(h2[...], grad_logits, TN).astype(BF)
+    dwo[:, :, 0:width] = dot(grad_t[other, :], att[...]).astype(BF).reshape(16, 32, width)
+    dwo[:, :, width : width + 128] = router_t[other, :].reshape(16, 32, 128)
+    over_o = remote(dwo, dwo_x, x_sem.at[12], x_sem.at[13], (1 - x, s))
     over_o.start()
     to_owners(0)
-    k_n[...] = jnp.transpose(k_t[...].astype(F32)).astype(BF)
+    to_owners(1)
     v_n[...] = jnp.transpose(v_t[...].astype(F32)).astype(BF)
     gkv[...] = jnp.zeros(gkv.shape, F32)
-    columns_all.over(0)
     heads.end()
-    columns_all.line(1)
-    delta[...] = jnp.sum(go_t[...].astype(F32) * o_t[...], axis=0, keepdims=True)
+    delta[...] = jnp.sum(o_low[...].astype(F32) * o_t[...], axis=0, keepdims=True)
 
     def query_block(i, _):
-        pl.when(i == 4)(lambda: to_owners(1))
+        @pl.when(i == 3)
+        def _():
+            two.flow()
+
+        @pl.when(i == 4)
+        def _():
+            columns_all.over(1)
+            to_owners(2)
+
+        @pl.when(i == 5)
+        def _():
+            columns_all.line(2)
+
         cols = lane_block(i)
-        queries, grads = q_t[:, cols], go_t[:, cols]
+        queries, grads = q_t[:, cols], o_low[:, cols]
         begin, log_total, shift = start[:, cols], lse[:, cols], delta[:, cols]
 
         def key_block(j, sofar):
@@ -910,19 +981,23 @@
             gkv[1, :, rows] += dot(grads, powers.astype(BF), NT)
             return sofar + dot(k_t[:, rows], grad_scores)
 
-        gq_t[:, cols] = lax.fori_loop(0, i + 1, key_block, jnp.zeros((HEAD_SIZE, QB), F32))
+        o_t[:, cols] = lax.fori_loop(0, i + 1, key_block, jnp.zeros((HEAD_SIZE, QB), F32))
         return 0
 
     lax.fori_loop(0, length // QB, query_block, 0)
-    columns_all.over(1)
-    columns_all.line(2)
-    two.flow()
-
-    pair = remote(gkv.at[1 - c], got, x_sem.at[2], x_sem.at[3], (x, seat(z, y, 1 - c)))
+    columns_all.over(2)
+
+    pair = remote(gkv.at[1 - c], got, x_sem.at[14], x_sem.at[15], (x, seat(z, y, 1 - c)))
     pair.start()
-    columns_all.over(2)
     columns_all.line(3)
-    columns_all.over(3)
+    over_o.wait_recv()
+    own = pl.ds(x * (width // 2), width // 2)
+    mine = dot(grad_t[own, :], att[...]).reshape(16, 32, width)
+    dwo_x[:, :, 0:width] = (dwo_x[:, :, 0:width].astype(F32) + mine).astype(BF)
+    mine = router_t[own, :].reshape(16, 32, 128).astype(F32)
+    dwo_x[:, :, width : width + 128] = (dwo_x[:, :, width : width + 128].astype(F32) + mine).astype(BF)
+    out = Reduce(dwo_x, dwo_sum, bufs_o, sems[2 * NSEM : 3 * NSEM])
+    out.begin()
     scaling = 1.0 / math.sqrt(HEAD_SIZE)
     co, si = cos[...], sin[...]
 
@@ -930,39 +1005,46 @@
         a, b = part[:32], part[32:]
         return jnp.concatenate([a * co + b * si, b * co - a * si], axis=0)
 
-    g_t[0] = unturn(gq_t[...] * scaling).astype(BF)
+    g_t[0] = unturn(o_t[...] * scaling).astype(BF)
     pair.wait()
     mine = gkv[c] + got[...]
     g_t[1] = jnp.where(c == 0, unturn(mine * scaling), mine).astype(BF)
-    tokens = Exchange(
-        lambda t: g_t.at[:, :, lane_block(t, 128)], lambda h: g_mine.at[h // 2, :, h % 2], b_send, b_recv
+    tokens = Swap(
+        lambda t: g_t.at[:, :, lane_block(t, 128)],
+        lambda h: g_mine.at[h // 2, :, h % 2],
+        g_mine,
+        g_t.at[:, :, 0 : length - 128],
+        r_send,
+        r_recv,
     )
     tokens.begin()
-    loads[1].wait()
-    wg[...] = jnp.transpose(dot(g_t[...].reshape(128, length), hid[...])).astype(BF).reshape(wg.shape)
-    columns = Exchange(lambda r: wg.at[r], lambda r: wg_all.at[r], v_send, v_recv, wide=True)
+    loads[0].wait()
+    wg[...] = jnp.transpose(dot(g_t[...].reshape(128, length), row_all[...].reshape(length, width))).astype(BF).reshape(
+        wg.shape
+    )
+    columns = Swap(lambda r: wg.at[r], lambda r: wg_all.at[r], wg_all, wg_all.at[0:31], v_send, v_recv, wide=True)
     columns.begin()
-    over_o.wait_recv()
-    dwo_x[...] = (dwo_x[...].astype(F32) + dwo[x].astype(F32)).astype(BF)
-    out = Reduce(dwo_x, dwo_sum, bufs, sems[:NSEM])
-    out.begin()
-    out.run()
+    columns_all.over(3)
     for t in range(4):
         columns_all.across(t)
-    tokens.end()
     for t in range(4):
         columns_all.done(t)
-    loads[0].wait()
-    w = jnp.transpose(dot(wp[...].reshape(width, 2 * width), g_mine[...].reshape(2 * width, 128)))
+    keep_w.wait()
+    for cond, zz, _ in out.order():
+        out.fold(zz, cond)
+    tokens.end()
+    halves = cot_all[...].reshape(32, 2, 32, width)
+    w = sum(dot(halves[:, h].reshape(width, width), g_mine[4 * h : 4 * h + 4].reshape(width, 128)) for h in range(2))
+    w = jnp.transpose(w)
     values = tok[...].astype(F32)
     scale_first = lax.rsqrt(jnp.mean(values * values, axis=-1, keepdims=True) + EPSILON)
     norm = values * scale_first
     grad_tokens[...] = g_res[...] + scale_first * (w - norm * jnp.mean(w * norm, axis=-1, keepdims=True))
-    to_owners(2)
+    out.flow()
     out.end()
     columns.end()
-    for m in range(3):
-        owners[m].end()
+    for owner in owners:
+        owner.end()
     over_o.wait_send()
     two.end()
     columns_all.end()
@@ -1000,7 +1082,7 @@
         for b in range(F // 128):
             lanes = slice(b * 128, b * 128 + 128)
             for e in range(E):
-                part = dw_all[e, m, :, lanes].astype(F32)
+                part = dw_all[m, e, :, lanes].astype(F32)
                 spread[b, pl.ds(e, 32, stride=E), :] = part
             plain = spread[b]
             if m == 2:
@@ -1041,18 +1123,10 @@
     cot_mine = cotangent.reshape(rows, D)
     powers = np.power(np.float32(ROPE_BASE), -np.arange(32, dtype=np.float32) * np.float32(2.0 / HEAD_SIZE))
     freq = jnp.asarray(np.broadcast_to(powers[:, None], (32, 128)).astype(np.float32))
-    (
-        hid, wo_all, mixp, q_t, k_t, v_t, o_t, lse, start, cos, sin,
-        residual, normed, scale, h2, att, probs, picked, wperm, back, g_all, dw,
-    ) = comm_call(
-        front,
-        [sds((16, rows, D), BF), sds((2, 16, 32, D + 128), BF), sds((16, rows, D), BF)]
-        + [sds((64, length), BF)] * 3
-        + [sds((64, length), F32), sds((1, length), F32), sds((1, length), jnp.int32)]
-        + [sds((32, length), F32)] * 2
-        + [sds((rows, D), F32), sds((rows, D), F32), sds((rows, 128), F32), sds((rows, D), BF), sds((rows, D), BF)]
-        + [sds((rows, 128), F32), sds((rows, 128), F32), sds((32, 2 * D), BF)]
-        + [sds((rows, D), BF), sds((16, 8, rows), F32), sds((3, 2, 16, 32, F), BF)],
+    _, _, dw_all, grad_tokens, dwo_sum, wg_all, mix, residual = comm_call(
+        layer,
+        [sds((16, rows, D), BF), sds((16, rows, D), BF), sds((3, 16, 32, F), BF), sds((rows, D), F32)]
+        + [sds((32, D + 128), BF), sds((32, 32, 128), BF), sds((rows, D), BF), sds((rows, D), F32)],
         [
             tok_mine,
             query_weight,
@@ -1071,12 +1145,25 @@
             rope_index.astype(jnp.int32),
             freq,
         ],
-        Reduce.SEMS + GATHER_SEMS + GATHER_ALL_SEMS + GATHER_SEMS * 2 + [DMA((16,))] * 14 + [DMA((12,))],
+        Reduce.SEMS * 3
+        + GATHER_SEMS
+        + GATHER_ALL_SEMS
+        + GATHER_SEMS * 2
+        + GATHER_ALL_SEMS
+        + [DMA((16,))] * 6
+        + [DMA((1,))] * 20
+        + [DMA((2, 3)), DMA((16,)), pltpu.SemaphoreType.REGULAR],
         0,
-        [
+        [VM((64, length), BF)] * 3
+        + [VM((64, length), F32), VM((1, length), F32), VM((1, length), jnp.int32)]
+        + [VM((32, length), F32)] * 2
+        + [VM((rows, D), F32), VM((rows, 128), F32), VM((rows, D), BF), VM((rows, D), BF)]
+        + [VM((rows, 128), F32), VM((rows, 128), F32), VM((64, D), BF), VM((rows, D), BF)]
+        + [VM((16, 8, rows), F32)]
+        + [
             VM((32, D + 128), BF),
             VM((E, 3, 32, F), BF),
-            VM((F // 128, 32 * E, 128), F32),
+            VM((32 * E, 128), F32),
             VM((8, rows), jnp.int32),
             VM((16, rows, D), BF),
             VM((2, 8, 2, 32, 256), BF),
@@ -1095,66 +1182,24 @@
             VM((16, 8, rows), F32),
             VM((3, D, F), F32),
         ]
-        + Reduce.bufs(rows, D),
-        [ANY] * 3 + [VM] * 19,
-        [VM] * 14 + [SM, VM],
-    )
-    wo_all = wo_all.reshape(D, D + 128)
-    hid = hid.reshape(length, D)
-    grad_tokens, dw_all, dwo_sum, wg_all, mix = comm_call(
-        rear,
-        [sds((rows, D), F32), sds((16, 3, 32, F), BF), sds((32, D + 128), BF), sds((32, 32, 128), BF)]
-        + [sds((rows, D), BF)],
-        [
-            back,
-            g_all,
-            cot_mine,
-            probs,
-            picked,
-            normed,
-            scale,
-            wo_all,
-            att,
-            h2,
-            dw,
-            mixp,
-            q_t,
-            k_t,
-            v_t,
-            lse,
-            o_t,
-            start,
-            hid,
-            cos,
-            sin,
-            wperm,
-            tok_mine,
-        ],
-        Reduce.SEMS * 2 + [DMA((16,))] * 10 + [DMA((32,))] * 2 + GATHER_ALL_SEMS + [DMA((2, 3)), DMA((10,))],
-        2,
-        [
+        + [
             VM((rows, D), F32),
-            VM((16, 64, rows), BF),
-            VM((2, 16, 32, D + 128), BF),
+            VM((D, rows), BF),
+            VM((D, 128), BF),
             VM((16, 32, D + 128), BF),
-            VM((64, length), BF),
-            VM((64, length), F32),
+            VM((16, 32, D + 128), BF),
             VM((2, 64, length), F32),
-            VM((length, 64), BF),
             VM((length, 64), BF),
             VM((1, length), F32),
             VM((64, length), F32),
             VM((2, 64, length), BF),
             VM((32, 32, 128), BF),
             VM((8, 2, 2, 64, rows), BF),
-            VM((2, 16, 32, 2 * D), BF),
-            VM((length, D), BF),
-            VM((3, 16, 32, F), BF),
         ]
-        + Reduce.bufs(32, D + 128)
-        + Reduce.bufs(rows, D),
-        None,
-        [VM] * 18 + [ANY] + [VM] * 4,
+        + Reduce.bufs(rows, D)
+        + Reduce.bufs(32, D + 128),
+        [ANY] * 3 + [VM] * 5,
+        [VM] * 14 + [SM, VM],
     )
     (
         mixed, grad_tokens, grad_a, grad_e, grad_q, grad_k, grad_v, grad_o, grad_r, grad_gate, grad_up, grad_down,

time: 305 us -> 290 us (0.951)
  Pallas kernels: 303 us -> 288 us
    pallas_call x2 -> x1, Pallas kernels: 297 us -> 283 us  [comm_call(): pl.pallas_call(body, out_shape=outs, in_specs=[pl.BlockSpec(memory_space=...]
where the time goes in v5:
time: 290 us; the launch traced here: 289 us
  Pallas kernels  288 us (99%)
    pallas_call x1, Pallas kernels, comm_call(): pl.pallas_call(body, out_shape=outs, in_specs=[pl.BlockSpec(memory_space=...  283 us

profile of v5, /device:TPU:0, one launch (start us, length us, event | category | flops | bytes accessed | tf_op | source)
XLA Modules:
  0.0 289.5 jit_solution(1755812115340712142)
XLA Ops:
  1.3 282.9 %shard_map.247 = (bf16[16,128,1024]{2,1,0:T(8,128)(2,1)}, bf16[16,128,1024]{2,1,0:T(8,128)(2,1)}, bf16[3,16,32,512]{3,2,1,0:T(8,128)(2,1)}, f32[128,1024]{1,0:T(...) custom-call(bf16[128,1024]{1,0:T(8,128)(2,1)} %bitcast.13, ...), custom_call_target="tpu_custom_call" | custom-call | tf_op jit(solution)/shard_map/pallas_call | solution.py:382
  284.2 5.3 %shard_map.248 = (bf16[128,1024]{1,0:T(8,128)(2,1)}, f32[128,1024]{1,0:T(8,128)}, f32[1,32]{1,0:T(1,128)}, f32[1,32]{1,0:T(1,128)}, f32[32,1024]{1,0:T(8,128)}, ...) custom-call(bf16[32,32,128]{2,1,0:T(8,128)(2,1)} %get-tuple-element., ...), custom_call_target="tpu_custom_call" | custom-call | tf_op jit(solution)/shard_map/pallas_call | solution.py:1206

commit v6 on v5

--- a/solution.py
+++ b/solution.py
@@ -98,8 +98,8 @@
     pl.semaphore_wait(sem, 2 + (z < 3).astype(jnp.int32) + (z > 0).astype(jnp.int32))
 
 
-QB = 256
-TOKENS_CUT, COTS_CUT, HIDDEN_CUT = 112, None, 96
+QB = 512
+TOKENS_CUT, COTS_CUT, HIDDEN_CUT = None, None, 64
 
 
 def lane_block(i, size=QB):
@@ -196,6 +196,8 @@
 
 
 class GatherAll(Gather):
+    first_y = False
+
     def device(self, k):
         return (1 - self.x, self.s) if k == ACROSS else Gather.device(self, k)
 
@@ -210,16 +212,19 @@
 
     def line(self, t):
         for cond, zz, k in self.sides(t):
-            src = seat(zz, self.y, self.c)
-            self.wait(src, cond)
-            for way in (k, SIDE, ACROSS, CORE):
-                self.go(src, way, cond)
+            mine, other = seat(zz, self.y, self.c), seat(zz, 1 - self.y, self.c)
+            for src in (mine, other) if self.first_y else (mine,):
+                self.wait(src, cond)
+                for way in (k, ACROSS, CORE) if self.first_y else (k, SIDE, ACROSS, CORE):
+                    self.go(src, way, cond)
 
     def over(self, t):
+        if self.first_y and t:
+            return
         for cond, zz, _ in self.sides(t):
             src = seat(zz, 1 - self.y, self.c)
             self.wait(src, cond)
-            for way in (ACROSS, CORE):
+            for way in (UP, DOWN, ACROSS, CORE) if self.first_y else (ACROSS, CORE):
                 self.go(src, way, cond)
 
     def across(self, t):
@@ -243,6 +248,10 @@
         Gather.end(self)
         for t in range(4):
             self.across(t)
+
+
+class GatherAllY(GatherAll):
+    first_y = True
 
 
 GATHER_ALL_SEMS = [DMA((2, 16, 5)), DMA((2, 16))]
@@ -657,23 +666,16 @@
     keep_hid.start()
 
     def query_block(i, _):
-        @pl.when(i == 2)
+        @pl.when(i == 1)
         def _():
             outw.over(1)
             outw.line(2)
 
-        @pl.when(i == 5)
+        @pl.when(i == 3)
         def _():
             outw.over(2)
             outw.line(3)
-
-        @pl.when(i == 6)
-        def _():
             cots.begin()
-
-        @pl.when(i == 7)
-        def _():
-            outw.over(3)
 
         cols = lane_block(i)
         queries = q_t[:, cols]
@@ -704,6 +706,7 @@
         return 0
 
     lax.fori_loop(0, length // QB, query_block, 0)
+    outw.over(3)
     for k in range(4, 8):
         cross(k)
     keep_hid.wait()
@@ -954,17 +957,14 @@
     delta[...] = jnp.sum(o_low[...].astype(F32) * o_t[...], axis=0, keepdims=True)
 
     def query_block(i, _):
-        @pl.when(i == 3)
+        @pl.when(i == 2)
         def _():
             two.flow()
 
-        @pl.when(i == 4)
+        @pl.when(i == 3)
         def _():
             columns_all.over(1)
             to_owners(2)
-
-        @pl.when(i == 5)
-        def _():
             columns_all.line(2)
 
         cols = lane_block(i)

time: 290 us -> 272 us (0.938)
  Pallas kernels: 288 us -> 270 us
    pallas_call x1, Pallas kernels: 283 us -> 265 us  [comm_call(): pl.pallas_call(body, out_shape=outs, in_specs=[pl.BlockSpec(memory_space=...]
where the time goes in v6:
time: 272 us
  Pallas kernels  270 us (99%)
    pallas_call x1, Pallas kernels, comm_call(): pl.pallas_call(body, out_shape=outs, in_specs=[pl.BlockSpec(memory_space=...  265 us

profile of v6, /device:TPU:0, one launch (start us, length us, event | category | flops | bytes accessed | tf_op | source)
XLA Modules:
  0.0 271.7 jit_solution(1211006705065110946)
XLA Ops:
  1.3 265.1 %shard_map.247 = (bf16[16,128,1024]{2,1,0:T(8,128)(2,1)}, bf16[16,128,1024]{2,1,0:T(8,128)(2,1)}, bf16[3,16,32,512]{3,2,1,0:T(8,128)(2,1)}, f32[128,1024]{1,0:T(...) custom-call(bf16[128,1024]{1,0:T(8,128)(2,1)} %bitcast.13, ...), custom_call_target="tpu_custom_call" | custom-call | tf_op jit(solution)/shard_map/pallas_call | solution.py:391
  266.4 5.3 %shard_map.248 = (bf16[128,1024]{1,0:T(8,128)(2,1)}, f32[128,1024]{1,0:T(8,128)}, f32[1,32]{1,0:T(1,128)}, f32[1,32]{1,0:T(1,128)}, f32[32,1024]{1,0:T(8,128)}, ...) custom-call(bf16[32,32,128]{2,1,0:T(8,128)(2,1)} %get-tuple-element., ...), custom_call_target="tpu_custom_call" | custom-call | tf_op jit(solution)/shard_map/pallas_call | solution.py:1206

commit v7 on v6

--- a/solution.py
+++ b/solution.py
@@ -1053,9 +1053,14 @@
 def finish(
     wg_all, dwo_sum, dw_all, query_w, key_w, value_w, router_w, gate_w, up_w, gain_a, gain_e, mix, residual, g_tok,
     mixed, grad_tokens, grad_a, grad_e, grad_q, grad_k, grad_v, grad_o, grad_r, grad_gate, grad_up, grad_down,
-    spread,
+    spread, arrived, staged, sem,
 ):
     width = grad_o.shape[1]
+    outs = (grad_gate, grad_up, grad_down)
+    loads = [pltpu.make_async_copy(dw_all.at[m], arrived.at[m], sem.at[0, m]) for m in range(3)]
+    stores = [pltpu.make_async_copy(staged.at[m], outs[m], sem.at[1, m]) for m in range(3)]
+    for copy in loads:
+        copy.start()
     mixed[...] = (residual[...] + mix[...].astype(F32)).astype(BF)
     grad_tokens[...] = g_tok[...]
     by_first, by_second = column(gain_a[...]), column(gain_e[...])
@@ -1078,11 +1083,13 @@
     router = jnp.transpose(router)[0:E, 0:32]
     grad_r[...] = router * gain_e[...].astype(F32)
     total = jnp.zeros((32 * E, 128), F32)
-    for m, (ref, weight) in enumerate(((grad_gate, gate_w), (grad_up, up_w), (grad_down, None))):
+    for m, weight in enumerate((gate_w, up_w, None)):
+        loads[m].wait()
+        ref = staged.at[m]
         for b in range(F // 128):
             lanes = slice(b * 128, b * 128 + 128)
             for e in range(E):
-                part = dw_all[m, e, :, lanes].astype(F32)
+                part = arrived[m, e, :, lanes].astype(F32)
                 spread[b, pl.ds(e, 32, stride=E), :] = part
             plain = spread[b]
             if m == 2:
@@ -1090,8 +1097,11 @@
             else:
                 ref[:, :, lanes] = plain.reshape(32, E, 128) * by_second[:, :, None]
                 total = total + plain * weight[:, :, lanes].astype(F32).reshape(32 * E, 128)
+        stores[m].start()
     sums = jnp.sum(jnp.sum(total.reshape(32, E, 128), axis=1), axis=1, keepdims=True)
     grad_e[...] = as_row(sums) + jnp.sum(router * router_w[...].astype(F32), axis=0, keepdims=True)
+    for copy in stores:
+        copy.wait()
 
 
 def frequencies(head_dim):
@@ -1209,7 +1219,14 @@
         + [sds((32, n), F32) for n in (D, 512, 512, D)]
         + [sds((E, 32), F32)]
         + [sds((32, E, F), F32)] * 3,
-        scratch_shapes=[VM((F // 128, 32 * E, 128), F32)],
+        in_specs=[pl.BlockSpec(memory_space=m) for m in [VM] * 2 + [ANY] + [VM] * 11],
+        out_specs=[pl.BlockSpec(memory_space=m) for m in [VM] * 9 + [ANY] * 3],
+        scratch_shapes=[
+            VM((F // 128, 32 * E, 128), F32),
+            VM((3, E, 32, F), BF),
+            VM((3, 32, E, F), F32),
+            DMA((2, 3)),
+        ],
         compiler_params=pltpu.CompilerParams(vmem_limit_bytes=VMEM_LIMIT),
     )(
         wg_all,

time: 272 us -> 274 us (level)
  no operation moved by 1% of the time
where the time goes in v7:
time: 274 us
  Pallas kernels  272 us (99%)
    pallas_call x1, Pallas kernels, comm_call(): pl.pallas_call(body, out_shape=outs, in_specs=[pl.BlockSpec(memory_space=...  265 us
    pallas_call x1, Pallas kernels, sixteen_seats(): pl.pallas_call(finish, out_shape=[sds((rows, D), BF), sds((rows, D), F32)...  7.07 us

profile of v7, /device:TPU:0, one launch (start us, length us, event | category | flops | bytes accessed | tf_op | source)
XLA Modules:
  0.0 273.7 jit_solution(3062118186998577268)
XLA Ops:
  1.3 265.1 %shard_map.247 = (bf16[16,128,1024]{2,1,0:T(8,128)(2,1)}, bf16[16,128,1024]{2,1,0:T(8,128)(2,1)}, bf16[3,16,32,512]{3,2,1,0:T(8,128)(2,1)}, f32[128,1024]{1,0:T(...) custom-call(bf16[128,1024]{1,0:T(8,128)(2,1)} %bitcast.13, ...), custom_call_target="tpu_custom_call" | custom-call | tf_op jit(solution)/shard_map/pallas_call | solution.py:391
  266.4 7.1 %shard_map.248 = (bf16[128,1024]{1,0:T(8,128)(2,1)}, f32[128,1024]{1,0:T(8,128)}, f32[1,32]{1,0:T(1,128)}, f32[1,32]{1,0:T(1,128)}, f32[32,1024]{1,0:T(8,128)}, ...) custom-call(bf16[32,32,128]{2,1,0:T(8,128)(2,1)} %get-tuple-element., ...), custom_call_target="tpu_custom_call" | custom-call | tf_op jit(solution)/shard_map/pallas_call | solution.py:1216
